TPU v7x, 32 devices: a whole 2x2x4 slice. The times are simulated.
32 devices in a mesh: groups: 2 (over y), sub: 4 (over z), scen: 2 (over x), half: 2 (over core).
Axes of the slice: x: 2, y: 2, z: 4, core: 2. Of those that a mesh axis runs over, the one named last changes fastest.
Arguments:
- inverses: bfloat16 [16, 512, 512], P(('groups', 'sub', 'half')), parts along dimension 0
- cotangent: bfloat16 [16, 64, 512], P(('groups', 'sub', 'half'), 'scen'), parts along dimension 0, may hold values from -6 to 6
- subnet_sizes: int32 [16], P(('groups', 'sub', 'half')), parts along dimension 0, may hold values from 256 to 512, as said below
- slot_into: int32 [16, 8, 8], P(('groups', 'sub', 'half')), parts along dimension 0, may hold values from 0 to 511, as said below
- slot_from: int32 [16, 8, 8], P(('groups', 'sub', 'half')), parts along dimension 0, may hold values from -1 to 511, as said below
- offsets: int32 [16, 8, 8], P(('groups', 'sub', 'half')), parts along dimension 0, may hold values from 2 to 4
- weights: float32 [16, 8, 8], P(('groups', 'sub', 'half')), parts along dimension 0, may hold values from 0 to 1
- admittance: float32 [16, 8, 8], P(('groups', 'sub', 'half')), parts along dimension 0, may hold values from 0.5 to 2
- fault_bus: int32 [128], P(('groups', 'scen')), parts along dimension 0, may hold values from 0 to 4095, as said below
Outputs:
- first_adjoint: bfloat16 [16, 64, 512], P(('groups', 'sub', 'half'), 'scen'), parts along dimension 0
- fault_grad: float32 [8, 128], P(None, ('groups', 'scen')), parts along dimension 1
There are 2 independent parts, one for each index of `groups`. A program takes and returns all parts, laid end to end along the dimension named above; each array names one. Nothing has to cross between parts.
Inputs may be any that keep to these rules, and one draw needn't show every extreme that they name: `subnet_sizes`: some subnetwork has exactly 512 live nodes. `slot_into`: names a live node of the sending device; 0 in slots that are empty. `slot_from`: names a live node of the receiving device; for each pair of devices the used slots come first; in every draw some receiving device has all 8 slots used from every sender. `fault_bus`: names a live node.
All inputs are finite; a program needn't handle non-finite values.
Results may differ from a plain program's by a relative error of at most 0.009.
Values may be sent and summed in bfloat16 or wider, within the bound.
No kernel may reach another device: no remote copies, remote signals or barrier semaphores. Data moves between devices by JAX's collectives and lax.ppermute only.
A program may use at most 64 MiB of HBM per device.

v0:
```python
import jax
import jax.numpy as jnp
from jax import lax
from jax.sharding import PartitionSpec as P

STEPS = 8


def per_device(
    inverses, cotangent, subnet_sizes, slot_into, slot_from, offsets, weights, admittance, fault_bus
):
    block_count, column_count, node_count = cotangent.shape
    owner_count = lax.axis_size(("sub", "half"))
    slot_depth = slot_into.shape[2]
    slot_count = owner_count * slot_depth
    local_span = block_count * node_count
    active = (jnp.arange(node_count, dtype=jnp.int32)[None, :] < subnet_sizes[:, None]).astype(
        jnp.float32
    )
    node_ids = jnp.arange(local_span, dtype=jnp.int32)[None, :]
    send_hot = (slot_into.reshape(slot_count)[:, None] == node_ids).astype(jnp.bfloat16)
    send_hot = send_hot.reshape(slot_count, block_count, node_count)
    from_local = slot_from.reshape(slot_count)
    is_used = (from_local >= 0).astype(jnp.float32)
    recv_hot = (
        (from_local[:, None] == node_ids)
        .astype(jnp.float32)
        .reshape(slot_count, block_count, node_count)
    )
    delay_steps = offsets.reshape(slot_count)
    fraction = weights.reshape(slot_count)
    conduct = admittance.reshape(slot_count) * is_used
    arrivals = {}
    results = {}
    for step_now in range(STEPS - 1, -1, -1):
        history = jnp.zeros((block_count, column_count, node_count), jnp.float32)
        terms = jnp.zeros((column_count, slot_count), jnp.float32)
        present = False
        for source_step in range(step_now + 2, min(step_now + 6, STEPS)):
            step_gap = source_step - step_now
            factor = conduct * (
                fraction * (delay_steps == step_gap).astype(jnp.float32)
                + (1.0 - fraction) * (delay_steps + 1 == step_gap).astype(jnp.float32)
            )
            terms = terms + factor[None, :] * arrivals[source_step].astype(jnp.float32)
            present = True
        if present:
            history = jnp.einsum("sk,kjn->jsn", terms, recv_hot, precision=lax.Precision.HIGHEST)
        if step_now == STEPS - 1:
            history = cotangent.astype(jnp.float32)
        driving = (history * active[:, None, :]).astype(jnp.bfloat16)
        adjoint = jnp.einsum("jsn,jnm->jsm", driving, inverses, preferred_element_type=jnp.float32)
        results[step_now] = (adjoint * active[:, None, :]).astype(jnp.bfloat16)
        if step_now >= 2:
            picked = jnp.einsum(
                "jsn,kjn->sk", results[step_now], send_hot, preferred_element_type=jnp.float32
            )
            arrivals[step_now] = lax.all_to_all(
                picked.astype(jnp.bfloat16)[None],
                ("sub", "half"),
                split_axis=2,
                concat_axis=2,
                tiled=True,
            )[0]
    owner_index = lax.axis_index(("sub", "half"))
    local_bus = fault_bus - owner_index * local_span
    owned = (local_bus >= 0) & (local_bus < local_span)
    clamped = jnp.clip(local_bus, 0, local_span - 1)
    position = (
        clamped // node_count * column_count * node_count
        + jnp.arange(column_count, dtype=jnp.int32) * node_count
        + clamped % node_count
    )
    sensitivity = jnp.stack(
        [
            jnp.where(
                owned, jnp.take(results[index].reshape(-1), position).astype(jnp.float32), 0.0
            )
            for index in range(STEPS)
        ]
    )
    fault_grad = lax.psum(sensitivity, ("sub", "half"))
    return (results[0], fault_grad)


def solution(mesh):
    return jax.shard_map(
        per_device,
        mesh=mesh,
        in_specs=(
            P(("groups", "sub", "half"), None, None),
            P(("groups", "sub", "half"), "scen", None),
            P(("groups", "sub", "half")),
            P(("groups", "sub", "half"), None, None),
            P(("groups", "sub", "half"), None, None),
            P(("groups", "sub", "half"), None, None),
            P(("groups", "sub", "half"), None, None),
            P(("groups", "sub", "half"), None, None),
            P(("groups", "scen")),
        ),
        out_specs=(P(("groups", "sub", "half"), "scen", None), P(None, ("groups", "scen"))),
        check_vma=False,
    )
```

profile of v0, /device:TPU:0, one launch (start us, length us, event | category | flops | bytes accessed | tf_op | source)
XLA Modules:
  0.0 85.0 jit_solution(10206183115102742730)
XLA Ops:
  1.3 0.8 eq.189
  2.1 0.9 %fusion.13 = bf16[32,512]{1,0:T(8,128)(2,1)S(1)} fusion(bf16[1,512,512]{2,1,0:T(8,128)(2,1)S(1)} %copy-done, bf16[1,32,512]{2,1,0:T(8,128)(2,1)} %param.12, f32[512]{0:T(512)S(1)} %fusion.108), kind=kOutput, calls=%fused_computation.35 | convolution fusion | flops 16859136 | bytes 591872 | tf_op jit(solution)/shard_map/jsn,jnm->jsm/dot_general | solution.py:52
  3.1 0.2 fusion.28
  3.3 0.1 copy.19
  3.4 0.5 broadcast.407
  4.0 0.7 reduce.1
  4.7 0.7 reshape.694
  5.4 6.3 %all-to-all-start.1 = ((bf16[8,2,128]{2,1,0:T(2,128)(2,1)}), bf16[8,2,128]{2,1,0:T(2,128)(2,1)S(1)}, u32[]{:S(2)}, u32[]{:S(2)}) async-start(bf16[8,2,128]{2,1,0:T(2,128)(2,1)} %reshape.694), calls=%async_computation.1 | async-start | bytes 8192 | tf_op jit(solution)/shard_map/all_to_all | solution.py:58
  11.7 0.2 fusion.12
  11.9 0.5 copy-done.2
  12.4 0.6 copy-done.3
  13.5 0.2 fusion.27
  13.7 0.1 copy.17
  13.8 0.7 reduce
  14.5 0.7 reshape.692
  15.2 1.9 %all-to-all-done.1 = bf16[8,2,128]{2,1,0:T(2,128)(2,1)S(1)} async-done(((bf16[8,2,128]{2,1,0:T(2,128)(2,1)}), bf16[8,2,128]{2,1,0:T(2,128)(2,1)S(1)}, u32[]{:S(2)}, u32[]{:S(2)}) %all-to-all-start.1) | async-done | bytes 4128 | tf_op jit(solution)/shard_map/all_to_all | solution.py:58
  17.2 3.3 %all-to-all-start = ((bf16[8,2,128]{2,1,0:T(2,128)(2,1)}), bf16[8,2,128]{2,1,0:T(2,128)(2,1)S(1)}, u32[]{:S(2)}, u32[]{:S(2)}) async-start(bf16[8,2,128]{2,1,0:T(2,128)(2,1)} %reshape.692), calls=%async_computation | async-start | bytes 8192 | tf_op jit(solution)/shard_map/all_to_all | solution.py:58
  20.6 0.1 copy.20
  20.7 5.3 %all-to-all-done = bf16[8,2,128]{2,1,0:T(2,128)(2,1)S(1)} async-done(((bf16[8,2,128]{2,1,0:T(2,128)(2,1)}), bf16[8,2,128]{2,1,0:T(2,128)(2,1)S(1)}, u32[]{:S(2)}, u32[]{:S(2)}) %all-to-all-start) | async-done | bytes 4128 | tf_op jit(solution)/shard_map/all_to_all | solution.py:58
  26.1 0.3 fusion.24
  26.4 0.2 fusion.25
  26.6 0.2 fusion.14
  26.8 0.2 fusion.29
  27.0 0.1 copy.21
  27.1 0.7 reduce.4
  27.8 0.7 reshape.700
  28.5 3.3 %all-to-all-start.2 = ((bf16[8,2,128]{2,1,0:T(2,128)(2,1)}), bf16[8,2,128]{2,1,0:T(2,128)(2,1)S(1)}, u32[]{:S(2)}, u32[]{:S(2)}) async-start(bf16[8,2,128]{2,1,0:T(2,128)(2,1)} %reshape.700), calls=%async_computation.2 | async-start | bytes 8192 | tf_op jit(solution)/shard_map/all_to_all | solution.py:58
  31.8 0.2 fusion.15
  32.0 0.2 fusion.30
  32.3 0.1 copy.23
  32.4 0.7 reduce.2
  33.1 0.7 reshape.696
  33.8 3.5 %all-to-all-done.2 = bf16[8,2,128]{2,1,0:T(2,128)(2,1)S(1)} async-done(((bf16[8,2,128]{2,1,0:T(2,128)(2,1)}), bf16[8,2,128]{2,1,0:T(2,128)(2,1)S(1)}, u32[]{:S(2)}, u32[]{:S(2)}) %all-to-all-start.2) | async-done | bytes 4128 | tf_op jit(solution)/shard_map/all_to_all | solution.py:58
  37.3 3.3 %all-to-all-start.3 = ((bf16[8,2,128]{2,1,0:T(2,128)(2,1)}), bf16[8,2,128]{2,1,0:T(2,128)(2,1)S(1)}, u32[]{:S(2)}, u32[]{:S(2)}) async-start(bf16[8,2,128]{2,1,0:T(2,128)(2,1)} %reshape.696), calls=%async_computation.3 | async-start | bytes 8192 | tf_op jit(solution)/shard_map/all_to_all | solution.py:58
  40.6 0.7 gather_fusion.7
  41.5 4.5 %all-to-all-done.3 = bf16[8,2,128]{2,1,0:T(2,128)(2,1)S(1)} async-done(((bf16[8,2,128]{2,1,0:T(2,128)(2,1)}), bf16[8,2,128]{2,1,0:T(2,128)(2,1)S(1)}, u32[]{:S(2)}, u32[]{:S(2)}) %all-to-all-start.3) | async-done | bytes 4128 | tf_op jit(solution)/shard_map/all_to_all | solution.py:58
  46.2 0.3 fusion.22
  46.4 0.2 fusion.17
  46.6 0.3 fusion.23
  46.9 0.2 fusion.16
  47.1 0.2 fusion.31
  47.3 0.1 copy.25
  47.4 0.7 reduce.5
  48.1 0.7 reshape.702
  48.8 3.3 %all-to-all-start.4 = ((bf16[8,2,128]{2,1,0:T(2,128)(2,1)}), bf16[8,2,128]{2,1,0:T(2,128)(2,1)S(1)}, u32[]{:S(2)}, u32[]{:S(2)}) async-start(bf16[8,2,128]{2,1,0:T(2,128)(2,1)} %reshape.702), calls=%async_computation.4 | async-start | bytes 8192 | tf_op jit(solution)/shard_map/all_to_all | solution.py:58
  52.1 0.2 fusion.32
  52.3 0.1 copy.27
  52.4 0.7 reduce.3
  53.1 0.7 reshape.698
  53.8 3.7 %all-to-all-done.4 = bf16[8,2,128]{2,1,0:T(2,128)(2,1)S(1)} async-done(((bf16[8,2,128]{2,1,0:T(2,128)(2,1)}), bf16[8,2,128]{2,1,0:T(2,128)(2,1)S(1)}, u32[]{:S(2)}, u32[]{:S(2)}) %all-to-all-start.4) | async-done | bytes 4128 | tf_op jit(solution)/shard_map/all_to_all | solution.py:58
  57.5 3.3 %all-to-all-start.5 = ((bf16[8,2,128]{2,1,0:T(2,128)(2,1)}), bf16[8,2,128]{2,1,0:T(2,128)(2,1)S(1)}, u32[]{:S(2)}, u32[]{:S(2)}) async-start(bf16[8,2,128]{2,1,0:T(2,128)(2,1)} %reshape.698), calls=%async_computation.5 | async-start | bytes 8192 | tf_op jit(solution)/shard_map/all_to_all | solution.py:58
  60.9 0.7 gather_fusion.6
  61.6 0.7 gather_fusion.4
  62.4 0.7 gather_fusion.5
  63.1 0.7 gather_fusion.2
  63.8 0.7 gather_fusion.3
  64.7 1.6 %all-to-all-done.5 = bf16[8,2,128]{2,1,0:T(2,128)(2,1)S(1)} async-done(((bf16[8,2,128]{2,1,0:T(2,128)(2,1)}), bf16[8,2,128]{2,1,0:T(2,128)(2,1)S(1)}, u32[]{:S(2)}, u32[]{:S(2)}) %all-to-all-start.5) | async-done | bytes 4128 | tf_op jit(solution)/shard_map/all_to_all | solution.py:58
  66.4 0.3 fusion.20
  66.7 0.2 fusion.21
  66.9 0.2 fusion.18
  67.1 0.2 fusion.26
  67.4 0.7 gather_fusion.1
  68.1 0.7 gather_fusion
  68.9 16.1 %psum.7 = f32[8,32]{1,0:T(8,128)} all-reduce(f32[8,32]{1,0:T(8,128)S(1)} %stack.35), channel_id=1, replica_groups=mesh['groups'=2,'sub'=4,'scen'=2,'half'=2] {'sub','half'}, use_global_device_ids=true, to_apply=%region_0.2 | all-reduce | flops 256 | bytes 2048 | tf_op jit(solution)/shard_map/psum | solution.py:82
  (46 shorter events, 1.7 us)
Async XLA Ops:
  0.6 1.5 %copy-start = (bf16[1,512,512]{2,1,0:T(8,128)(2,1)S(1)}, bf16[1,512,512]{2,1,0:T(8,128)(2,1)}, u32[]{:S(2)}) copy-start(bf16[1,512,512]{2,1,0:T(8,128)(2,1)} %param.11) | copy-start | bytes 1572868
  5.4 11.8 %all-to-all-start.1 = ((bf16[8,2,128]{2,1,0:T(2,128)(2,1)}), bf16[8,2,128]{2,1,0:T(2,128)(2,1)S(1)}, u32[]{:S(2)}, u32[]{:S(2)}) async-start(bf16[8,2,128]{2,1,0:T(2,128)(2,1)} %reshape.694), calls=%async_computation.1 | async-start | bytes 8192 | tf_op jit(solution)/shard_map/all_to_all | solution.py:58
  11.7 0.7 copy-start.2
  11.7 1.5 %copy-start.5 = (s32[1,8,8]{2,1,0:T(8,128)S(1)}, s32[1,8,8]{2,1,0:T(8,128)}, u32[]{:S(2)}) copy-start(s32[1,8,8]{2,1,0:T(8,128)} %param.16) | copy-start | bytes 772
  12.4 0.7 copy-start.3
  12.4 0.8 copy-start.4
  15.2 5.3 %copy-start.6 = (s32[32]{0:T(128)S(1)}, s32[32]{0:T(128)}, u32[]{:S(2)}) copy-start(s32[32]{0:T(128)} %param.19) | copy-start | bytes 388
  17.2 8.8 %all-to-all-start = ((bf16[8,2,128]{2,1,0:T(2,128)(2,1)}), bf16[8,2,128]{2,1,0:T(2,128)(2,1)S(1)}, u32[]{:S(2)}, u32[]{:S(2)}) async-start(bf16[8,2,128]{2,1,0:T(2,128)(2,1)} %reshape.692), calls=%async_computation | async-start | bytes 8192 | tf_op jit(solution)/shard_map/all_to_all | solution.py:58
  28.5 8.7 %all-to-all-start.2 = ((bf16[8,2,128]{2,1,0:T(2,128)(2,1)}), bf16[8,2,128]{2,1,0:T(2,128)(2,1)S(1)}, u32[]{:S(2)}, u32[]{:S(2)}) async-start(bf16[8,2,128]{2,1,0:T(2,128)(2,1)} %reshape.700), calls=%async_computation.2 | async-start | bytes 8192 | tf_op jit(solution)/shard_map/all_to_all | solution.py:58
  37.3 8.7 %all-to-all-start.3 = ((bf16[8,2,128]{2,1,0:T(2,128)(2,1)}), bf16[8,2,128]{2,1,0:T(2,128)(2,1)S(1)}, u32[]{:S(2)}, u32[]{:S(2)}) async-start(bf16[8,2,128]{2,1,0:T(2,128)(2,1)} %reshape.696), calls=%async_computation.3 | async-start | bytes 8192 | tf_op jit(solution)/shard_map/all_to_all | solution.py:58
  48.8 8.7 %all-to-all-start.4 = ((bf16[8,2,128]{2,1,0:T(2,128)(2,1)}), bf16[8,2,128]{2,1,0:T(2,128)(2,1)S(1)}, u32[]{:S(2)}, u32[]{:S(2)}) async-start(bf16[8,2,128]{2,1,0:T(2,128)(2,1)} %reshape.702), calls=%async_computation.4 | async-start | bytes 8192 | tf_op jit(solution)/shard_map/all_to_all | solution.py:58
  57.5 8.7 %all-to-all-start.5 = ((bf16[8,2,128]{2,1,0:T(2,128)(2,1)}), bf16[8,2,128]{2,1,0:T(2,128)(2,1)S(1)}, u32[]{:S(2)}, u32[]{:S(2)}) async-start(bf16[8,2,128]{2,1,0:T(2,128)(2,1)} %reshape.698), calls=%async_computation.5 | async-start | bytes 8192 | tf_op jit(solution)/shard_map/all_to_all | solution.py:58
  67.1 1.0 %copy-start.1 = (bf16[32,512]{1,0:T(8,128)(2,1)}, bf16[32,512]{1,0:T(8,128)(2,1)S(1)}, u32[]{:S(2)}) copy-start(bf16[32,512]{1,0:T(8,128)(2,1)S(1)} %fusion.18) | copy-start | bytes 98308
where the time goes:
time: 85.6 us; the launch traced here: 85 us
  starting transfers between devices  22.9 us (27%)
  waiting for transfers between devices  20.4 us (24%)
  blocking collectives  16.1 us (19%)
  local copies, waits for them, and re-layouts  14.6 us (17%)
  matrix products  5.07 us (6%)
  other arithmetic  4.32 us (5%)
  between operations  1.62 us (2%)
    all_to_all x6, starting transfers between devices, per_device(): lax.all_to_all(picked.astype(jnp.bfloat16)[None], ('sub', 'half'), split_...  22.9 us
    all_to_all x6, waiting for transfers between devices, per_device(): lax.all_to_all(picked.astype(jnp.bfloat16)[None], ('sub', 'half'), split_...  20.4 us
    psum x1, blocking collectives, per_device(): fault_grad = lax.psum(sensitivity, ('sub', 'half'))  16.1 us
    unnamed x35, local copies, waits for them, and re-layouts  6.39 us
    gather x8, local copies, waits for them, and re-layouts, per_device(): jnp.take(results[index].reshape(-1), position).astype(jnp.float32)  5.71 us
    unnamed x6, other arithmetic  4.23 us
    dot_general x8, matrix products, per_device(): jnp.einsum('jsn,jnm->jsm', driving, inverses, preferred_element_type=jnp....  2.26 us
  transfers between devices with their start and end apart: 6, of which 6 were waited for; matrix products, arithmetic and copies ran while one was open for 13% of the time, Pallas kernels for 0%

commit v1 on v0

--- a/solution.py
+++ b/solution.py
@@ -1,16 +1,236 @@
 import jax
 import jax.numpy as jnp
+import numpy as np
 from jax import lax
+from jax.experimental import pallas as pl
+from jax.experimental.pallas import tpu as pltpu
 from jax.sharding import PartitionSpec as P
 
 STEPS = 8
-
-
-def per_device(
+LANES = 128
+OWNER_AXES = ("sub", "half")
+VARIANTS = (
+    (2, 3, 0, 2),
+    (2, 2, 3, 3),
+    (4, 5, 0, 4),
+    (2, 2, 0, 2),
+    (0, 3, 0, 0),
+    (4, 5, 3, 4),
+)
+NT = (((1,), (1,)), ((), ()))
+TN = (((0,), (0,)), ((), ()))
+
+
+def dot(left, right, dims=(((1,), (0,)), ((), ()))):
+    return lax.dot_general(left, right, dims, preferred_element_type=jnp.float32)
+
+
+def spread_matrix(column_count, slot_count):
+    spread = np.zeros((LANES, (len(VARIANTS) + 1) * LANES), np.float32)
+    for variant, gaps in enumerate(VARIANTS):
+        for quarter, gap in enumerate(gaps):
+            if gap:
+                lane = variant * LANES + quarter * column_count
+                for piece in range(3):
+                    row = slot_count + column_count + 3 * (gap - 2) + piece
+                    spread[row, lane : lane + column_count] = 1
+    for lane in range(LANES):
+        spread[slot_count + lane % column_count, len(VARIANTS) * LANES + lane] = 1
+    return spread
+
+
+def column_of(ref, peers, depth):
+    eye = lax.broadcasted_iota(jnp.int32, (depth, depth), 0) == lax.broadcasted_iota(
+        jnp.int32, (depth, depth), 1
+    )
+    rows = [
+        jnp.where(eye, jnp.broadcast_to(ref[0, peer : peer + 1, :].astype(jnp.float32), (depth, depth)), 0.0)
+        for peer in range(peers)
+    ]
+    return jnp.sum(jnp.concatenate(rows, axis=0), axis=1, keepdims=True)
+
+
+def pick_kernel(
+    size_ref, owner_ref, inverse_hbm, cotangent_ref, into_ref, from_ref, offset_ref, weight_ref, admit_ref, bus_ref,
+    message_ref, rows_ref, inverse_ref, semaphore,
+):
+    load = pltpu.make_async_copy(inverse_hbm.at[0], inverse_ref, semaphore)
+    load.start()
+    _, peers, depth = into_ref.shape
+    slots = peers * depth
+    columns, nodes = cotangent_ref.shape[1:]
+    live = size_ref[0]
+    lane = lax.broadcasted_iota(jnp.int32, (slots, nodes), 1)
+    lane_f = lane.astype(jnp.float32)
+    alive = lane < live
+    into = column_of(into_ref, peers, depth)
+    source = column_of(from_ref, peers, depth)
+    delay = column_of(offset_ref, peers, depth)
+    weight = column_of(weight_ref, peers, depth)
+    admit = column_of(admit_ref, peers, depth)
+    recv_hot = jnp.where((source == lane_f) & alive, 1.0, 0.0).astype(jnp.bfloat16)
+    send_hot = jnp.where(into == lane_f, 1.0, 0.0).astype(jnp.bfloat16)
+    driving = jnp.where(alive[:columns], cotangent_ref[0].astype(jnp.float32), 0.0).astype(jnp.bfloat16)
+    bus = (bus_ref[...] - owner_ref[0] * nodes).astype(jnp.float32)
+    eye = lax.broadcasted_iota(jnp.int32, (columns, columns), 0) == lax.broadcasted_iota(
+        jnp.int32, (columns, columns), 1
+    )
+    bus = jnp.sum(jnp.where(eye, jnp.broadcast_to(bus, (columns, columns)), 0.0), axis=1, keepdims=True)
+    fault_hot = jnp.where(bus == lane_f[:columns], 1.0, 0.0).astype(jnp.bfloat16)
+    hot = jnp.concatenate([send_hot, fault_hot], axis=0)
+    conduct = jnp.where(source >= 0, admit, 0.0)
+    near, far = conduct * weight, conduct * (1.0 - weight)
+    factors = [
+        jnp.where(delay == 2, near, 0.0),
+        jnp.where(delay == 3, near, 0.0) + jnp.where(delay == 2, far, 0.0),
+        jnp.where(delay == 4, near, 0.0) + jnp.where(delay == 3, far, 0.0),
+        jnp.where(delay == 4, far, 0.0),
+    ]
+    spot = lax.broadcasted_iota(jnp.int32, (slots, LANES), 1)
+    params = jnp.zeros((slots, LANES), jnp.float32)
+    for index, factor in enumerate(factors):
+        rest = factor
+        for piece in range(3):
+            part = rest.astype(jnp.bfloat16).astype(jnp.float32)
+            rest = rest - part
+            params = jnp.where(spot == slots + columns + 3 * index + piece, part, params)
+    load.wait()
+    stack = jnp.concatenate([recv_hot, driving], axis=0)
+    picked = dot(stack, inverse_ref[...])
+    lane = lax.broadcasted_iota(jnp.int32, picked.shape, 1)
+    picked = jnp.where(lane < live, picked, 0.0).astype(jnp.bfloat16)
+    rows_ref[...] = picked[:slots]
+    picked = jnp.concatenate([picked, jnp.zeros((LANES - slots - columns, nodes), jnp.bfloat16)], axis=0)
+    body = dot(hot, picked, NT)
+    body = body + jnp.concatenate([params, jnp.zeros((columns, LANES), jnp.float32)], axis=0)
+    message_ref[...] = body.astype(jnp.bfloat16)
+
+
+def march_kernel(place_ref, gathered_ref, spread_ref, rows_ref, first_ref, fault_ref, last_ref):
+    owners, height, _ = gathered_ref.shape
+    slots = rows_ref.shape[0]
+    columns = height - slots
+    depth = slots // owners
+    place = place_ref[0]
+
+    def exchange(parts):
+        return [
+            jnp.concatenate([part[depth * owner : depth * (owner + 1)] for part in parts], axis=0)
+            for owner in range(owners)
+        ]
+
+    def rounded(value):
+        return value.astype(jnp.bfloat16).astype(jnp.float32)
+
+    blocks = [gathered_ref[lax.bitwise_xor(jnp.int32(owner), place)] for owner in range(owners)]
+    count = len(VARIANTS)
+    spread = [dot(block[:slots], spread_ref[...]) for block in blocks]
+    factor = [[part[:, LANES * v : LANES * (v + 1)] for part in spread] for v in range(count)]
+    seven = exchange([part[:, LANES * count :] for part in spread])
+    system = [block[:, :slots] for block in blocks]
+
+    drive = [
+        jnp.concatenate([factor[0][o] * seven[o], factor[1][o] * seven[o]], axis=1).astype(jnp.bfloat16)
+        for o in range(owners)
+    ]
+    result = [dot(system[o], drive[o]) for o in range(owners)]
+    fault_a = sum(part[slots:, :LANES] for part in result[1:]) + result[0][slots:, :LANES]
+    arrived = exchange([rounded(part) for part in result])
+    low = [part[:, :LANES] for part in arrived]
+    high = [part[:, LANES:] for part in arrived]
+    drive = [
+        (factor[2][o] * seven[o] + factor[3][o] * low[o] + factor[4][o] * high[o]).astype(jnp.bfloat16)
+        for o in range(owners)
+    ]
+    later = [factor[5][o] * high[o] for o in range(owners)]
+    result = [dot(system[o], drive[o]) for o in range(owners)]
+    fault_b = sum(part[slots:] for part in result[1:]) + result[0][slots:]
+    arrived = exchange([rounded(part) for part in result])
+    later = [later[o] + factor[1][o] * arrived[o] for o in range(owners)]
+    drive = [(part + pltpu.roll(part, 2 * columns, 1)).astype(jnp.bfloat16) for part in later]
+    for o in range(owners):
+        last_ref[o] = drive[o]
+    own = last_ref[place]
+    adjoint = dot(own, rows_ref[...], TN)
+    first_ref[0] = adjoint[columns : 2 * columns].astype(jnp.bfloat16)
+    fault_c = sum(dot(system[o][slots:], drive[o]) for o in range(owners))
+    fault_s = sum(block[slots:].astype(jnp.float32) for block in blocks)
+
+    lane = lax.broadcasted_iota(jnp.int32, (columns, LANES), 1)
+    mine = lane % columns == lax.broadcasted_iota(jnp.int32, (columns, LANES), 0)
+
+    def row(value):
+        return rounded(jnp.sum(jnp.where(mine, value, 0.0), axis=0, keepdims=True))
+
+    row_a, row_b, row_c, row_s = row(fault_a), row(fault_b), row(fault_c), row(fault_s)
+
+    def back(value, quarters):
+        return pltpu.roll(value, LANES - quarters * columns, 1)
+
+    table = [
+        back(row_c, 1),
+        row_c,
+        back(row_b, 1),
+        row_b,
+        back(row_a, 1),
+        row_a,
+        jnp.zeros_like(row_a),
+        back(row_s, 2),
+    ]
+    step = lax.broadcasted_iota(jnp.int32, (STEPS, LANES), 0)
+    total = jnp.zeros((STEPS, LANES), jnp.float32)
+    for index, value in enumerate(table):
+        total = jnp.where(step == index, jnp.broadcast_to(value, total.shape), total)
+    fault_ref[...] = total[:, :columns]
+
+
+def gathered_plan(
+    inverses, cotangent, subnet_sizes, slot_into, slot_from, offsets, weights, admittance, fault_bus
+):
+    _, columns, nodes = cotangent.shape
+    owners, depth = slot_into.shape[1:]
+    slots = owners * depth
+    height = slots + columns
+    owner = lax.axis_index(OWNER_AXES).astype(jnp.int32)[None]
+    vmem = pl.BlockSpec(memory_space=pltpu.VMEM)
+    smem = pl.BlockSpec(memory_space=pltpu.SMEM)
+    message, rows = pl.pallas_call(
+        pick_kernel,
+        out_shape=(
+            jax.ShapeDtypeStruct((height, LANES), jnp.bfloat16),
+            jax.ShapeDtypeStruct((slots, nodes), jnp.bfloat16),
+        ),
+        in_specs=[smem, smem, pl.BlockSpec(memory_space=pl.ANY)] + [vmem] * 7,
+        out_specs=(vmem, vmem),
+        scratch_shapes=[pltpu.VMEM((nodes, nodes), jnp.bfloat16), pltpu.SemaphoreType.DMA],
+        name="pick",
+    )(
+        subnet_sizes, owner, inverses, cotangent, slot_into, slot_from, offsets, weights, admittance, fault_bus[None],
+    )
+    bits = owners.bit_length() - 1
+    held = message[None]
+    for bit in range(bits):
+        other = lax.ppermute(held, OWNER_AXES, [(i, i ^ (1 << bit)) for i in range(owners)])
+        held = jnp.concatenate([held, other], axis=0)
+    spread = jnp.asarray(spread_matrix(columns, slots), jnp.bfloat16)
+    return pl.pallas_call(
+        march_kernel,
+        out_shape=(
+            jax.ShapeDtypeStruct((1, columns, nodes), jnp.bfloat16),
+            jax.ShapeDtypeStruct((STEPS, columns), jnp.float32),
+        ),
+        in_specs=[smem, vmem, vmem, vmem],
+        out_specs=(vmem, vmem),
+        scratch_shapes=[pltpu.VMEM((owners, slots, LANES), jnp.bfloat16)],
+        name="march",
+    )(owner, held, spread, rows)
+
+
+def exchanged_plan(
     inverses, cotangent, subnet_sizes, slot_into, slot_from, offsets, weights, admittance, fault_bus
 ):
     block_count, column_count, node_count = cotangent.shape
-    owner_count = lax.axis_size(("sub", "half"))
+    owner_count = lax.axis_size(OWNER_AXES)
     slot_depth = slot_into.shape[2]
     slot_count = owner_count * slot_depth
     local_span = block_count * node_count
@@ -56,13 +276,9 @@
                 "jsn,kjn->sk", results[step_now], send_hot, preferred_element_type=jnp.float32
             )
             arrivals[step_now] = lax.all_to_all(
-                picked.astype(jnp.bfloat16)[None],
-                ("sub", "half"),
-                split_axis=2,
-                concat_axis=2,
-                tiled=True,
+                picked.astype(jnp.bfloat16)[None], OWNER_AXES, split_axis=2, concat_axis=2, tiled=True
             )[0]
-    owner_index = lax.axis_index(("sub", "half"))
+    owner_index = lax.axis_index(OWNER_AXES)
     local_bus = fault_bus - owner_index * local_span
     owned = (local_bus >= 0) & (local_bus < local_span)
     clamped = jnp.clip(local_bus, 0, local_span - 1)
@@ -79,8 +295,22 @@
             for index in range(STEPS)
         ]
     )
-    fault_grad = lax.psum(sensitivity, ("sub", "half"))
-    return (results[0], fault_grad)
+    return results[0], lax.psum(sensitivity, OWNER_AXES)
+
+
+def per_device(*arrays):
+    blocks, columns, nodes = arrays[1].shape
+    owners, depth = arrays[3].shape[1:]
+    slots = owners * depth
+    fits = (
+        blocks == 1
+        and columns * 4 == LANES
+        and depth == 8
+        and owners & (owners - 1) == 0
+        and slots + columns + 12 <= LANES
+        and nodes % LANES == 0
+    )
+    return gathered_plan(*arrays) if fits else exchanged_plan(*arrays)
 
 
 def solution(mesh):

time: 85.6 us -> 22.8 us (0.27)
  starting transfers between devices: 22.9 us -> 6.54 us
  blocking collectives: 16.1 us -> 0 us
  local copies, waits for them, and re-layouts: 14.6 us -> 0.01 us
  waiting for transfers between devices: 20.4 us -> 7.22 us
  Pallas kernels: 0 us -> 5.93 us
  matrix products: 5.07 us -> 0 us
  other arithmetic: 4.32 us -> 1.45 us
    all_to_all x6 -> x0, starting transfers between devices: 22.9 us -> none  [per_device(): lax.all_to_all(picked.astype(jnp.bfloat16)[None], ('sub', 'half'), split_...]
    all_to_all x6 -> x0, waiting for transfers between devices: 20.4 us -> none  [per_device(): lax.all_to_all(picked.astype(jnp.bfloat16)[None], ('sub', 'half'), split_...]
    psum x1 -> x0, blocking collectives: 16.1 us -> none  [per_device(): fault_grad = lax.psum(sensitivity, ('sub', 'half'))]
    ppermute x0 -> x3, waiting for transfers between devices: none -> 7.22 us  [gathered_plan(): lax.ppermute(held, OWNER_AXES, [(i, i ^ 1 << bit) for i in range(owners)])]
    ppermute x0 -> x3, starting transfers between devices: none -> 6.54 us  [gathered_plan(): lax.ppermute(held, OWNER_AXES, [(i, i ^ 1 << bit) for i in range(owners)])]
    unnamed x35 -> x2, local copies, waits for them, and re-layouts: 6.39 us -> 0.01 us
    pallas_call x0 -> x2, Pallas kernels: none -> 5.93 us  [the longest x1 3.06 us: gathered_plan(): pl.pallas_call(march_kernel, out_shape=(jax.ShapeDtypeStruct((1, columns,...]
    gather x8 -> x0, local copies, waits for them, and re-layouts: 5.71 us -> none  [per_device(): jnp.take(results[index].reshape(-1), position).astype(jnp.float32)]
  transfers between devices with their start and end apart: 6 -> 3, of which waited for: 6 -> 3; matrix products, arithmetic and copies ran while one was open for 13% -> 0% of each run, Pallas kernels for 0% -> 0%
where the time goes in v1:
time: 22.8 us; the launch traced here: 22.4 us
  waiting for transfers between devices  7.22 us (32%)
  starting transfers between devices  6.54 us (29%)
  Pallas kernels  5.93 us (26%)
  other arithmetic  1.45 us (6%)
  between operations  1.31 us (6%)
    ppermute x3, waiting for transfers between devices, gathered_plan(): lax.ppermute(held, OWNER_AXES, [(i, i ^ 1 << bit) for i in range(owners)])  7.22 us
    ppermute x3, starting transfers between devices, gathered_plan(): lax.ppermute(held, OWNER_AXES, [(i, i ^ 1 << bit) for i in range(owners)])  6.54 us
    pallas_call x1, Pallas kernels, gathered_plan(): pl.pallas_call(march_kernel, out_shape=(jax.ShapeDtypeStruct((1, columns,...  3.06 us
    pallas_call x1, Pallas kernels, gathered_plan(): pl.pallas_call(pick_kernel, out_shape=(jax.ShapeDtypeStruct((height, LANE...  2.87 us
    concatenate x3, other arithmetic, gathered_plan(): held = jnp.concatenate([held, other], axis=0)  1.45 us
  transfers between devices with their start and end apart: 3, of which 3 were waited for; matrix products, arithmetic and copies ran while one was open for 0% of the time, Pallas kernels for 0%

profile of v1, /device:TPU:0, one launch (start us, length us, event | category | flops | bytes accessed | tf_op | source)
XLA Modules:
  0.0 22.4 jit_solution(1989614867839921650)
XLA Ops:
  1.3 2.9 %pick.1 = (bf16[96,128]{1,0:T(8,128)(2,1)}, bf16[64,512]{1,0:T(8,128)(2,1)}) custom-call(s32[1]{0:T(128)S(6)} %copy.12.size_ref, s32[1]{0:T(128)} %bitcast.owner_ref.place_ref, bf16[1,512,512]{2,1,0:T(8,128)(2,1)} %inverse_hbm.1, bf16[1,32,512]{2,1,0:T(8,128)(2,1)} %cotangent_ref.1, s32[1,8,8]{2,1,0:T(8,128)} %into_ref.1, s32[1,8,8]{2,1,0:T(8,128)} %from_ref.1, ...), custom_call_target="tpu_custom_call" | custom-call | tf_op jit(solution)/shard_map/pick/pallas_call | solution.py:197
  4.2 0.0 copy-start
  4.2 0.5 %collective-permute-start = (bf16[1,96,128]{2,1,0:T(8,128)(2,1)}, bf16[1,96,128]{2,1,0:T(8,128)(2,1)S(1)}, u32[]{:S(2)}, u32[]{:S(2)}) collective-permute-start(bf16[1,96,128]{2,1,0:T(8,128)(2,1)} %bitcast.3), channel_id=1, source_target_pairs={{0,1},{1,0},{4,5},{5,4},{8,9},{9,8},{12,13},{13,12},{2,3},{3,2},{6... | collective-permute-start | bytes 73736 | tf_op jit(solution)/shard_map/ppermute | solution.py:213
  4.7 1.1 %collective-permute-done = bf16[1,96,128]{2,1,0:T(8,128)(2,1)S(1)} collective-permute-done((bf16[1,96,128]{2,1,0:T(8,128)(2,1)}, bf16[1,96,128]{2,1,0:T(8,128)(2,1)S(1)}, u32[]{:S(2)}, u32[]{:S(2)}) %collective-permute-start) | collective-permute-done | bytes 24608 | tf_op jit(solution)/shard_map/ppermute | solution.py:213
  5.7 0.7 %pad_maximum_fusion.2 = bf16[2,96,128]{2,1,0:T(8,128)(2,1)S(1)} fusion(bf16[1,96,128]{2,1,0:T(8,128)(2,1)S(1)} %collective-permute-done, bf16[1,96,128]{2,1,0:T(8,128)(2,1)} %bitcast.4), kind=kLoop, calls=%fused_computation.2 | loop fusion | flops 24576 | bytes 98304 | tf_op jit(solution)/shard_map/concatenate | solution.py:214
  6.5 2.9 %collective-permute-start.1 = (bf16[2,96,128]{2,1,0:T(8,128)(2,1)S(1)}, bf16[2,96,128]{2,1,0:T(8,128)(2,1)S(1)}, u32[]{:S(2)}, u32[]{:S(2)}) collective-permute-start(bf16[2,96,128]{2,1,0:T(8,128)(2,1)S(1)} %pad_maximum_fusion.2), channel_id=1, source_target_pairs={{0,4},{1,5},{4,0},{5,1},{8,12},{9,13},{12,8},{13,9},{2,6},{3,7},{6... | collective-permute-start | bytes 147464 | tf_op jit(solution)/shard_map/ppermute | solution.py:213
  9.4 2.1 %collective-permute-done.1 = bf16[2,96,128]{2,1,0:T(8,128)(2,1)S(1)} collective-permute-done((bf16[2,96,128]{2,1,0:T(8,128)(2,1)S(1)}, bf16[2,96,128]{2,1,0:T(8,128)(2,1)S(1)}, u32[]{:S(2)}, u32[]{:S(2)}) %collective-permute-start.1) | collective-permute-done | bytes 49184 | tf_op jit(solution)/shard_map/ppermute | solution.py:213
  11.5 0.0 copy-done
  11.5 3.1 %collective-permute-start.2 = (bf16[4,96,128]{2,1,0:T(8,128)(2,1)S(1)}, bf16[4,96,128]{2,1,0:T(8,128)(2,1)S(1)}, u32[]{:S(2)}, u32[]{:S(2)}) collective-permute-start(bf16[4,96,128]{2,1,0:T(8,128)(2,1)S(1)} %pad_maximum_fusion.1), channel_id=1, source_target_pairs={{0,8},{1,9},{4,12},{5,13},{8,0},{9,1},{12,4},{13,5},{2,10},{3,11},... | collective-permute-start | bytes 294920 | tf_op jit(solution)/shard_map/ppermute | solution.py:213
  14.6 4.1 %collective-permute-done.2 = bf16[4,96,128]{2,1,0:T(8,128)(2,1)S(1)} collective-permute-done((bf16[4,96,128]{2,1,0:T(8,128)(2,1)S(1)}, bf16[4,96,128]{2,1,0:T(8,128)(2,1)S(1)}, u32[]{:S(2)}, u32[]{:S(2)}) %collective-permute-start.2) | collective-permute-done | bytes 98336 | tf_op jit(solution)/shard_map/ppermute | solution.py:213
  18.7 0.7 %pad_maximum_fusion.gathered_ref = bf16[8,96,128]{2,1,0:T(8,128)(2,1)} fusion(bf16[4,96,128]{2,1,0:T(8,128)(2,1)S(1)} %collective-permute-done.2, bf16[2,96,128]{2,1,0:T(8,128)(2,1)S(1)} %collective-permute-done.1, bf16[1,96,128]{2,1,0:T(8,128)(2,1)S(1)} %collective-permute-done, bf16[1,96,128]{2,1,0:T(8,128)(2,1)S(1)} %bitcast.6), kind=kLoop, calls=%fused_computation | loop fusion | flops 294912 | bytes 393216 | tf_op jit(solution)/shard_map/concatenate | solution.py:214
  19.4 3.1 %march.1 = (bf16[1,32,512]{2,1,0:T(8,128)(2,1)}, f32[8,32]{1,0:T(8,128)}) custom-call(s32[1]{0:T(128)} %bitcast.owner_ref.place_ref, bf16[8,96,128]{2,1,0:T(8,128)(2,1)} %pad_maximum_fusion.gathered_ref, bf16[128,896]{1,0:T(8,128)(2,1)} %constant.13.clone.spread_ref, bf16[64,512]{1,0:T(8,128)(2,1)} %get-tuple-element.5.rows_ref), custom_call_target="tpu_custom_call" | custom-call | tf_op jit(solution)/shard_map/march/pallas_call | solution.py:216
  (1 shorter events, 0.0 us)
Async XLA Ops:
  4.2 7.3 %copy-start = (bf16[96,128]{1,0:T(8,128)(2,1)S(1)}, bf16[96,128]{1,0:T(8,128)(2,1)}, u32[]{:S(2)}) copy-start(bf16[96,128]{1,0:T(8,128)(2,1)} %get-tuple-element.4) | copy-start | bytes 73732
  4.2 1.6 %collective-permute-start = (bf16[1,96,128]{2,1,0:T(8,128)(2,1)}, bf16[1,96,128]{2,1,0:T(8,128)(2,1)S(1)}, u32[]{:S(2)}, u32[]{:S(2)}) collective-permute-start(bf16[1,96,128]{2,1,0:T(8,128)(2,1)} %bitcast.3), channel_id=1, source_target_pairs={{0,1},{1,0},{4,5},{5,4},{8,9},{9,8},{12,13},{13,12},{2,3},{3,2},{6... | collective-permute-start | bytes 73736 | tf_op jit(solution)/shard_map/ppermute | solution.py:213
  6.5 5.0 %collective-permute-start.1 = (bf16[2,96,128]{2,1,0:T(8,128)(2,1)S(1)}, bf16[2,96,128]{2,1,0:T(8,128)(2,1)S(1)}, u32[]{:S(2)}, u32[]{:S(2)}) collective-permute-start(bf16[2,96,128]{2,1,0:T(8,128)(2,1)S(1)} %pad_maximum_fusion.2), channel_id=1, source_target_pairs={{0,4},{1,5},{4,0},{5,1},{8,12},{9,13},{12,8},{13,9},{2,6},{3,7},{6... | collective-permute-start | bytes 147464 | tf_op jit(solution)/shard_map/ppermute | solution.py:213
  11.5 7.2 %collective-permute-start.2 = (bf16[4,96,128]{2,1,0:T(8,128)(2,1)S(1)}, bf16[4,96,128]{2,1,0:T(8,128)(2,1)S(1)}, u32[]{:S(2)}, u32[]{:S(2)}) collective-permute-start(bf16[4,96,128]{2,1,0:T(8,128)(2,1)S(1)} %pad_maximum_fusion.1), channel_id=1, source_target_pairs={{0,8},{1,9},{4,12},{5,13},{8,0},{9,1},{12,4},{13,5},{2,10},{3,11},... | collective-permute-start | bytes 294920 | tf_op jit(solution)/shard_map/ppermute | solution.py:213

commit v2 on v1

--- a/solution.py
+++ b/solution.py
@@ -8,6 +8,8 @@
 
 STEPS = 8
 LANES = 128
+VMEM_LIMIT = 16 * 2**20
+BANDS = 2
 OWNER_AXES = ("sub", "half")
 VARIANTS = (
     (2, 3, 0, 2),
@@ -18,25 +20,47 @@
     (4, 5, 3, 4),
 )
 NT = (((1,), (1,)), ((), ()))
-TN = (((0,), (0,)), ((), ()))
 
 
 def dot(left, right, dims=(((1,), (0,)), ((), ()))):
     return lax.dot_general(left, right, dims, preferred_element_type=jnp.float32)
 
 
-def spread_matrix(column_count, slot_count):
-    spread = np.zeros((LANES, (len(VARIANTS) + 1) * LANES), np.float32)
+def spread_matrix(column_count, owners):
+    half = LANES // 2
+    spread = np.zeros((LANES, (len(VARIANTS) + 2) * LANES), np.float32)
     for variant, gaps in enumerate(VARIANTS):
         for quarter, gap in enumerate(gaps):
-            if gap:
-                lane = variant * LANES + quarter * column_count
-                for piece in range(3):
-                    row = slot_count + column_count + 3 * (gap - 2) + piece
-                    spread[row, lane : lane + column_count] = 1
+            lane = variant * LANES + quarter * column_count
+            for piece in range(3 * (gap - 2), 3 * (gap - 1)) if gap else ():
+                for owner in range(owners):
+                    spread[piece // 8 * half + owner * 8 + piece % 8, lane : lane + column_count] = 1
     for lane in range(LANES):
-        spread[slot_count + lane % column_count, len(VARIANTS) * LANES + lane] = 1
+        for part in range(2):
+            start = half + part * column_count
+            spread[start + lane % column_count, (len(VARIANTS) + part) * LANES + lane] = 1
     return spread
+
+
+def exchange_masks(owners):
+    masks = []
+    reach = owners // 2
+    while reach > 1:
+        masks.append(reach + 1)
+        reach //= 2
+    return masks + [1]
+
+
+def held_spots(owners):
+    masks = exchange_masks(owners)
+    place_of = {}
+    for place in range(owners):
+        apart = 0
+        for bit, mask in enumerate(masks):
+            if place >> bit & 1:
+                apart ^= mask
+        place_of[apart] = place
+    return [place_of[1 << bit] for bit in range(len(masks))]
 
 
 def column_of(ref, peers, depth):
@@ -50,18 +74,39 @@
     return jnp.sum(jnp.concatenate(rows, axis=0), axis=1, keepdims=True)
 
 
+def owner_here():
+    return lax.axis_index(OWNER_AXES[0]) * lax.axis_size(OWNER_AXES[1]) + lax.axis_index(OWNER_AXES[1])
+
+
 def pick_kernel(
-    size_ref, owner_ref, inverse_hbm, cotangent_ref, into_ref, from_ref, offset_ref, weight_ref, admit_ref, bus_ref,
-    message_ref, rows_ref, inverse_ref, semaphore,
+    size_ref, inverse_hbm, cotangent_hbm, into_hbm, from_hbm, offset_hbm, weight_hbm, admit_hbm, bus_hbm,
+    message_ref, rows_ref,
+    inverse_ref, cotangent_ref, into_ref, from_ref, offset_ref, weight_ref, admit_ref, bus_ref, semaphores,
 ):
-    load = pltpu.make_async_copy(inverse_hbm.at[0], inverse_ref, semaphore)
-    load.start()
+    sources = (into_hbm, from_hbm, offset_hbm, weight_hbm, admit_hbm, bus_hbm, cotangent_hbm)
+    targets = (into_ref, from_ref, offset_ref, weight_ref, admit_ref, bus_ref, cotangent_ref)
+    loads = [
+        pltpu.make_async_copy(source, target, semaphores.at[index])
+        for index, (source, target) in enumerate(zip(sources, targets))
+    ]
+    for load in loads:
+        load.start()
+    nodes = inverse_ref.shape[0]
+    bands = [pl.ds(nodes // BANDS * band, nodes // BANDS) for band in range(BANDS)]
+    wide = [
+        pltpu.make_async_copy(inverse_hbm.at[0, band], inverse_ref.at[band], semaphores.at[len(loads) + index])
+        for index, band in enumerate(bands)
+    ]
+    for load in wide:
+        load.start()
     _, peers, depth = into_ref.shape
     slots = peers * depth
-    columns, nodes = cotangent_ref.shape[1:]
-    live = size_ref[0]
+    columns = cotangent_ref.shape[1]
     lane = lax.broadcasted_iota(jnp.int32, (slots, nodes), 1)
     lane_f = lane.astype(jnp.float32)
+    for load in loads:
+        load.wait()
+    live = size_ref[...]
     alive = lane < live
     into = column_of(into_ref, peers, depth)
     source = column_of(from_ref, peers, depth)
@@ -71,13 +116,12 @@
     recv_hot = jnp.where((source == lane_f) & alive, 1.0, 0.0).astype(jnp.bfloat16)
     send_hot = jnp.where(into == lane_f, 1.0, 0.0).astype(jnp.bfloat16)
     driving = jnp.where(alive[:columns], cotangent_ref[0].astype(jnp.float32), 0.0).astype(jnp.bfloat16)
-    bus = (bus_ref[...] - owner_ref[0] * nodes).astype(jnp.float32)
+    bus = (bus_ref[...] - owner_here() * nodes).astype(jnp.float32)
     eye = lax.broadcasted_iota(jnp.int32, (columns, columns), 0) == lax.broadcasted_iota(
         jnp.int32, (columns, columns), 1
     )
     bus = jnp.sum(jnp.where(eye, jnp.broadcast_to(bus, (columns, columns)), 0.0), axis=1, keepdims=True)
     fault_hot = jnp.where(bus == lane_f[:columns], 1.0, 0.0).astype(jnp.bfloat16)
-    hot = jnp.concatenate([send_hot, fault_hot], axis=0)
     conduct = jnp.where(source >= 0, admit, 0.0)
     near, far = conduct * weight, conduct * (1.0 - weight)
     factors = [
@@ -86,32 +130,59 @@
         jnp.where(delay == 4, near, 0.0) + jnp.where(delay == 3, far, 0.0),
         jnp.where(delay == 4, far, 0.0),
     ]
+    pieces = []
+    for factor in factors:
+        for _ in range(3):
+            part = factor.astype(jnp.bfloat16).astype(jnp.float32)
+            factor = factor - part
+            pieces.append(part)
     spot = lax.broadcasted_iota(jnp.int32, (slots, LANES), 1)
-    params = jnp.zeros((slots, LANES), jnp.float32)
-    for index, factor in enumerate(factors):
-        rest = factor
-        for piece in range(3):
-            part = rest.astype(jnp.bfloat16).astype(jnp.float32)
-            rest = rest - part
-            params = jnp.where(spot == slots + columns + 3 * index + piece, part, params)
-    load.wait()
+    upper = jnp.zeros((slots, LANES), jnp.float32)
+    lower = jnp.zeros((slots, LANES), jnp.float32)
+    for index, piece in enumerate(pieces):
+        if index < 8:
+            upper = jnp.where(spot == index, piece, upper)
+        else:
+            lower = jnp.where(spot == index - 8, piece, lower)
+    eye = jnp.where(
+        lax.broadcasted_iota(jnp.int32, (8, LANES), 0) == lax.broadcasted_iota(jnp.int32, (8, LANES), 1), 1.0, 0.0
+    ).astype(jnp.bfloat16)
+    table = dot(eye, jnp.concatenate([upper, lower], axis=0).astype(jnp.bfloat16), NT)
     stack = jnp.concatenate([recv_hot, driving], axis=0)
+    for load in wide:
+        load.wait()
     picked = dot(stack, inverse_ref[...])
     lane = lax.broadcasted_iota(jnp.int32, picked.shape, 1)
     picked = jnp.where(lane < live, picked, 0.0).astype(jnp.bfloat16)
-    rows_ref[...] = picked[:slots]
-    picked = jnp.concatenate([picked, jnp.zeros((LANES - slots - columns, nodes), jnp.bfloat16)], axis=0)
-    body = dot(hot, picked, NT)
-    body = body + jnp.concatenate([params, jnp.zeros((columns, LANES), jnp.float32)], axis=0)
-    message_ref[...] = body.astype(jnp.bfloat16)
-
-
-def march_kernel(place_ref, gathered_ref, spread_ref, rows_ref, first_ref, fault_ref, last_ref):
-    owners, height, _ = gathered_ref.shape
+    rows = picked[:slots]
+    rows_ref[...] = rows
+    blank = jnp.zeros((columns, nodes), jnp.bfloat16)
+    body = dot(send_hot, jnp.concatenate([picked, blank], axis=0), NT) + dot(
+        rows, jnp.concatenate([blank] * (slots // columns + 1) + [fault_hot], axis=0), NT
+    )
+    found = jnp.concatenate([blank] * (slots // columns) + [picked[slots:] * fault_hot, blank], axis=0)
+    last = jnp.where(lax.broadcasted_iota(jnp.int32, (8, nodes), 0) == 7, 1.0, 0.0).astype(jnp.bfloat16)
+    table = table + dot(last, found, NT)
+    message_ref[...] = jnp.concatenate([body, table], axis=0).astype(jnp.bfloat16)
+
+
+def march_kernel(
+    gathered_ref, spread_ref, rows_ref, first_hbm, fault_hbm, last_ref, first_ref, fault_ref, semaphores
+):
+    owners = gathered_ref.shape[0]
     slots = rows_ref.shape[0]
-    columns = height - slots
+    columns = first_ref.shape[1]
     depth = slots // owners
-    place = place_ref[0]
+    count = len(VARIANTS)
+    place = owner_here()
+    spots = held_spots(owners)
+
+    def held_at(owner):
+        apart = lax.bitwise_xor(jnp.int32(owner), place)
+        spot = 0
+        for bit in range(len(spots)):
+            spot = lax.bitwise_xor(spot, ((apart >> bit) & 1) * spots[bit])
+        return spot
 
     def exchange(parts):
         return [
@@ -122,47 +193,54 @@
     def rounded(value):
         return value.astype(jnp.bfloat16).astype(jnp.float32)
 
-    blocks = [gathered_ref[lax.bitwise_xor(jnp.int32(owner), place)] for owner in range(owners)]
-    count = len(VARIANTS)
-    spread = [dot(block[:slots], spread_ref[...]) for block in blocks]
-    factor = [[part[:, LANES * v : LANES * (v + 1)] for part in spread] for v in range(count)]
-    seven = exchange([part[:, LANES * count :] for part in spread])
+    def lanes(value, index):
+        return value[:, LANES * index : LANES * (index + 1)]
+
+    places = [held_at(owner) for owner in range(owners)]
+    blocks = [gathered_ref[spot, :slots, :] for spot in places]
+    tables = jnp.concatenate([gathered_ref[spot, slots:, :].astype(jnp.float32) for spot in places], axis=0)
+    turned = jnp.concatenate([tables, tables], axis=0).T
+    lane = lax.broadcasted_iota(jnp.int32, (slots, LANES), 1)
+    turned = jnp.where(lane < LANES // 2, turned[:slots], turned[slots:])
+    owner_lane = lane % (LANES // 2) // 8
+    pieces = [jnp.where(owner_lane == o, turned, 0.0).astype(jnp.bfloat16) for o in range(owners)]
+    factor = [dot(piece, spread_ref[:, : LANES * count]) for piece in pieces]
+    factor = [[lanes(part, v) for part in factor] for v in range(count)]
+    repeated = [dot(block, spread_ref[:, LANES * count :]) for block in blocks]
+    seven = exchange([lanes(part, 0) for part in repeated])
+    fault = [lanes(part, 1) for part in repeated]
     system = [block[:, :slots] for block in blocks]
 
+    def seen(drive):
+        total = fault[0] * drive[0].astype(jnp.float32)
+        for o in range(1, owners):
+            total = total + fault[o] * drive[o].astype(jnp.float32)
+        return rounded(jnp.sum(total, axis=0, keepdims=True))
+
+    near = [(factor[0][o] * seven[o]).astype(jnp.bfloat16) for o in range(owners)]
+    wide = [(factor[1][o] * seven[o]).astype(jnp.bfloat16) for o in range(owners)]
+    result = [dot(system[o], jnp.concatenate([near[o], wide[o]], axis=1)) for o in range(owners)]
+    row_a = seen(near)
+    arrived = exchange([rounded(part) for part in result])
     drive = [
-        jnp.concatenate([factor[0][o] * seven[o], factor[1][o] * seven[o]], axis=1).astype(jnp.bfloat16)
+        factor[2][o] * seven[o] + factor[3][o] * lanes(arrived[o], 0) + factor[4][o] * lanes(arrived[o], 1)
         for o in range(owners)
     ]
+    drive = [part.astype(jnp.bfloat16) for part in drive]
+    later = [factor[5][o] * lanes(arrived[o], 1) for o in range(owners)]
     result = [dot(system[o], drive[o]) for o in range(owners)]
-    fault_a = sum(part[slots:, :LANES] for part in result[1:]) + result[0][slots:, :LANES]
-    arrived = exchange([rounded(part) for part in result])
-    low = [part[:, :LANES] for part in arrived]
-    high = [part[:, LANES:] for part in arrived]
-    drive = [
-        (factor[2][o] * seven[o] + factor[3][o] * low[o] + factor[4][o] * high[o]).astype(jnp.bfloat16)
-        for o in range(owners)
-    ]
-    later = [factor[5][o] * high[o] for o in range(owners)]
-    result = [dot(system[o], drive[o]) for o in range(owners)]
-    fault_b = sum(part[slots:] for part in result[1:]) + result[0][slots:]
+    row_b = seen(drive)
     arrived = exchange([rounded(part) for part in result])
     later = [later[o] + factor[1][o] * arrived[o] for o in range(owners)]
-    drive = [(part + pltpu.roll(part, 2 * columns, 1)).astype(jnp.bfloat16) for part in later]
+    drive = [part + pltpu.roll(part, 2 * columns, 1) for part in later]
     for o in range(owners):
         last_ref[o] = drive[o]
-    own = last_ref[place]
-    adjoint = dot(own, rows_ref[...], TN)
-    first_ref[0] = adjoint[columns : 2 * columns].astype(jnp.bfloat16)
-    fault_c = sum(dot(system[o][slots:], drive[o]) for o in range(owners))
-    fault_s = sum(block[slots:].astype(jnp.float32) for block in blocks)
-
-    lane = lax.broadcasted_iota(jnp.int32, (columns, LANES), 1)
-    mine = lane % columns == lax.broadcasted_iota(jnp.int32, (columns, LANES), 0)
-
-    def row(value):
-        return rounded(jnp.sum(jnp.where(mine, value, 0.0), axis=0, keepdims=True))
-
-    row_a, row_b, row_c, row_s = row(fault_a), row(fault_b), row(fault_c), row(fault_s)
+    own = last_ref[place].T[columns : 2 * columns].astype(jnp.bfloat16)
+    first_ref[0] = dot(own, rows_ref[...]).astype(jnp.bfloat16)
+    save_first = pltpu.make_async_copy(first_ref, first_hbm, semaphores.at[0])
+    save_first.start()
+    row_c = seen([part.astype(jnp.bfloat16) for part in drive])
+    row_s = sum(tables[8 * o + 7 : 8 * o + 8] for o in range(owners))
 
     def back(value, quarters):
         return pltpu.roll(value, LANES - quarters * columns, 1)
@@ -182,6 +260,10 @@
     for index, value in enumerate(table):
         total = jnp.where(step == index, jnp.broadcast_to(value, total.shape), total)
     fault_ref[...] = total[:, :columns]
+    save_fault = pltpu.make_async_copy(fault_ref, fault_hbm, semaphores.at[1])
+    save_fault.start()
+    save_first.wait()
+    save_fault.wait()
 
 
 def gathered_plan(
@@ -190,40 +272,49 @@
     _, columns, nodes = cotangent.shape
     owners, depth = slot_into.shape[1:]
     slots = owners * depth
-    height = slots + columns
-    owner = lax.axis_index(OWNER_AXES).astype(jnp.int32)[None]
+    height = slots + 8
     vmem = pl.BlockSpec(memory_space=pltpu.VMEM)
-    smem = pl.BlockSpec(memory_space=pltpu.SMEM)
+    hbm = pl.BlockSpec(memory_space=pltpu.HBM)
+    arrays = (
+        subnet_sizes[None], inverses, cotangent, slot_into, slot_from, offsets, weights, admittance, fault_bus[None],
+    )
     message, rows = pl.pallas_call(
         pick_kernel,
         out_shape=(
             jax.ShapeDtypeStruct((height, LANES), jnp.bfloat16),
             jax.ShapeDtypeStruct((slots, nodes), jnp.bfloat16),
         ),
-        in_specs=[smem, smem, pl.BlockSpec(memory_space=pl.ANY)] + [vmem] * 7,
+        in_specs=[vmem] + [hbm] * (len(arrays) - 1),
         out_specs=(vmem, vmem),
-        scratch_shapes=[pltpu.VMEM((nodes, nodes), jnp.bfloat16), pltpu.SemaphoreType.DMA],
+        scratch_shapes=[
+            pltpu.VMEM(array.shape[1:] if array is inverses else array.shape, array.dtype) for array in arrays[1:]
+        ]
+        + [pltpu.SemaphoreType.DMA((len(arrays) - 2 + BANDS,))],
+        compiler_params=pltpu.CompilerParams(vmem_limit_bytes=VMEM_LIMIT),
         name="pick",
-    )(
-        subnet_sizes, owner, inverses, cotangent, slot_into, slot_from, offsets, weights, admittance, fault_bus[None],
-    )
-    bits = owners.bit_length() - 1
+    )(arrays[0], *(pltpu.with_memory_space_constraint(array, pltpu.HBM) for array in arrays[1:]))
     held = message[None]
-    for bit in range(bits):
-        other = lax.ppermute(held, OWNER_AXES, [(i, i ^ (1 << bit)) for i in range(owners)])
+    for mask in exchange_masks(owners):
+        other = lax.ppermute(held, OWNER_AXES, [(i, i ^ mask) for i in range(owners)])
         held = jnp.concatenate([held, other], axis=0)
-    spread = jnp.asarray(spread_matrix(columns, slots), jnp.bfloat16)
+    spread = jnp.asarray(spread_matrix(columns, owners), jnp.bfloat16)
+    outputs = (
+        jax.ShapeDtypeStruct((1, columns, nodes), jnp.bfloat16),
+        jax.ShapeDtypeStruct((STEPS, columns), jnp.float32),
+    )
     return pl.pallas_call(
         march_kernel,
-        out_shape=(
-            jax.ShapeDtypeStruct((1, columns, nodes), jnp.bfloat16),
-            jax.ShapeDtypeStruct((STEPS, columns), jnp.float32),
-        ),
-        in_specs=[smem, vmem, vmem, vmem],
-        out_specs=(vmem, vmem),
-        scratch_shapes=[pltpu.VMEM((owners, slots, LANES), jnp.bfloat16)],
+        out_shape=outputs,
+        in_specs=[vmem] * 3,
+        out_specs=(hbm, hbm),
+        scratch_shapes=[
+            pltpu.VMEM((owners, slots, LANES), jnp.float32),
+            *(pltpu.VMEM(output.shape, output.dtype) for output in outputs),
+            pltpu.SemaphoreType.DMA((2,)),
+        ],
+        compiler_params=pltpu.CompilerParams(vmem_limit_bytes=VMEM_LIMIT),
         name="march",
-    )(owner, held, spread, rows)
+    )(held, spread, rows)
 
 
 def exchanged_plan(
@@ -307,7 +398,7 @@
         and columns * 4 == LANES
         and depth == 8
         and owners & (owners - 1) == 0
-        and slots + columns + 12 <= LANES
+        and slots + 2 * columns == LANES
         and nodes % LANES == 0
     )
     return gathered_plan(*arrays) if fits else exchanged_plan(*arrays)

time: 22.8 us -> 15.1 us (0.66)
  waiting for transfers between devices: 7.22 us -> 4.03 us
  Pallas kernels: 5.93 us -> 3.51 us
  other arithmetic: 1.45 us -> 0.03 us
  starting transfers between devices: 6.54 us -> 6.01 us
    ppermute x3, waiting for transfers between devices: 7.22 us -> 4.03 us  [gathered_plan(): lax.ppermute(held, OWNER_AXES, [(i, i ^ mask) for i in range(owners)])]
    concatenate x3, other arithmetic: 1.45 us -> 0.03 us  [gathered_plan(): held = jnp.concatenate([held, other], axis=0)]
    pallas_call x1, Pallas kernels: 2.87 us -> 1.65 us  [gathered_plan(): pl.pallas_call(pick_kernel, out_shape=(jax.ShapeDtypeStruct((height, LANE...]
    pallas_call x1, Pallas kernels: 3.06 us -> 1.86 us  [gathered_plan(): pl.pallas_call(march_kernel, out_shape=outputs, in_specs=[vmem] * 3, out_...]
    ppermute x3, starting transfers between devices: 6.54 us -> 6.01 us  [gathered_plan(): lax.ppermute(held, OWNER_AXES, [(i, i ^ mask) for i in range(owners)])]
where the time goes in v2:
time: 15.1 us; the launch traced here: 14.9 us
  starting transfers between devices  6.01 us (40%)
  waiting for transfers between devices  4.03 us (27%)
  Pallas kernels  3.51 us (23%)
  between operations  1.31 us (9%)
    ppermute x3, starting transfers between devices, gathered_plan(): lax.ppermute(held, OWNER_AXES, [(i, i ^ mask) for i in range(owners)])  6.01 us
    ppermute x3, waiting for transfers between devices, gathered_plan(): lax.ppermute(held, OWNER_AXES, [(i, i ^ mask) for i in range(owners)])  4.03 us
    pallas_call x1, Pallas kernels, gathered_plan(): pl.pallas_call(march_kernel, out_shape=outputs, in_specs=[vmem] * 3, out_...  1.86 us
    pallas_call x1, Pallas kernels, gathered_plan(): pl.pallas_call(pick_kernel, out_shape=(jax.ShapeDtypeStruct((height, LANE...  1.65 us
  transfers between devices with their start and end apart: 3, of which 3 were waited for; matrix products, arithmetic and copies ran while one was open for 0% of the time, Pallas kernels for 0%

profile of v2, /device:TPU:0, one launch (start us, length us, event | category | flops | bytes accessed | tf_op | source)
XLA Modules:
  0.0 14.9 jit_solution(17691386885261307829)
XLA Ops:
  1.3 1.7 %pick.1 = (bf16[72,128]{1,0:T(8,128)(2,1)S(1)}, bf16[64,512]{1,0:T(8,128)(2,1)S(1)}) custom-call(s32[1,1]{1,0:T(1,128)} %bitcast.3.size_ref, bf16[1,512,512]{2,1,0:T(8,128)(2,1)} %inverse_hbm.1, bf16[1,32,512]{2,1,0:T(8,128)(2,1)} %cotangent_hbm.1, s32[1,8,8]{2,1,0:T(8,128)} %into_hbm.1, s32[1,8,8]{2,1,0:T(8,128)} %from_hbm.1, s32[1,8,8]{2,1,0:T(8,128)} %offset_hbm.1, ...), custom_call_target="tpu_custom_call" | custom-call | tf_op jit(solution)/shard_map/pick/pallas_call | solution.py:281
  2.9 0.0 copy-start
  3.0 3.5 %collective-permute-start = (bf16[1,72,128]{2,1,0:T(8,128)(2,1)S(1)}, bf16[1,72,128]{2,1,0:T(8,128)(2,1)S(1)}, u32[]{:S(2)}, u32[]{:S(2)}) collective-permute-start(bf16[1,72,128]{2,1,0:T(8,128)(2,1)S(1)} %bitcast.4), channel_id=1, source_target_pairs={{0,9},{1,8},{4,13},{5,12},{8,1},{9,0},{12,5},{13,4},{2,11},{3,10},... | collective-permute-start | bytes 55304 | tf_op jit(solution)/shard_map/ppermute | solution.py:298
  6.5 1.5 %collective-permute-done = bf16[1,72,128]{2,1,0:T(8,128)(2,1)S(1)} collective-permute-done((bf16[1,72,128]{2,1,0:T(8,128)(2,1)S(1)}, bf16[1,72,128]{2,1,0:T(8,128)(2,1)S(1)}, u32[]{:S(2)}, u32[]{:S(2)}) %collective-permute-start) | collective-permute-done | bytes 18464 | tf_op jit(solution)/shard_map/ppermute | solution.py:298
  8.0 1.9 %collective-permute-start.1 = (bf16[2,72,128]{2,1,0:T(8,128)(2,1)S(1)}, bf16[2,72,128]{2,1,0:T(8,128)(2,1)S(1)}, u32[]{:S(2)}, u32[]{:S(2)}) collective-permute-start(bf16[2,72,128]{2,1,0:T(8,128)(2,1)S(1)} %pad_maximum_fusion.2), channel_id=1, source_target_pairs={{0,5},{1,4},{4,1},{5,0},{8,13},{9,12},{12,9},{13,8},{2,7},{3,6},{6... | collective-permute-start | bytes 110600 | tf_op jit(solution)/shard_map/ppermute | solution.py:298
  9.9 1.6 %collective-permute-done.1 = bf16[2,72,128]{2,1,0:T(8,128)(2,1)S(1)} collective-permute-done((bf16[2,72,128]{2,1,0:T(8,128)(2,1)S(1)}, bf16[2,72,128]{2,1,0:T(8,128)(2,1)S(1)}, u32[]{:S(2)}, u32[]{:S(2)}) %collective-permute-start.1) | collective-permute-done | bytes 36896 | tf_op jit(solution)/shard_map/ppermute | solution.py:298
  11.5 0.6 %collective-permute-start.2 = (bf16[4,72,128]{2,1,0:T(8,128)(2,1)S(1)}, bf16[4,72,128]{2,1,0:T(8,128)(2,1)S(1)}, u32[]{:S(2)}, u32[]{:S(2)}) collective-permute-start(bf16[4,72,128]{2,1,0:T(8,128)(2,1)S(1)} %pad_maximum_fusion.1), channel_id=1, source_target_pairs={{0,1},{1,0},{4,5},{5,4},{8,9},{9,8},{12,13},{13,12},{2,3},{3,2},{6... | collective-permute-start | bytes 221192 | tf_op jit(solution)/shard_map/ppermute | solution.py:298
  12.1 0.9 %collective-permute-done.2 = bf16[4,72,128]{2,1,0:T(8,128)(2,1)S(1)} collective-permute-done((bf16[4,72,128]{2,1,0:T(8,128)(2,1)S(1)}, bf16[4,72,128]{2,1,0:T(8,128)(2,1)S(1)}, u32[]{:S(2)}, u32[]{:S(2)}) %collective-permute-start.2) | collective-permute-done | bytes 73760 | tf_op jit(solution)/shard_map/ppermute | solution.py:298
  13.0 0.0 copy-done
  13.0 1.9 %march.1 = (bf16[1,32,512]{2,1,0:T(8,128)(2,1)}, f32[8,32]{1,0:T(8,128)}) custom-call(bf16[8,72,128]{2,1,0:T(8,128)(2,1)S(1)} %pad_maximum_fusion.gathered_ref, bf16[128,1024]{1,0:T(8,128)(2,1)S(1)} %copy-done, bf16[64,512]{1,0:T(8,128)(2,1)S(1)} %get-tuple-element.5.rows_ref), custom_call_target="tpu_custom_call" | custom-call | tf_op jit(solution)/shard_map/march/pallas_call | solution.py:305
  (3 shorter events, 0.0 us)
Async XLA Ops:
  2.9 10.1 %copy-start = (bf16[128,1024]{1,0:T(8,128)(2,1)S(1)}, bf16[128,1024]{1,0:T(8,128)(2,1)}, u32[]{:S(2)}) copy-start(bf16[128,1024]{1,0:T(8,128)(2,1)} %constant.2.clone.spread_ref) | copy-start | bytes 786436
  3.0 5.0 %collective-permute-start = (bf16[1,72,128]{2,1,0:T(8,128)(2,1)S(1)}, bf16[1,72,128]{2,1,0:T(8,128)(2,1)S(1)}, u32[]{:S(2)}, u32[]{:S(2)}) collective-permute-start(bf16[1,72,128]{2,1,0:T(8,128)(2,1)S(1)} %bitcast.4), channel_id=1, source_target_pairs={{0,9},{1,8},{4,13},{5,12},{8,1},{9,0},{12,5},{13,4},{2,11},{3,10},... | collective-permute-start | bytes 55304 | tf_op jit(solution)/shard_map/ppermute | solution.py:298
  8.0 3.5 %collective-permute-start.1 = (bf16[2,72,128]{2,1,0:T(8,128)(2,1)S(1)}, bf16[2,72,128]{2,1,0:T(8,128)(2,1)S(1)}, u32[]{:S(2)}, u32[]{:S(2)}) collective-permute-start(bf16[2,72,128]{2,1,0:T(8,128)(2,1)S(1)} %pad_maximum_fusion.2), channel_id=1, source_target_pairs={{0,5},{1,4},{4,1},{5,0},{8,13},{9,12},{12,9},{13,8},{2,7},{3,6},{6... | collective-permute-start | bytes 110600 | tf_op jit(solution)/shard_map/ppermute | solution.py:298
  11.5 1.5 %collective-permute-start.2 = (bf16[4,72,128]{2,1,0:T(8,128)(2,1)S(1)}, bf16[4,72,128]{2,1,0:T(8,128)(2,1)S(1)}, u32[]{:S(2)}, u32[]{:S(2)}) collective-permute-start(bf16[4,72,128]{2,1,0:T(8,128)(2,1)S(1)} %pad_maximum_fusion.1), channel_id=1, source_target_pairs={{0,1},{1,0},{4,5},{5,4},{8,9},{9,8},{12,13},{13,12},{2,3},{3,2},{6... | collective-permute-start | bytes 221192 | tf_op jit(solution)/shard_map/ppermute | solution.py:298

commit v3 on v2

--- a/solution.py
+++ b/solution.py
@@ -9,7 +9,8 @@
 STEPS = 8
 LANES = 128
 VMEM_LIMIT = 16 * 2**20
-BANDS = 2
+HINT_FLOPS = 4 * 2**30
+HINT_BYTES = 8 * 2**20
 OWNER_AXES = ("sub", "half")
 VARIANTS = (
     (2, 3, 0, 2),
@@ -51,25 +52,21 @@
     return masks + [1]
 
 
-def held_spots(owners):
-    masks = exchange_masks(owners)
-    place_of = {}
-    for place in range(owners):
-        apart = 0
-        for bit, mask in enumerate(masks):
-            if place >> bit & 1:
-                apart ^= mask
-        place_of[apart] = place
-    return [place_of[1 << bit] for bit in range(len(masks))]
-
-
-def column_of(ref, peers, depth):
+def held_order(owners):
+    far, near, core = exchange_masks(owners)
+    first = [0, far]
+    later = [near, near ^ far]
+    return first + [x ^ core for x in first] + later + [x ^ core for x in later]
+
+
+def column_of(ref, place):
+    _, peers, depth = ref.shape
     eye = lax.broadcasted_iota(jnp.int32, (depth, depth), 0) == lax.broadcasted_iota(
         jnp.int32, (depth, depth), 1
     )
     rows = [
-        jnp.where(eye, jnp.broadcast_to(ref[0, peer : peer + 1, :].astype(jnp.float32), (depth, depth)), 0.0)
-        for peer in range(peers)
+        jnp.where(eye, jnp.broadcast_to(row.astype(jnp.float32), (depth, depth)), 0.0)
+        for row in (ref[0, pl.ds(lax.bitwise_xor(place, jnp.int32(apart)), 1), :] for apart in range(peers))
     ]
     return jnp.sum(jnp.concatenate(rows, axis=0), axis=1, keepdims=True)
 
@@ -78,45 +75,31 @@
     return lax.axis_index(OWNER_AXES[0]) * lax.axis_size(OWNER_AXES[1]) + lax.axis_index(OWNER_AXES[1])
 
 
+def lane_kernel(lane_ref):
+    lane_ref[...] = lax.broadcasted_iota(jnp.int32, lane_ref.shape, 1).astype(jnp.float32)
+
+
 def pick_kernel(
-    size_ref, inverse_hbm, cotangent_hbm, into_hbm, from_hbm, offset_hbm, weight_hbm, admit_hbm, bus_hbm,
+    size_ref, lane_ref, into_ref, from_ref, offset_ref, weight_ref, admit_ref, bus_ref, inverse_ref, cotangent_ref,
     message_ref, rows_ref,
-    inverse_ref, cotangent_ref, into_ref, from_ref, offset_ref, weight_ref, admit_ref, bus_ref, semaphores,
 ):
-    sources = (into_hbm, from_hbm, offset_hbm, weight_hbm, admit_hbm, bus_hbm, cotangent_hbm)
-    targets = (into_ref, from_ref, offset_ref, weight_ref, admit_ref, bus_ref, cotangent_ref)
-    loads = [
-        pltpu.make_async_copy(source, target, semaphores.at[index])
-        for index, (source, target) in enumerate(zip(sources, targets))
-    ]
-    for load in loads:
-        load.start()
-    nodes = inverse_ref.shape[0]
-    bands = [pl.ds(nodes // BANDS * band, nodes // BANDS) for band in range(BANDS)]
-    wide = [
-        pltpu.make_async_copy(inverse_hbm.at[0, band], inverse_ref.at[band], semaphores.at[len(loads) + index])
-        for index, band in enumerate(bands)
-    ]
-    for load in wide:
-        load.start()
+    nodes = inverse_ref.shape[1]
     _, peers, depth = into_ref.shape
     slots = peers * depth
     columns = cotangent_ref.shape[1]
-    lane = lax.broadcasted_iota(jnp.int32, (slots, nodes), 1)
-    lane_f = lane.astype(jnp.float32)
-    for load in loads:
-        load.wait()
-    live = size_ref[...]
-    alive = lane < live
-    into = column_of(into_ref, peers, depth)
-    source = column_of(from_ref, peers, depth)
-    delay = column_of(offset_ref, peers, depth)
-    weight = column_of(weight_ref, peers, depth)
-    admit = column_of(admit_ref, peers, depth)
+    lane_f = jnp.broadcast_to(lane_ref[:1], (slots, nodes))
+    live = size_ref[0]
+    alive = lane_f < live.astype(jnp.float32)
+    place = owner_here()
+    into = column_of(into_ref, place)
+    source = column_of(from_ref, place)
+    delay = column_of(offset_ref, place)
+    weight = column_of(weight_ref, place)
+    admit = column_of(admit_ref, place)
     recv_hot = jnp.where((source == lane_f) & alive, 1.0, 0.0).astype(jnp.bfloat16)
     send_hot = jnp.where(into == lane_f, 1.0, 0.0).astype(jnp.bfloat16)
     driving = jnp.where(alive[:columns], cotangent_ref[0].astype(jnp.float32), 0.0).astype(jnp.bfloat16)
-    bus = (bus_ref[...] - owner_here() * nodes).astype(jnp.float32)
+    bus = (bus_ref[...] - place * nodes).astype(jnp.float32)
     eye = lax.broadcasted_iota(jnp.int32, (columns, columns), 0) == lax.broadcasted_iota(
         jnp.int32, (columns, columns), 1
     )
@@ -149,9 +132,7 @@
     ).astype(jnp.bfloat16)
     table = dot(eye, jnp.concatenate([upper, lower], axis=0).astype(jnp.bfloat16), NT)
     stack = jnp.concatenate([recv_hot, driving], axis=0)
-    for load in wide:
-        load.wait()
-    picked = dot(stack, inverse_ref[...])
+    picked = dot(stack, inverse_ref[0])
     lane = lax.broadcasted_iota(jnp.int32, picked.shape, 1)
     picked = jnp.where(lane < live, picked, 0.0).astype(jnp.bfloat16)
     rows = picked[:slots]
@@ -166,50 +147,68 @@
     message_ref[...] = jnp.concatenate([body, table], axis=0).astype(jnp.bfloat16)
 
 
+def lanes(value, index):
+    return value[:, LANES * index : LANES * (index + 1)]
+
+
+def turned_pieces(messages):
+    slots = LANES // 2
+    tables = [message[slots:].astype(jnp.float32) for message in messages]
+    filled = tables + [jnp.zeros((8, LANES), jnp.float32)] * (8 - len(tables))
+    turned = jnp.concatenate(filled * 2, axis=0).T
+    lane = lax.broadcasted_iota(jnp.int32, (slots, LANES), 1)
+    turned = jnp.where(lane < LANES // 2, turned[:slots], turned[slots:])
+    group = lane % (LANES // 2) // 8
+    return [jnp.where(group == index, turned, 0.0).astype(jnp.bfloat16) for index in range(len(messages))]
+
+
+def widen_kernel(*refs):
+    *held_refs, spread_ref, wide_ref = refs
+    messages = [ref[p] for ref in held_refs for p in range(ref.shape[0])]
+    count = LANES * len(VARIANTS)
+    for index, piece in enumerate(turned_pieces(messages)):
+        wide_ref[index, :, :count] = dot(piece, spread_ref[:, :count])
+        wide_ref[index, :, count:] = dot(messages[index][: LANES // 2], spread_ref[:, count:])
+
+
 def march_kernel(
-    gathered_ref, spread_ref, rows_ref, first_hbm, fault_hbm, last_ref, first_ref, fault_ref, semaphores
+    first_pair, first_other, later_pair, later_other, first_wide, later_wide, spread_ref, rows_ref,
+    first_hbm, fault_hbm, first_ref, fault_ref, semaphores,
 ):
-    owners = gathered_ref.shape[0]
+    held = (first_pair, first_other, later_pair, later_other)
+    owners = sum(ref.shape[0] for ref in held)
     slots = rows_ref.shape[0]
     columns = first_ref.shape[1]
     depth = slots // owners
     count = len(VARIANTS)
-    place = owner_here()
-    spots = held_spots(owners)
-
-    def held_at(owner):
-        apart = lax.bitwise_xor(jnp.int32(owner), place)
-        spot = 0
-        for bit in range(len(spots)):
-            spot = lax.bitwise_xor(spot, ((apart >> bit) & 1) * spots[bit])
-        return spot
+    order = held_order(owners)
+    spot = {apart: index for index, apart in enumerate(order)}
 
     def exchange(parts):
         return [
-            jnp.concatenate([part[depth * owner : depth * (owner + 1)] for part in parts], axis=0)
-            for owner in range(owners)
+            jnp.concatenate(
+                [parts[spot[mine ^ other]][depth * other : depth * (other + 1)] for other in range(owners)], axis=0
+            )
+            for mine in order
         ]
 
     def rounded(value):
         return value.astype(jnp.bfloat16).astype(jnp.float32)
 
-    def lanes(value, index):
-        return value[:, LANES * index : LANES * (index + 1)]
-
-    places = [held_at(owner) for owner in range(owners)]
-    blocks = [gathered_ref[spot, :slots, :] for spot in places]
-    tables = jnp.concatenate([gathered_ref[spot, slots:, :].astype(jnp.float32) for spot in places], axis=0)
-    turned = jnp.concatenate([tables, tables], axis=0).T
-    lane = lax.broadcasted_iota(jnp.int32, (slots, LANES), 1)
-    turned = jnp.where(lane < LANES // 2, turned[:slots], turned[slots:])
-    owner_lane = lane % (LANES // 2) // 8
-    pieces = [jnp.where(owner_lane == o, turned, 0.0).astype(jnp.bfloat16) for o in range(owners)]
-    factor = [dot(piece, spread_ref[:, : LANES * count]) for piece in pieces]
-    factor = [[lanes(part, v) for part in factor] for v in range(count)]
-    repeated = [dot(block, spread_ref[:, LANES * count :]) for block in blocks]
-    seven = exchange([lanes(part, 0) for part in repeated])
-    fault = [lanes(part, 1) for part in repeated]
-    system = [block[:, :slots] for block in blocks]
+    blocks = [ref[p] for ref in held for p in range(ref.shape[0])]
+    system = [block[:slots, :slots] for block in blocks]
+    fresh = blocks[-later_other.shape[0] :]
+    pieces = turned_pieces(fresh)
+
+    def spread_of(index, sources):
+        pair = slice(LANES * index, LANES * (index + 2))
+        known = [ref[p, :, pair] for ref in (first_wide, later_wide) for p in range(ref.shape[0])]
+        both = known + [dot(source, spread_ref[:, pair]) for source in sources]
+        return [lanes(part, 0) for part in both], [lanes(part, 1) for part in both]
+
+    seven, fault = spread_of(count, [block[:slots] for block in fresh])
+    seven = exchange(seven)
+    factor = [*spread_of(0, pieces)]
 
     def seen(drive):
         total = fault[0] * drive[0].astype(jnp.float32)
@@ -220,6 +219,7 @@
     near = [(factor[0][o] * seven[o]).astype(jnp.bfloat16) for o in range(owners)]
     wide = [(factor[1][o] * seven[o]).astype(jnp.bfloat16) for o in range(owners)]
     result = [dot(system[o], jnp.concatenate([near[o], wide[o]], axis=1)) for o in range(owners)]
+    factor += [*spread_of(2, pieces), *spread_of(4, pieces)]
     row_a = seen(near)
     arrived = exchange([rounded(part) for part in result])
     drive = [
@@ -233,14 +233,12 @@
     arrived = exchange([rounded(part) for part in result])
     later = [later[o] + factor[1][o] * arrived[o] for o in range(owners)]
     drive = [part + pltpu.roll(part, 2 * columns, 1) for part in later]
-    for o in range(owners):
-        last_ref[o] = drive[o]
-    own = last_ref[place].T[columns : 2 * columns].astype(jnp.bfloat16)
+    own = drive[0].T[columns : 2 * columns].astype(jnp.bfloat16)
     first_ref[0] = dot(own, rows_ref[...]).astype(jnp.bfloat16)
     save_first = pltpu.make_async_copy(first_ref, first_hbm, semaphores.at[0])
     save_first.start()
     row_c = seen([part.astype(jnp.bfloat16) for part in drive])
-    row_s = sum(tables[8 * o + 7 : 8 * o + 8] for o in range(owners))
+    row_s = sum(block[slots + 7 : slots + 8].astype(jnp.float32) for block in blocks)
 
     def back(value, quarters):
         return pltpu.roll(value, LANES - quarters * columns, 1)
@@ -275,8 +273,18 @@
     height = slots + 8
     vmem = pl.BlockSpec(memory_space=pltpu.VMEM)
     hbm = pl.BlockSpec(memory_space=pltpu.HBM)
+    smem = pl.BlockSpec(memory_space=pltpu.SMEM)
+    lane = pl.pallas_call(
+        lane_kernel,
+        out_shape=jax.ShapeDtypeStruct((8, nodes), jnp.float32),
+        out_specs=vmem,
+        compiler_params=pltpu.CompilerParams(vmem_limit_bytes=VMEM_LIMIT),
+        cost_estimate=pl.CostEstimate(flops=HINT_FLOPS, bytes_accessed=HINT_BYTES, transcendentals=0),
+        name="lane",
+    )()
+    lane, sizes = lax.optimization_barrier((lane, subnet_sizes))
     arrays = (
-        subnet_sizes[None], inverses, cotangent, slot_into, slot_from, offsets, weights, admittance, fault_bus[None],
+        sizes, lane, slot_into, slot_from, offsets, weights, admittance, fault_bus[None], inverses, cotangent,
     )
     message, rows = pl.pallas_call(
         pick_kernel,
@@ -284,20 +292,38 @@
             jax.ShapeDtypeStruct((height, LANES), jnp.bfloat16),
             jax.ShapeDtypeStruct((slots, nodes), jnp.bfloat16),
         ),
-        in_specs=[vmem] + [hbm] * (len(arrays) - 1),
+        in_specs=[smem] + [vmem] * (len(arrays) - 1),
         out_specs=(vmem, vmem),
-        scratch_shapes=[
-            pltpu.VMEM(array.shape[1:] if array is inverses else array.shape, array.dtype) for array in arrays[1:]
-        ]
-        + [pltpu.SemaphoreType.DMA((len(arrays) - 2 + BANDS,))],
         compiler_params=pltpu.CompilerParams(vmem_limit_bytes=VMEM_LIMIT),
         name="pick",
-    )(arrays[0], *(pltpu.with_memory_space_constraint(array, pltpu.HBM) for array in arrays[1:]))
-    held = message[None]
-    for mask in exchange_masks(owners):
-        other = lax.ppermute(held, OWNER_AXES, [(i, i ^ mask) for i in range(owners)])
-        held = jnp.concatenate([held, other], axis=0)
-    spread = jnp.asarray(spread_matrix(columns, owners), jnp.bfloat16)
+    )(*arrays)
+    spread = jnp.asarray(spread_matrix(columns, 8), jnp.bfloat16)
+    width = spread.shape[1]
+
+    def swap(held, mask):
+        return lax.ppermute(held, OWNER_AXES, [(i, i ^ mask) for i in range(owners)])
+
+    def widen(*held):
+        count = sum(part.shape[0] for part in held)
+        return pl.pallas_call(
+            widen_kernel,
+            out_shape=jax.ShapeDtypeStruct((count, slots, width), jnp.float32),
+            in_specs=[vmem] * (len(held) + 1),
+            out_specs=vmem,
+            compiler_params=pltpu.CompilerParams(vmem_limit_bytes=VMEM_LIMIT),
+            cost_estimate=pl.CostEstimate(
+                flops=2 * count * slots * LANES * width, bytes_accessed=4 * count * slots * width, transcendentals=0
+            ),
+            name="widen",
+        )(*held, spread)
+
+    far, near, core = exchange_masks(owners)
+    first = jnp.concatenate([message[None], swap(message[None], far)], axis=0)
+    later = swap(first, near)
+    first_other = swap(first, core)
+    first_wide = widen(first, first_other)
+    later_other = swap(later, core)
+    later_wide = widen(later)
     outputs = (
         jax.ShapeDtypeStruct((1, columns, nodes), jnp.bfloat16),
         jax.ShapeDtypeStruct((STEPS, columns), jnp.float32),
@@ -305,16 +331,15 @@
     return pl.pallas_call(
         march_kernel,
         out_shape=outputs,
-        in_specs=[vmem] * 3,
+        in_specs=[vmem] * 8,
         out_specs=(hbm, hbm),
         scratch_shapes=[
-            pltpu.VMEM((owners, slots, LANES), jnp.float32),
             *(pltpu.VMEM(output.shape, output.dtype) for output in outputs),
             pltpu.SemaphoreType.DMA((2,)),
         ],
         compiler_params=pltpu.CompilerParams(vmem_limit_bytes=VMEM_LIMIT),
         name="march",
-    )(held, spread, rows)
+    )(first, first_other, later, later_other, first_wide, later_wide, spread, rows)
 
 
 def exchanged_plan(
@@ -397,7 +422,7 @@
         blocks == 1
         and columns * 4 == LANES
         and depth == 8
-        and owners & (owners - 1) == 0
+        and owners == 8
         and slots + 2 * columns == LANES
         and nodes % LANES == 0
     )

time: 15.1 us -> 14.2 us (0.940)
  waiting for transfers between devices: 4.03 us -> 2.92 us
  Pallas kernels: 3.51 us -> 2.64 us
  local copies, waits for them, and re-layouts: 0.01 us -> 0.69 us
  starting transfers between devices: 6.01 us -> 6.3 us
    pallas_call x1, Pallas kernels: 1.65 us -> 0.49 us  [gathered_plan(): pl.pallas_call(pick_kernel, out_shape=(jax.ShapeDtypeStruct((height, LANE...]
    ppermute x3 -> x4, waiting for transfers between devices: 4.03 us -> 2.92 us  [swap(): lax.ppermute(held, OWNER_AXES, [(i, i ^ mask) for i in range(owners)])]
    unnamed x2 -> x18, local copies, waits for them, and re-layouts: 0.01 us -> 0.69 us
    ppermute x3 -> x4, starting transfers between devices: 6.01 us -> 6.3 us  [swap(): lax.ppermute(held, OWNER_AXES, [(i, i ^ mask) for i in range(owners)])]
    pallas_call x1 -> x4, Pallas kernels: 1.86 us -> 2.14 us  [the longest x1 1.49 us: gathered_plan(): pl.pallas_call(march_kernel, out_shape=outputs, in_specs=[vmem] * 8, out_...]
  transfers between devices with their start and end apart: 3 -> 4, of which waited for: 3 -> 3; matrix products, arithmetic and copies ran while one was open for 0% -> 0% of each run, Pallas kernels for 0% -> 5%
where the time goes in v3:
time: 14.2 us; the launch traced here: 14 us
  starting transfers between devices  6.3 us (44%)
  waiting for transfers between devices  2.92 us (21%)
  Pallas kernels  2.64 us (19%)
  between operations  1.44 us (10%)
  local copies, waits for them, and re-layouts  0.69 us (5%)
    ppermute x4, starting transfers between devices, swap(): lax.ppermute(held, OWNER_AXES, [(i, i ^ mask) for i in range(owners)])  6.3 us
    ppermute x4, waiting for transfers between devices, swap(): lax.ppermute(held, OWNER_AXES, [(i, i ^ mask) for i in range(owners)])  2.92 us
    pallas_call x1, Pallas kernels, gathered_plan(): pl.pallas_call(march_kernel, out_shape=outputs, in_specs=[vmem] * 8, out_...  1.49 us
    unnamed x18, local copies, waits for them, and re-layouts  0.69 us
    pallas_call x2, Pallas kernels, widen(): pl.pallas_call(widen_kernel, out_shape=jax.ShapeDtypeStruct((count, slots...  0.64 us
    pallas_call x1, Pallas kernels, gathered_plan(): pl.pallas_call(pick_kernel, out_shape=(jax.ShapeDtypeStruct((height, LANE...  0.49 us
  transfers between devices with their start and end apart: 4, of which 3 were waited for; matrix products, arithmetic and copies ran while one was open for 0% of the time, Pallas kernels for 5%

profile of v3, /device:TPU:0, one launch (start us, length us, event | category | flops | bytes accessed | tf_op | source)
XLA Modules:
  0.0 14.0 jit_solution(11350693957106434608)
XLA Ops:
  0.6 0.0 copy-start.2
  0.6 0.0 copy-start.1
  0.7 0.0 copy-start.3
  0.7 0.0 copy-start.4
  0.7 0.0 copy-start.5
  0.7 0.0 copy-start.6
  0.7 0.0 copy-start.7
  1.4 0.0 copy-start.8
  1.4 0.0 copy-done.2
  1.4 0.3 %copy-done.1 = bf16[1,512,512]{2,1,0:T(8,128)(2,1)S(1)} copy-done((bf16[1,512,512]{2,1,0:T(8,128)(2,1)S(1)}, bf16[1,512,512]{2,1,0:T(8,128)(2,1)}, u32[]{:S(2)}) %copy-start.1) | copy-done | bytes 524312
  1.7 0.0 copy-done.3
  1.7 0.0 copy-done.4
  1.7 0.0 copy-done.5
  1.7 0.0 copy-done.6
  1.7 0.0 copy-done.7
  1.7 0.4 %copy-done.8 = s32[32]{0:T(128)S(1)} copy-done((s32[32]{0:T(128)S(1)}, s32[32]{0:T(128)}, u32[]{:S(2)}) %copy-start.8) | copy-done | bytes 152
  2.1 0.0 copy-start
  2.1 0.5 %pick.1 = (bf16[72,128]{1,0:T(8,128)(2,1)S(1)}, bf16[64,512]{1,0:T(8,128)(2,1)S(1)}) custom-call(s32[1]{0:T(128)S(6)} %copy.12.size_ref, f32[8,512]{1,0:T(8,128)S(1)} %lane.1.lane_ref, s32[1,8,8]{2,1,0:T(8,128)S(1)} %copy-done.3, s32[1,8,8]{2,1,0:T(8,128)S(1)} %copy-done.4, s32[1,8,8]{2,1,0:T(8,128)S(1)} %copy-done.5, f32[1,8,8]{2,1,0:T(8,128)S(1)} %copy-done.6, ...), custom_call_target="tpu_custom_call" | custom-call | tf_op jit(solution)/shard_map/pick/pallas_call | solution.py:289
  2.6 3.5 %collective-permute-start = (bf16[1,72,128]{2,1,0:T(8,128)(2,1)S(1)}, bf16[1,72,128]{2,1,0:T(8,128)(2,1)S(1)}, u32[]{:S(2)}, u32[]{:S(2)}) collective-permute-start(bf16[1,72,128]{2,1,0:T(8,128)(2,1)S(1)} %bitcast.2), channel_id=1, source_target_pairs={{0,9},{1,8},{4,13},{5,12},{8,1},{9,0},{12,5},{13,4},{2,11},{3,10},... | collective-permute-start | bytes 55304 | tf_op jit(solution)/shard_map/ppermute | solution.py:304
  6.1 1.5 %collective-permute-done = bf16[1,72,128]{2,1,0:T(8,128)(2,1)S(1)} collective-permute-done((bf16[1,72,128]{2,1,0:T(8,128)(2,1)S(1)}, bf16[1,72,128]{2,1,0:T(8,128)(2,1)S(1)}, u32[]{:S(2)}, u32[]{:S(2)}) %collective-permute-start) | collective-permute-done | bytes 18464 | tf_op jit(solution)/shard_map/ppermute | solution.py:304
  7.6 1.9 %collective-permute-start.2 = (bf16[2,72,128]{2,1,0:T(8,128)(2,1)S(1)}, bf16[2,72,128]{2,1,0:T(8,128)(2,1)S(1)}, u32[]{:S(2)}, u32[]{:S(2)}) collective-permute-start(bf16[2,72,128]{2,1,0:T(8,128)(2,1)S(1)} %pad_maximum_fusion.refs_0_.first_pair), channel_id=1, source_target_pairs={{0,5},{1,4},{4,1},{5,0},{8,13},{9,12},{12,9},{13,8},{2,7},{3,6},{6... | collective-permute-start | bytes 110600 | tf_op jit(solution)/shard_map/ppermute | solution.py:304
  9.5 0.4 %collective-permute-start.1 = (bf16[2,72,128]{2,1,0:T(8,128)(2,1)S(1)}, bf16[2,72,128]{2,1,0:T(8,128)(2,1)S(1)}, u32[]{:S(2)}, u32[]{:S(2)}) collective-permute-start(bf16[2,72,128]{2,1,0:T(8,128)(2,1)S(1)} %pad_maximum_fusion.refs_0_.first_pair), channel_id=1, source_target_pairs={{0,1},{1,0},{4,5},{5,4},{8,9},{9,8},{12,13},{13,12},{2,3},{3,2},{6... | collective-permute-start | bytes 110600 | tf_op jit(solution)/shard_map/ppermute | solution.py:304
  9.9 1.2 %collective-permute-done.2.refs_0_.later_pair = bf16[2,72,128]{2,1,0:T(8,128)(2,1)S(1)} collective-permute-done((bf16[2,72,128]{2,1,0:T(8,128)(2,1)S(1)}, bf16[2,72,128]{2,1,0:T(8,128)(2,1)S(1)}, u32[]{:S(2)}, u32[]{:S(2)}) %collective-permute-start.2) | collective-permute-done | bytes 36896 | tf_op jit(solution)/shard_map/ppermute | solution.py:304
  11.1 0.5 %collective-permute-start.3 = (bf16[2,72,128]{2,1,0:T(8,128)(2,1)S(1)}, bf16[2,72,128]{2,1,0:T(8,128)(2,1)S(1)}, u32[]{:S(2)}, u32[]{:S(2)}) collective-permute-start(bf16[2,72,128]{2,1,0:T(8,128)(2,1)S(1)} %collective-permute-done.2.refs_0_.later_pair), channel_id=1, source_target_pairs={{0,1},{1,0},{4,5},{5,4},{8,9},{9,8},{12,13},{13,12},{2,3},{3,2},{6... | collective-permute-start | bytes 110600 | tf_op jit(solution)/shard_map/ppermute | solution.py:304
  11.6 0.0 copy-done
  11.6 0.3 %widen.3.later_wide = f32[2,64,1024]{2,1,0:T(8,128)S(1)} custom-call(bf16[2,72,128]{2,1,0:T(8,128)(2,1)S(1)} %collective-permute-done.2.refs_0_.later_pair, bf16[128,1024]{1,0:T(8,128)(2,1)S(1)} %copy-done), custom_call_target="tpu_custom_call" | custom-call | flops 33554432 | bytes 524288 | tf_op jit(solution)/shard_map/widen/pallas_call | solution.py:308
  11.9 0.0 collective-permute-done.1.refs_1_.first_other
  11.9 0.4 %widen.2.first_wide = f32[4,64,1024]{2,1,0:T(8,128)S(1)} custom-call(bf16[2,72,128]{2,1,0:T(8,128)(2,1)S(1)} %pad_maximum_fusion.refs_0_.first_pair, bf16[2,72,128]{2,1,0:T(8,128)(2,1)S(1)} %collective-permute-done.1.refs_1_.first_other, bf16[128,1024]{1,0:T(8,128)(2,1)S(1)} %copy-done), custom_call_target="tpu_custom_call" | custom-call | flops 67108864 | bytes 1048576 | tf_op jit(solution)/shard_map/widen/pallas_call | solution.py:308
  12.3 0.2 %collective-permute-done.3.later_other = bf16[2,72,128]{2,1,0:T(8,128)(2,1)S(1)} collective-permute-done((bf16[2,72,128]{2,1,0:T(8,128)(2,1)S(1)}, bf16[2,72,128]{2,1,0:T(8,128)(2,1)S(1)}, u32[]{:S(2)}, u32[]{:S(2)}) %collective-permute-start.3) | collective-permute-done | bytes 36896 | tf_op jit(solution)/shard_map/ppermute | solution.py:304
  12.5 1.5 %march.1 = (bf16[1,32,512]{2,1,0:T(8,128)(2,1)}, f32[8,32]{1,0:T(8,128)}) custom-call(bf16[2,72,128]{2,1,0:T(8,128)(2,1)S(1)} %pad_maximum_fusion.refs_0_.first_pair, bf16[2,72,128]{2,1,0:T(8,128)(2,1)S(1)} %collective-permute-done.1.refs_1_.first_other, bf16[2,72,128]{2,1,0:T(8,128)(2,1)S(1)} %collective-permute-done.2.refs_0_.later_pair, ...), custom_call_target="tpu_custom_call" | custom-call | tf_op jit(solution)/shard_map/march/pallas_call | solution.py:331
  (2 shorter events, 0.0 us)
Async XLA Ops:
  0.6 0.8 %copy-start.2 = (bf16[1,32,512]{2,1,0:T(8,128)(2,1)S(1)}, bf16[1,32,512]{2,1,0:T(8,128)(2,1)}, u32[]{:S(2)}) copy-start(bf16[1,32,512]{2,1,0:T(8,128)(2,1)} %cotangent_ref.1) | copy-start | bytes 98308
  0.6 1.1 %copy-start.1 = (bf16[1,512,512]{2,1,0:T(8,128)(2,1)S(1)}, bf16[1,512,512]{2,1,0:T(8,128)(2,1)}, u32[]{:S(2)}) copy-start(bf16[1,512,512]{2,1,0:T(8,128)(2,1)} %inverse_ref.1) | copy-start | bytes 1572868
  0.7 1.1 %copy-start.3 = (s32[1,8,8]{2,1,0:T(8,128)S(1)}, s32[1,8,8]{2,1,0:T(8,128)}, u32[]{:S(2)}) copy-start(s32[1,8,8]{2,1,0:T(8,128)} %into_ref.1) | copy-start | bytes 772
  0.7 1.1 %copy-start.4 = (s32[1,8,8]{2,1,0:T(8,128)S(1)}, s32[1,8,8]{2,1,0:T(8,128)}, u32[]{:S(2)}) copy-start(s32[1,8,8]{2,1,0:T(8,128)} %from_ref.1) | copy-start | bytes 772
  0.7 1.0 %copy-start.5 = (s32[1,8,8]{2,1,0:T(8,128)S(1)}, s32[1,8,8]{2,1,0:T(8,128)}, u32[]{:S(2)}) copy-start(s32[1,8,8]{2,1,0:T(8,128)} %offset_ref.1) | copy-start | bytes 772
  0.7 1.0 %copy-start.6 = (f32[1,8,8]{2,1,0:T(8,128)S(1)}, f32[1,8,8]{2,1,0:T(8,128)}, u32[]{:S(2)}) copy-start(f32[1,8,8]{2,1,0:T(8,128)} %weight_ref.1) | copy-start | bytes 772
  0.7 1.0 %copy-start.7 = (f32[1,8,8]{2,1,0:T(8,128)S(1)}, f32[1,8,8]{2,1,0:T(8,128)}, u32[]{:S(2)}) copy-start(f32[1,8,8]{2,1,0:T(8,128)} %admit_ref.1) | copy-start | bytes 772
  1.4 0.7 %copy-start.8 = (s32[32]{0:T(128)S(1)}, s32[32]{0:T(128)}, u32[]{:S(2)}) copy-start(s32[32]{0:T(128)} %param.18) | copy-start | bytes 388
  2.1 9.5 %copy-start = (bf16[128,1024]{1,0:T(8,128)(2,1)S(1)}, bf16[128,1024]{1,0:T(8,128)(2,1)}, u32[]{:S(2)}) copy-start(bf16[128,1024]{1,0:T(8,128)(2,1)} %constant.2.clone.refs_2_.refs_1_.spread_ref) | copy-start | bytes 786436
  2.6 5.0 %collective-permute-start = (bf16[1,72,128]{2,1,0:T(8,128)(2,1)S(1)}, bf16[1,72,128]{2,1,0:T(8,128)(2,1)S(1)}, u32[]{:S(2)}, u32[]{:S(2)}) collective-permute-start(bf16[1,72,128]{2,1,0:T(8,128)(2,1)S(1)} %bitcast.2), channel_id=1, source_target_pairs={{0,9},{1,8},{4,13},{5,12},{8,1},{9,0},{12,5},{13,4},{2,11},{3,10},... | collective-permute-start | bytes 55304 | tf_op jit(solution)/shard_map/ppermute | solution.py:304
  7.6 3.5 %collective-permute-start.2 = (bf16[2,72,128]{2,1,0:T(8,128)(2,1)S(1)}, bf16[2,72,128]{2,1,0:T(8,128)(2,1)S(1)}, u32[]{:S(2)}, u32[]{:S(2)}) collective-permute-start(bf16[2,72,128]{2,1,0:T(8,128)(2,1)S(1)} %pad_maximum_fusion.refs_0_.first_pair), channel_id=1, source_target_pairs={{0,5},{1,4},{4,1},{5,0},{8,13},{9,12},{12,9},{13,8},{2,7},{3,6},{6... | collective-permute-start | bytes 110600 | tf_op jit(solution)/shard_map/ppermute | solution.py:304
  9.5 2.4 %collective-permute-start.1 = (bf16[2,72,128]{2,1,0:T(8,128)(2,1)S(1)}, bf16[2,72,128]{2,1,0:T(8,128)(2,1)S(1)}, u32[]{:S(2)}, u32[]{:S(2)}) collective-permute-start(bf16[2,72,128]{2,1,0:T(8,128)(2,1)S(1)} %pad_maximum_fusion.refs_0_.first_pair), channel_id=1, source_target_pairs={{0,1},{1,0},{4,5},{5,4},{8,9},{9,8},{12,13},{13,12},{2,3},{3,2},{6... | collective-permute-start | bytes 110600 | tf_op jit(solution)/shard_map/ppermute | solution.py:304
  11.1 1.4 %collective-permute-start.3 = (bf16[2,72,128]{2,1,0:T(8,128)(2,1)S(1)}, bf16[2,72,128]{2,1,0:T(8,128)(2,1)S(1)}, u32[]{:S(2)}, u32[]{:S(2)}) collective-permute-start(bf16[2,72,128]{2,1,0:T(8,128)(2,1)S(1)} %collective-permute-done.2.refs_0_.later_pair), channel_id=1, source_target_pairs={{0,1},{1,0},{4,5},{5,4},{8,9},{9,8},{12,13},{13,12},{2,3},{3,2},{6... | collective-permute-start | bytes 110600 | tf_op jit(solution)/shard_map/ppermute | solution.py:304

commit v4 on v3

--- a/solution.py
+++ b/solution.py
@@ -43,20 +43,8 @@
     return spread
 
 
-def exchange_masks(owners):
-    masks = []
-    reach = owners // 2
-    while reach > 1:
-        masks.append(reach + 1)
-        reach //= 2
-    return masks + [1]
-
-
-def held_order(owners):
-    far, near, core = exchange_masks(owners)
-    first = [0, far]
-    later = [near, near ^ far]
-    return first + [x ^ core for x in first] + later + [x ^ core for x in later]
+SOURCES = ((1, 0, 3, 2), (2, 3, 1, 0), (3, 2, 0, 1))
+HELD = (0, 3, 5, 7, 1, 2, 4, 6)
 
 
 def column_of(ref, place):
@@ -93,18 +81,22 @@
     place = owner_here()
     into = column_of(into_ref, place)
     source = column_of(from_ref, place)
+    recv_hot = jnp.where((source == lane_f) & alive, 1.0, 0.0).astype(jnp.bfloat16)
+    send_hot = jnp.where(into == lane_f, 1.0, 0.0).astype(jnp.bfloat16)
+    driving = jnp.where(alive[:columns], cotangent_ref[0].astype(jnp.float32), 0.0).astype(jnp.bfloat16)
+    stack = jnp.concatenate([recv_hot, driving], axis=0)
+    picked = dot(stack, inverse_ref[0])
+    lane = lax.broadcasted_iota(jnp.int32, picked.shape, 1)
+    picked = jnp.where(lane < live, picked, 0.0).astype(jnp.bfloat16)
+    bus = (bus_ref[...] - place * nodes).astype(jnp.float32)
+    eye = lax.broadcasted_iota(jnp.int32, (columns, columns), 0) == lax.broadcasted_iota(
+        jnp.int32, (columns, columns), 1
+    )
+    bus = jnp.sum(jnp.where(eye, jnp.broadcast_to(bus, (columns, columns)), 0.0), axis=1, keepdims=True)
+    fault_hot = jnp.where(bus == lane_f[:columns], 1.0, 0.0).astype(jnp.bfloat16)
     delay = column_of(offset_ref, place)
     weight = column_of(weight_ref, place)
     admit = column_of(admit_ref, place)
-    recv_hot = jnp.where((source == lane_f) & alive, 1.0, 0.0).astype(jnp.bfloat16)
-    send_hot = jnp.where(into == lane_f, 1.0, 0.0).astype(jnp.bfloat16)
-    driving = jnp.where(alive[:columns], cotangent_ref[0].astype(jnp.float32), 0.0).astype(jnp.bfloat16)
-    bus = (bus_ref[...] - place * nodes).astype(jnp.float32)
-    eye = lax.broadcasted_iota(jnp.int32, (columns, columns), 0) == lax.broadcasted_iota(
-        jnp.int32, (columns, columns), 1
-    )
-    bus = jnp.sum(jnp.where(eye, jnp.broadcast_to(bus, (columns, columns)), 0.0), axis=1, keepdims=True)
-    fault_hot = jnp.where(bus == lane_f[:columns], 1.0, 0.0).astype(jnp.bfloat16)
     conduct = jnp.where(source >= 0, admit, 0.0)
     near, far = conduct * weight, conduct * (1.0 - weight)
     factors = [
@@ -131,10 +123,6 @@
         lax.broadcasted_iota(jnp.int32, (8, LANES), 0) == lax.broadcasted_iota(jnp.int32, (8, LANES), 1), 1.0, 0.0
     ).astype(jnp.bfloat16)
     table = dot(eye, jnp.concatenate([upper, lower], axis=0).astype(jnp.bfloat16), NT)
-    stack = jnp.concatenate([recv_hot, driving], axis=0)
-    picked = dot(stack, inverse_ref[0])
-    lane = lax.broadcasted_iota(jnp.int32, picked.shape, 1)
-    picked = jnp.where(lane < live, picked, 0.0).astype(jnp.bfloat16)
     rows = picked[:slots]
     rows_ref[...] = rows
     blank = jnp.zeros((columns, nodes), jnp.bfloat16)
@@ -162,9 +150,8 @@
     return [jnp.where(group == index, turned, 0.0).astype(jnp.bfloat16) for index in range(len(messages))]
 
 
-def widen_kernel(*refs):
-    *held_refs, spread_ref, wide_ref = refs
-    messages = [ref[p] for ref in held_refs for p in range(ref.shape[0])]
+def widen_kernel(near_ref, spread_ref, wide_ref):
+    messages = [near_ref[p] for p in range(near_ref.shape[0])]
     count = LANES * len(VARIANTS)
     for index, piece in enumerate(turned_pieces(messages)):
         wide_ref[index, :, :count] = dot(piece, spread_ref[:, :count])
@@ -172,16 +159,15 @@
 
 
 def march_kernel(
-    first_pair, first_other, later_pair, later_other, first_wide, later_wide, spread_ref, rows_ref,
-    first_hbm, fault_hbm, first_ref, fault_ref, semaphores,
+    near_ref, far_ref, wide_ref, spread_ref, rows_ref, first_hbm, fault_hbm, first_ref, fault_ref, semaphores
 ):
-    held = (first_pair, first_other, later_pair, later_other)
+    held = (near_ref, far_ref)
     owners = sum(ref.shape[0] for ref in held)
     slots = rows_ref.shape[0]
     columns = first_ref.shape[1]
     depth = slots // owners
     count = len(VARIANTS)
-    order = held_order(owners)
+    order = HELD
     spot = {apart: index for index, apart in enumerate(order)}
 
     def exchange(parts):
@@ -197,12 +183,12 @@
 
     blocks = [ref[p] for ref in held for p in range(ref.shape[0])]
     system = [block[:slots, :slots] for block in blocks]
-    fresh = blocks[-later_other.shape[0] :]
+    fresh = blocks[-far_ref.shape[0] :]
     pieces = turned_pieces(fresh)
 
     def spread_of(index, sources):
         pair = slice(LANES * index, LANES * (index + 2))
-        known = [ref[p, :, pair] for ref in (first_wide, later_wide) for p in range(ref.shape[0])]
+        known = [wide_ref[p, :, pair] for p in range(wide_ref.shape[0])]
         both = known + [dot(source, spread_ref[:, pair]) for source in sources]
         return [lanes(part, 0) for part in both], [lanes(part, 1) for part in both]
 
@@ -300,30 +286,27 @@
     spread = jnp.asarray(spread_matrix(columns, 8), jnp.bfloat16)
     width = spread.shape[1]
 
-    def swap(held, mask):
-        return lax.ppermute(held, OWNER_AXES, [(i, i ^ mask) for i in range(owners)])
-
-    def widen(*held):
-        count = sum(part.shape[0] for part in held)
-        return pl.pallas_call(
-            widen_kernel,
-            out_shape=jax.ShapeDtypeStruct((count, slots, width), jnp.float32),
-            in_specs=[vmem] * (len(held) + 1),
-            out_specs=vmem,
-            compiler_params=pltpu.CompilerParams(vmem_limit_bytes=VMEM_LIMIT),
-            cost_estimate=pl.CostEstimate(
-                flops=2 * count * slots * LANES * width, bytes_accessed=4 * count * slots * width, transcendentals=0
-            ),
-            name="widen",
-        )(*held, spread)
-
-    far, near, core = exchange_masks(owners)
-    first = jnp.concatenate([message[None], swap(message[None], far)], axis=0)
-    later = swap(first, near)
-    first_other = swap(first, core)
-    first_wide = widen(first, first_other)
-    later_other = swap(later, core)
-    later_wide = widen(later)
+
+    def send(held, sources):
+        pairs = [(2 * source + core, 2 * z + 1 - core) for z, source in enumerate(sources) for core in range(2)]
+        return lax.ppermute(held, OWNER_AXES, pairs)
+
+    own = message[None]
+    beside, second, third = (send(own, sources) for sources in SOURCES)
+    low = lax.axis_index(OWNER_AXES[0]) < 2
+    near = jnp.concatenate([own, beside, jnp.where(low, second, third), jnp.where(low, third, second)], axis=0)
+    far = send(near, range(len(SOURCES) + 1))
+    wide = pl.pallas_call(
+        widen_kernel,
+        out_shape=jax.ShapeDtypeStruct((near.shape[0], slots, width), jnp.float32),
+        in_specs=[vmem] * 2,
+        out_specs=vmem,
+        compiler_params=pltpu.CompilerParams(vmem_limit_bytes=VMEM_LIMIT),
+        cost_estimate=pl.CostEstimate(
+            flops=2 * near.shape[0] * slots * LANES * width, bytes_accessed=4 * near.shape[0] * slots * width, transcendentals=0
+        ),
+        name="widen",
+    )(near, spread)
     outputs = (
         jax.ShapeDtypeStruct((1, columns, nodes), jnp.bfloat16),
         jax.ShapeDtypeStruct((STEPS, columns), jnp.float32),
@@ -331,7 +314,7 @@
     return pl.pallas_call(
         march_kernel,
         out_shape=outputs,
-        in_specs=[vmem] * 8,
+        in_specs=[vmem] * 5,
         out_specs=(hbm, hbm),
         scratch_shapes=[
             *(pltpu.VMEM(output.shape, output.dtype) for output in outputs),
@@ -339,7 +322,7 @@
         ],
         compiler_params=pltpu.CompilerParams(vmem_limit_bytes=VMEM_LIMIT),
         name="march",
-    )(first, first_other, later, later_other, first_wide, later_wide, spread, rows)
+    )(near, far, wide, spread, rows)
 
 
 def exchanged_plan(
@@ -422,7 +405,8 @@
         blocks == 1
         and columns * 4 == LANES
         and depth == 8
-        and owners == 8
+        and lax.axis_size(OWNER_AXES[0]) == 4
+        and lax.axis_size(OWNER_AXES[1]) == 2
         and slots + 2 * columns == LANES
         and nodes % LANES == 0
     )

time: 14.2 us -> 13.8 us (0.972)
  Pallas kernels: 2.64 us -> 2.4 us
  starting transfers between devices: 6.3 us -> 6.11 us
    pallas_call x3 -> x2, Pallas kernels: 2.14 us -> 1.9 us  [the longest x1 1.54 us: gathered_plan(): pl.pallas_call(march_kernel, out_shape=outputs, in_specs=[vmem] * 5, out_...]
    ppermute x4, starting transfers between devices: 6.3 us -> 6.11 us  [send(): return lax.ppermute(held, OWNER_AXES, pairs)]
  transfers between devices with their start and end apart: 4 -> 4, of which waited for: 3 -> 4; matrix products, arithmetic and copies ran while one was open for 0% -> 0% of each run, Pallas kernels for 5% -> 3%
where the time goes in v4:
time: 13.8 us; the launch traced here: 13.6 us
  starting transfers between devices  6.11 us (44%)
  waiting for transfers between devices  2.96 us (21%)
  Pallas kernels  2.4 us (17%)
  between operations  1.43 us (10%)
  local copies, waits for them, and re-layouts  0.69 us (5%)
    ppermute x4, starting transfers between devices, send(): return lax.ppermute(held, OWNER_AXES, pairs)  6.11 us
    ppermute x4, waiting for transfers between devices, send(): return lax.ppermute(held, OWNER_AXES, pairs)  2.96 us
    pallas_call x1, Pallas kernels, gathered_plan(): pl.pallas_call(march_kernel, out_shape=outputs, in_specs=[vmem] * 5, out_...  1.54 us
    unnamed x18, local copies, waits for them, and re-layouts  0.69 us
    pallas_call x1, Pallas kernels, gathered_plan(): pl.pallas_call(pick_kernel, out_shape=(jax.ShapeDtypeStruct((height, LANE...  0.49 us
    pallas_call x1, Pallas kernels, gathered_plan(): pl.pallas_call(widen_kernel, out_shape=jax.ShapeDtypeStruct((near.shape[0...  0.36 us
  transfers between devices with their start and end apart: 4, of which 4 were waited for; matrix products, arithmetic and copies ran while one was open for 0% of the time, Pallas kernels for 3%

profile of v4, /device:TPU:0, one launch (start us, length us, event | category | flops | bytes accessed | tf_op | source)
XLA Modules:
  0.0 13.6 jit_solution(4694965861968935825)
XLA Ops:
  0.6 0.0 copy-start.2
  0.6 0.0 copy-start.1
  0.7 0.0 copy-start.3
  0.7 0.0 copy-start.4
  0.7 0.0 copy-start.5
  0.7 0.0 copy-start.6
  0.7 0.0 copy-start.7
  1.4 0.0 copy-start.8
  1.4 0.0 copy-done.2
  1.4 0.3 %copy-done.1 = bf16[1,512,512]{2,1,0:T(8,128)(2,1)S(1)} copy-done((bf16[1,512,512]{2,1,0:T(8,128)(2,1)S(1)}, bf16[1,512,512]{2,1,0:T(8,128)(2,1)}, u32[]{:S(2)}) %copy-start.1) | copy-done | bytes 524312
  1.7 0.0 copy-done.3
  1.7 0.0 copy-done.4
  1.7 0.0 copy-done.5
  1.7 0.0 copy-done.6
  1.7 0.0 copy-done.7
  1.7 0.4 %copy-done.8 = s32[32]{0:T(128)S(1)} copy-done((s32[32]{0:T(128)S(1)}, s32[32]{0:T(128)}, u32[]{:S(2)}) %copy-start.8) | copy-done | bytes 152
  2.1 0.0 copy-start
  2.1 0.5 %pick.1 = (bf16[72,128]{1,0:T(8,128)(2,1)S(1)}, bf16[64,512]{1,0:T(8,128)(2,1)S(1)}) custom-call(s32[1]{0:T(128)S(6)} %copy.12.size_ref, f32[8,512]{1,0:T(8,128)S(1)} %lane.1.lane_ref, s32[1,8,8]{2,1,0:T(8,128)S(1)} %copy-done.3, s32[1,8,8]{2,1,0:T(8,128)S(1)} %copy-done.4, s32[1,8,8]{2,1,0:T(8,128)S(1)} %copy-done.5, f32[1,8,8]{2,1,0:T(8,128)S(1)} %copy-done.6, ...), custom_call_target="tpu_custom_call" | custom-call | tf_op jit(solution)/shard_map/pick/pallas_call | solution.py:275
  2.6 3.5 %collective-permute-start.2 = (bf16[1,72,128]{2,1,0:T(8,128)(2,1)S(1)}, bf16[1,72,128]{2,1,0:T(8,128)(2,1)S(1)}, u32[]{:S(2)}, u32[]{:S(2)}) collective-permute-start(bf16[1,72,128]{2,1,0:T(8,128)(2,1)S(1)} %bitcast.2), channel_id=1, source_target_pairs={{12,1},{13,0},{8,5},{9,4},{0,9},{1,8},{4,13},{5,12},{14,3},{15,2},... | collective-permute-start | bytes 55304 | tf_op jit(solution)/shard_map/ppermute | solution.py:292
  6.1 1.1 %collective-permute-start.1 = (bf16[1,72,128]{2,1,0:T(8,128)(2,1)S(1)}, bf16[1,72,128]{2,1,0:T(8,128)(2,1)S(1)}, u32[]{:S(2)}, u32[]{:S(2)}) collective-permute-start(bf16[1,72,128]{2,1,0:T(8,128)(2,1)S(1)} %bitcast.3), channel_id=1, source_target_pairs={{8,1},{9,0},{12,5},{13,4},{4,9},{5,8},{0,13},{1,12},{10,3},{11,2},... | collective-permute-start | bytes 55304 | tf_op jit(solution)/shard_map/ppermute | solution.py:292
  7.2 0.8 %collective-permute-start = (bf16[1,72,128]{2,1,0:T(8,128)(2,1)S(1)}, bf16[1,72,128]{2,1,0:T(8,128)(2,1)S(1)}, u32[]{:S(2)}, u32[]{:S(2)}) collective-permute-start(bf16[1,72,128]{2,1,0:T(8,128)(2,1)S(1)} %bitcast.4), channel_id=1, source_target_pairs={{4,1},{5,0},{0,5},{1,4},{12,9},{13,8},{8,13},{9,12},{6,3},{7,2},{2... | collective-permute-start | bytes 55304 | tf_op jit(solution)/shard_map/ppermute | solution.py:292
  8.0 0.7 %collective-permute-done.2 = bf16[1,72,128]{2,1,0:T(8,128)(2,1)S(1)} collective-permute-done((bf16[1,72,128]{2,1,0:T(8,128)(2,1)S(1)}, bf16[1,72,128]{2,1,0:T(8,128)(2,1)S(1)}, u32[]{:S(2)}, u32[]{:S(2)}) %collective-permute-start.2) | collective-permute-done | bytes 18464 | tf_op jit(solution)/shard_map/ppermute | solution.py:292
  8.7 1.5 %collective-permute-done.1 = bf16[1,72,128]{2,1,0:T(8,128)(2,1)S(1)} collective-permute-done((bf16[1,72,128]{2,1,0:T(8,128)(2,1)S(1)}, bf16[1,72,128]{2,1,0:T(8,128)(2,1)S(1)}, u32[]{:S(2)}, u32[]{:S(2)}) %collective-permute-start.1) | collective-permute-done | bytes 18464 | tf_op jit(solution)/shard_map/ppermute | solution.py:292
  10.2 0.2 %collective-permute-done = bf16[1,72,128]{2,1,0:T(8,128)(2,1)S(1)} collective-permute-done((bf16[1,72,128]{2,1,0:T(8,128)(2,1)S(1)}, bf16[1,72,128]{2,1,0:T(8,128)(2,1)S(1)}, u32[]{:S(2)}, u32[]{:S(2)}) %collective-permute-start) | collective-permute-done | bytes 18464 | tf_op jit(solution)/shard_map/ppermute | solution.py:292
  10.4 0.8 %collective-permute-start.3 = (bf16[4,72,128]{2,1,0:T(8,128)(2,1)S(1)}, bf16[4,72,128]{2,1,0:T(8,128)(2,1)S(1)}, u32[]{:S(2)}, u32[]{:S(2)}) collective-permute-start(bf16[4,72,128]{2,1,0:T(8,128)(2,1)S(1)} %pad_maximum_fusion.near_ref), channel_id=1, source_target_pairs={{0,1},{1,0},{4,5},{5,4},{8,9},{9,8},{12,13},{13,12},{2,3},{3,2},{6... | collective-permute-start | bytes 221192 | tf_op jit(solution)/shard_map/ppermute | solution.py:292
  11.2 0.0 copy-done
  11.2 0.4 %widen.1.wide_ref = f32[4,64,1024]{2,1,0:T(8,128)S(1)} custom-call(bf16[4,72,128]{2,1,0:T(8,128)(2,1)S(1)} %pad_maximum_fusion.near_ref, bf16[128,1024]{1,0:T(8,128)(2,1)S(1)} %copy-done), custom_call_target="tpu_custom_call" | custom-call | flops 67108864 | bytes 1048576 | tf_op jit(solution)/shard_map/widen/pallas_call | solution.py:299
  11.5 0.5 %collective-permute-done.3.far_ref = bf16[4,72,128]{2,1,0:T(8,128)(2,1)S(1)} collective-permute-done((bf16[4,72,128]{2,1,0:T(8,128)(2,1)S(1)}, bf16[4,72,128]{2,1,0:T(8,128)(2,1)S(1)}, u32[]{:S(2)}, u32[]{:S(2)}) %collective-permute-start.3) | collective-permute-done | bytes 73760 | tf_op jit(solution)/shard_map/ppermute | solution.py:292
  12.1 1.5 %march.1 = (bf16[1,32,512]{2,1,0:T(8,128)(2,1)}, f32[8,32]{1,0:T(8,128)}) custom-call(bf16[4,72,128]{2,1,0:T(8,128)(2,1)S(1)} %pad_maximum_fusion.near_ref, bf16[4,72,128]{2,1,0:T(8,128)(2,1)S(1)} %collective-permute-done.3.far_ref, f32[4,64,1024]{2,1,0:T(8,128)S(1)} %widen.1.wide_ref, bf16[128,1024]{1,0:T(8,128)(2,1)S(1)} %copy-done, ...), custom_call_target="tpu_custom_call" | custom-call | tf_op jit(solution)/shard_map/march/pallas_call | solution.py:314
  (3 shorter events, 0.0 us)
Async XLA Ops:
  0.6 0.8 %copy-start.2 = (bf16[1,32,512]{2,1,0:T(8,128)(2,1)S(1)}, bf16[1,32,512]{2,1,0:T(8,128)(2,1)}, u32[]{:S(2)}) copy-start(bf16[1,32,512]{2,1,0:T(8,128)(2,1)} %cotangent_ref.1) | copy-start | bytes 98308
  0.6 1.1 %copy-start.1 = (bf16[1,512,512]{2,1,0:T(8,128)(2,1)S(1)}, bf16[1,512,512]{2,1,0:T(8,128)(2,1)}, u32[]{:S(2)}) copy-start(bf16[1,512,512]{2,1,0:T(8,128)(2,1)} %inverse_ref.1) | copy-start | bytes 1572868
  0.7 1.1 %copy-start.3 = (s32[1,8,8]{2,1,0:T(8,128)S(1)}, s32[1,8,8]{2,1,0:T(8,128)}, u32[]{:S(2)}) copy-start(s32[1,8,8]{2,1,0:T(8,128)} %into_ref.1) | copy-start | bytes 772
  0.7 1.1 %copy-start.4 = (s32[1,8,8]{2,1,0:T(8,128)S(1)}, s32[1,8,8]{2,1,0:T(8,128)}, u32[]{:S(2)}) copy-start(s32[1,8,8]{2,1,0:T(8,128)} %from_ref.1) | copy-start | bytes 772
  0.7 1.0 %copy-start.5 = (s32[1,8,8]{2,1,0:T(8,128)S(1)}, s32[1,8,8]{2,1,0:T(8,128)}, u32[]{:S(2)}) copy-start(s32[1,8,8]{2,1,0:T(8,128)} %offset_ref.1) | copy-start | bytes 772
  0.7 1.0 %copy-start.6 = (f32[1,8,8]{2,1,0:T(8,128)S(1)}, f32[1,8,8]{2,1,0:T(8,128)}, u32[]{:S(2)}) copy-start(f32[1,8,8]{2,1,0:T(8,128)} %weight_ref.1) | copy-start | bytes 772
  0.7 1.0 %copy-start.7 = (f32[1,8,8]{2,1,0:T(8,128)S(1)}, f32[1,8,8]{2,1,0:T(8,128)}, u32[]{:S(2)}) copy-start(f32[1,8,8]{2,1,0:T(8,128)} %admit_ref.1) | copy-start | bytes 772
  1.4 0.7 %copy-start.8 = (s32[32]{0:T(128)S(1)}, s32[32]{0:T(128)}, u32[]{:S(2)}) copy-start(s32[32]{0:T(128)} %param.18) | copy-start | bytes 388
  2.1 9.1 %copy-start = (bf16[128,1024]{1,0:T(8,128)(2,1)S(1)}, bf16[128,1024]{1,0:T(8,128)(2,1)}, u32[]{:S(2)}) copy-start(bf16[128,1024]{1,0:T(8,128)(2,1)} %constant.9.clone.spread_ref) | copy-start | bytes 786436
  2.6 6.1 %collective-permute-start.2 = (bf16[1,72,128]{2,1,0:T(8,128)(2,1)S(1)}, bf16[1,72,128]{2,1,0:T(8,128)(2,1)S(1)}, u32[]{:S(2)}, u32[]{:S(2)}) collective-permute-start(bf16[1,72,128]{2,1,0:T(8,128)(2,1)S(1)} %bitcast.2), channel_id=1, source_target_pairs={{12,1},{13,0},{8,5},{9,4},{0,9},{1,8},{4,13},{5,12},{14,3},{15,2},... | collective-permute-start | bytes 55304 | tf_op jit(solution)/shard_map/ppermute | solution.py:292
  6.1 4.1 %collective-permute-start.1 = (bf16[1,72,128]{2,1,0:T(8,128)(2,1)S(1)}, bf16[1,72,128]{2,1,0:T(8,128)(2,1)S(1)}, u32[]{:S(2)}, u32[]{:S(2)}) collective-permute-start(bf16[1,72,128]{2,1,0:T(8,128)(2,1)S(1)} %bitcast.3), channel_id=1, source_target_pairs={{8,1},{9,0},{12,5},{13,4},{4,9},{5,8},{0,13},{1,12},{10,3},{11,2},... | collective-permute-start | bytes 55304 | tf_op jit(solution)/shard_map/ppermute | solution.py:292
  7.2 3.2 %collective-permute-start = (bf16[1,72,128]{2,1,0:T(8,128)(2,1)S(1)}, bf16[1,72,128]{2,1,0:T(8,128)(2,1)S(1)}, u32[]{:S(2)}, u32[]{:S(2)}) collective-permute-start(bf16[1,72,128]{2,1,0:T(8,128)(2,1)S(1)} %bitcast.4), channel_id=1, source_target_pairs={{4,1},{5,0},{0,5},{1,4},{12,9},{13,8},{8,13},{9,12},{6,3},{7,2},{2... | collective-permute-start | bytes 55304 | tf_op jit(solution)/shard_map/ppermute | solution.py:292
  10.4 1.7 %collective-permute-start.3 = (bf16[4,72,128]{2,1,0:T(8,128)(2,1)S(1)}, bf16[4,72,128]{2,1,0:T(8,128)(2,1)S(1)}, u32[]{:S(2)}, u32[]{:S(2)}) collective-permute-start(bf16[4,72,128]{2,1,0:T(8,128)(2,1)S(1)} %pad_maximum_fusion.near_ref), channel_id=1, source_target_pairs={{0,1},{1,0},{4,5},{5,4},{8,9},{9,8},{12,13},{13,12},{2,3},{3,2},{6... | collective-permute-start | bytes 221192 | tf_op jit(solution)/shard_map/ppermute | solution.py:292

commit v5 on v4

--- a/solution.py
+++ b/solution.py
@@ -68,7 +68,7 @@
 
 
 def pick_kernel(
-    size_ref, lane_ref, into_ref, from_ref, offset_ref, weight_ref, admit_ref, bus_ref, inverse_ref, cotangent_ref,
+    packed_ref, lane_ref, into_ref, from_ref, offset_ref, weight_ref, admit_ref, inverse_ref, cotangent_ref,
     message_ref, rows_ref,
 ):
     nodes = inverse_ref.shape[1]
@@ -76,7 +76,7 @@
     slots = peers * depth
     columns = cotangent_ref.shape[1]
     lane_f = jnp.broadcast_to(lane_ref[:1], (slots, nodes))
-    live = size_ref[0]
+    live = packed_ref[:, :1]
     alive = lane_f < live.astype(jnp.float32)
     place = owner_here()
     into = column_of(into_ref, place)
@@ -88,11 +88,12 @@
     picked = dot(stack, inverse_ref[0])
     lane = lax.broadcasted_iota(jnp.int32, picked.shape, 1)
     picked = jnp.where(lane < live, picked, 0.0).astype(jnp.bfloat16)
-    bus = (bus_ref[...] - place * nodes).astype(jnp.float32)
-    eye = lax.broadcasted_iota(jnp.int32, (columns, columns), 0) == lax.broadcasted_iota(
-        jnp.int32, (columns, columns), 1
-    )
-    bus = jnp.sum(jnp.where(eye, jnp.broadcast_to(bus, (columns, columns)), 0.0), axis=1, keepdims=True)
+    width = columns + 1
+    bus = (packed_ref[...] - place * nodes).astype(jnp.float32)
+    eye = lax.broadcasted_iota(jnp.int32, (columns, width), 0) + 1 == lax.broadcasted_iota(
+        jnp.int32, (columns, width), 1
+    )
+    bus = jnp.sum(jnp.where(eye, jnp.broadcast_to(bus, (columns, width)), 0.0), axis=1, keepdims=True)
     fault_hot = jnp.where(bus == lane_f[:columns], 1.0, 0.0).astype(jnp.bfloat16)
     delay = column_of(offset_ref, place)
     weight = column_of(weight_ref, place)
@@ -259,7 +260,6 @@
     height = slots + 8
     vmem = pl.BlockSpec(memory_space=pltpu.VMEM)
     hbm = pl.BlockSpec(memory_space=pltpu.HBM)
-    smem = pl.BlockSpec(memory_space=pltpu.SMEM)
     lane = pl.pallas_call(
         lane_kernel,
         out_shape=jax.ShapeDtypeStruct((8, nodes), jnp.float32),
@@ -268,17 +268,15 @@
         cost_estimate=pl.CostEstimate(flops=HINT_FLOPS, bytes_accessed=HINT_BYTES, transcendentals=0),
         name="lane",
     )()
-    lane, sizes = lax.optimization_barrier((lane, subnet_sizes))
-    arrays = (
-        sizes, lane, slot_into, slot_from, offsets, weights, admittance, fault_bus[None], inverses, cotangent,
-    )
+    packed = jnp.concatenate([subnet_sizes, fault_bus])[None]
+    arrays = (packed, lane, slot_into, slot_from, offsets, weights, admittance, inverses, cotangent)
     message, rows = pl.pallas_call(
         pick_kernel,
         out_shape=(
             jax.ShapeDtypeStruct((height, LANES), jnp.bfloat16),
             jax.ShapeDtypeStruct((slots, nodes), jnp.bfloat16),
         ),
-        in_specs=[smem] + [vmem] * (len(arrays) - 1),
+        in_specs=[vmem] * len(arrays),
         out_specs=(vmem, vmem),
         compiler_params=pltpu.CompilerParams(vmem_limit_bytes=VMEM_LIMIT),
         name="pick",

time: 13.8 us -> 13.4 us (0.971)
  local copies, waits for them, and re-layouts: 0.69 us -> 0.25 us
    unnamed x18, local copies, waits for them, and re-layouts: 0.69 us -> 0.25 us
where the time goes in v5:
time: 13.4 us; the launch traced here: 13.3 us
  starting transfers between devices  6.11 us (46%)
  waiting for transfers between devices  2.95 us (22%)
  Pallas kernels  2.4 us (18%)
  between operations  1.45 us (11%)
  local copies, waits for them, and re-layouts  0.25 us (2%)
    ppermute x4, starting transfers between devices, send(): return lax.ppermute(held, OWNER_AXES, pairs)  6.11 us
    ppermute x4, waiting for transfers between devices, send(): return lax.ppermute(held, OWNER_AXES, pairs)  2.95 us
    pallas_call x1, Pallas kernels, gathered_plan(): pl.pallas_call(march_kernel, out_shape=outputs, in_specs=[vmem] * 5, out_...  1.54 us
    pallas_call x1, Pallas kernels, gathered_plan(): pl.pallas_call(pick_kernel, out_shape=(jax.ShapeDtypeStruct((height, LANE...  0.49 us
    pallas_call x1, Pallas kernels, gathered_plan(): pl.pallas_call(widen_kernel, out_shape=jax.ShapeDtypeStruct((near.shape[0...  0.36 us
  transfers between devices with their start and end apart: 4, of which 4 were waited for; matrix products, arithmetic and copies ran while one was open for 0% of the time, Pallas kernels for 3%

profile of v5, /device:TPU:0, one launch (start us, length us, event | category | flops | bytes accessed | tf_op | source)
XLA Modules:
  0.0 13.3 jit_solution(5751770684133698383)
XLA Ops:
  0.6 0.0 copy-start.2
  0.6 0.0 copy-start.1
  0.7 0.0 copy-start.3
  0.7 0.0 copy-start.4
  0.7 0.0 copy-start.5
  0.7 0.0 copy-start.6
  0.7 0.0 copy-start.7
  0.7 0.0 copy-start.8
  1.4 0.0 copy-done.8
  1.4 0.1 add_bitcast_fusion.packed_ref
  1.5 0.0 copy-done.2
  1.5 0.2 %copy-done.1 = bf16[1,512,512]{2,1,0:T(8,128)(2,1)S(1)} copy-done((bf16[1,512,512]{2,1,0:T(8,128)(2,1)S(1)}, bf16[1,512,512]{2,1,0:T(8,128)(2,1)}, u32[]{:S(2)}) %copy-start.1) | copy-done | bytes 524312
  1.7 0.0 copy-done.3
  1.7 0.0 copy-done.4
  1.7 0.0 copy-done.5
  1.7 0.0 copy-done.6
  1.7 0.0 copy-done.7
  1.7 0.0 copy-start
  1.8 0.5 %pick.1 = (bf16[72,128]{1,0:T(8,128)(2,1)S(1)}, bf16[64,512]{1,0:T(8,128)(2,1)S(1)}) custom-call(s32[1,33]{1,0:T(1,128)S(1)} %add_bitcast_fusion.packed_ref, f32[8,512]{1,0:T(8,128)S(1)} %lane.1.lane_ref, s32[1,8,8]{2,1,0:T(8,128)S(1)} %copy-done.3, s32[1,8,8]{2,1,0:T(8,128)S(1)} %copy-done.4, s32[1,8,8]{2,1,0:T(8,128)S(1)} %copy-done.5, ...), custom_call_target="tpu_custom_call" | custom-call | tf_op jit(solution)/shard_map/pick/pallas_call | solution.py:273
  2.3 3.5 %collective-permute-start.2 = (bf16[1,72,128]{2,1,0:T(8,128)(2,1)S(1)}, bf16[1,72,128]{2,1,0:T(8,128)(2,1)S(1)}, u32[]{:S(2)}, u32[]{:S(2)}) collective-permute-start(bf16[1,72,128]{2,1,0:T(8,128)(2,1)S(1)} %bitcast.3), channel_id=1, source_target_pairs={{12,1},{13,0},{8,5},{9,4},{0,9},{1,8},{4,13},{5,12},{14,3},{15,2},... | collective-permute-start | bytes 55304 | tf_op jit(solution)/shard_map/ppermute | solution.py:290
  5.8 1.1 %collective-permute-start.1 = (bf16[1,72,128]{2,1,0:T(8,128)(2,1)S(1)}, bf16[1,72,128]{2,1,0:T(8,128)(2,1)S(1)}, u32[]{:S(2)}, u32[]{:S(2)}) collective-permute-start(bf16[1,72,128]{2,1,0:T(8,128)(2,1)S(1)} %bitcast.4), channel_id=1, source_target_pairs={{8,1},{9,0},{12,5},{13,4},{4,9},{5,8},{0,13},{1,12},{10,3},{11,2},... | collective-permute-start | bytes 55304 | tf_op jit(solution)/shard_map/ppermute | solution.py:290
  6.8 0.8 %collective-permute-start = (bf16[1,72,128]{2,1,0:T(8,128)(2,1)S(1)}, bf16[1,72,128]{2,1,0:T(8,128)(2,1)S(1)}, u32[]{:S(2)}, u32[]{:S(2)}) collective-permute-start(bf16[1,72,128]{2,1,0:T(8,128)(2,1)S(1)} %bitcast.5), channel_id=1, source_target_pairs={{4,1},{5,0},{0,5},{1,4},{12,9},{13,8},{8,13},{9,12},{6,3},{7,2},{2... | collective-permute-start | bytes 55304 | tf_op jit(solution)/shard_map/ppermute | solution.py:290
  7.6 0.7 %collective-permute-done.2 = bf16[1,72,128]{2,1,0:T(8,128)(2,1)S(1)} collective-permute-done((bf16[1,72,128]{2,1,0:T(8,128)(2,1)S(1)}, bf16[1,72,128]{2,1,0:T(8,128)(2,1)S(1)}, u32[]{:S(2)}, u32[]{:S(2)}) %collective-permute-start.2) | collective-permute-done | bytes 18464 | tf_op jit(solution)/shard_map/ppermute | solution.py:290
  8.3 1.5 %collective-permute-done.1 = bf16[1,72,128]{2,1,0:T(8,128)(2,1)S(1)} collective-permute-done((bf16[1,72,128]{2,1,0:T(8,128)(2,1)S(1)}, bf16[1,72,128]{2,1,0:T(8,128)(2,1)S(1)}, u32[]{:S(2)}, u32[]{:S(2)}) %collective-permute-start.1) | collective-permute-done | bytes 18464 | tf_op jit(solution)/shard_map/ppermute | solution.py:290
  9.9 0.2 %collective-permute-done = bf16[1,72,128]{2,1,0:T(8,128)(2,1)S(1)} collective-permute-done((bf16[1,72,128]{2,1,0:T(8,128)(2,1)S(1)}, bf16[1,72,128]{2,1,0:T(8,128)(2,1)S(1)}, u32[]{:S(2)}, u32[]{:S(2)}) %collective-permute-start) | collective-permute-done | bytes 18464 | tf_op jit(solution)/shard_map/ppermute | solution.py:290
  10.1 0.7 %collective-permute-start.3 = (bf16[4,72,128]{2,1,0:T(8,128)(2,1)S(1)}, bf16[4,72,128]{2,1,0:T(8,128)(2,1)S(1)}, u32[]{:S(2)}, u32[]{:S(2)}) collective-permute-start(bf16[4,72,128]{2,1,0:T(8,128)(2,1)S(1)} %pad_maximum_fusion.near_ref), channel_id=1, source_target_pairs={{0,1},{1,0},{4,5},{5,4},{8,9},{9,8},{12,13},{13,12},{2,3},{3,2},{6... | collective-permute-start | bytes 221192 | tf_op jit(solution)/shard_map/ppermute | solution.py:290
  10.8 0.0 copy-done
  10.8 0.4 %widen.1.wide_ref = f32[4,64,1024]{2,1,0:T(8,128)S(1)} custom-call(bf16[4,72,128]{2,1,0:T(8,128)(2,1)S(1)} %pad_maximum_fusion.near_ref, bf16[128,1024]{1,0:T(8,128)(2,1)S(1)} %copy-done), custom_call_target="tpu_custom_call" | custom-call | flops 67108864 | bytes 1048576 | tf_op jit(solution)/shard_map/widen/pallas_call | solution.py:297
  11.2 0.5 %collective-permute-done.3.far_ref = bf16[4,72,128]{2,1,0:T(8,128)(2,1)S(1)} collective-permute-done((bf16[4,72,128]{2,1,0:T(8,128)(2,1)S(1)}, bf16[4,72,128]{2,1,0:T(8,128)(2,1)S(1)}, u32[]{:S(2)}, u32[]{:S(2)}) %collective-permute-start.3) | collective-permute-done | bytes 73760 | tf_op jit(solution)/shard_map/ppermute | solution.py:290
  11.7 1.5 %march.1 = (bf16[1,32,512]{2,1,0:T(8,128)(2,1)}, f32[8,32]{1,0:T(8,128)}) custom-call(bf16[4,72,128]{2,1,0:T(8,128)(2,1)S(1)} %pad_maximum_fusion.near_ref, bf16[4,72,128]{2,1,0:T(8,128)(2,1)S(1)} %collective-permute-done.3.far_ref, f32[4,64,1024]{2,1,0:T(8,128)S(1)} %widen.1.wide_ref, bf16[128,1024]{1,0:T(8,128)(2,1)S(1)} %copy-done, ...), custom_call_target="tpu_custom_call" | custom-call | tf_op jit(solution)/shard_map/march/pallas_call | solution.py:312
  (3 shorter events, 0.0 us)
Async XLA Ops:
  0.6 0.9 %copy-start.2 = (bf16[1,32,512]{2,1,0:T(8,128)(2,1)S(1)}, bf16[1,32,512]{2,1,0:T(8,128)(2,1)}, u32[]{:S(2)}) copy-start(bf16[1,32,512]{2,1,0:T(8,128)(2,1)} %cotangent_ref.1) | copy-start | bytes 98308
  0.6 1.1 %copy-start.1 = (bf16[1,512,512]{2,1,0:T(8,128)(2,1)S(1)}, bf16[1,512,512]{2,1,0:T(8,128)(2,1)}, u32[]{:S(2)}) copy-start(bf16[1,512,512]{2,1,0:T(8,128)(2,1)} %inverse_ref.1) | copy-start | bytes 1572868
  0.7 1.1 %copy-start.3 = (s32[1,8,8]{2,1,0:T(8,128)S(1)}, s32[1,8,8]{2,1,0:T(8,128)}, u32[]{:S(2)}) copy-start(s32[1,8,8]{2,1,0:T(8,128)} %into_ref.1) | copy-start | bytes 772
  0.7 1.1 %copy-start.4 = (s32[1,8,8]{2,1,0:T(8,128)S(1)}, s32[1,8,8]{2,1,0:T(8,128)}, u32[]{:S(2)}) copy-start(s32[1,8,8]{2,1,0:T(8,128)} %from_ref.1) | copy-start | bytes 772
  0.7 1.1 %copy-start.5 = (s32[1,8,8]{2,1,0:T(8,128)S(1)}, s32[1,8,8]{2,1,0:T(8,128)}, u32[]{:S(2)}) copy-start(s32[1,8,8]{2,1,0:T(8,128)} %offset_ref.1) | copy-start | bytes 772
  0.7 1.1 %copy-start.6 = (f32[1,8,8]{2,1,0:T(8,128)S(1)}, f32[1,8,8]{2,1,0:T(8,128)}, u32[]{:S(2)}) copy-start(f32[1,8,8]{2,1,0:T(8,128)} %weight_ref.1) | copy-start | bytes 772
  0.7 1.0 %copy-start.7 = (f32[1,8,8]{2,1,0:T(8,128)S(1)}, f32[1,8,8]{2,1,0:T(8,128)}, u32[]{:S(2)}) copy-start(f32[1,8,8]{2,1,0:T(8,128)} %admit_ref.1) | copy-start | bytes 772
  0.7 0.7 %copy-start.8 = (s32[32]{0:T(128)S(1)}, s32[32]{0:T(128)}, u32[]{:S(2)}) copy-start(s32[32]{0:T(128)} %param.18) | copy-start | bytes 388
  1.7 9.1 %copy-start = (bf16[128,1024]{1,0:T(8,128)(2,1)S(1)}, bf16[128,1024]{1,0:T(8,128)(2,1)}, u32[]{:S(2)}) copy-start(bf16[128,1024]{1,0:T(8,128)(2,1)} %constant.9.clone.spread_ref) | copy-start | bytes 786436
  2.3 6.1 %collective-permute-start.2 = (bf16[1,72,128]{2,1,0:T(8,128)(2,1)S(1)}, bf16[1,72,128]{2,1,0:T(8,128)(2,1)S(1)}, u32[]{:S(2)}, u32[]{:S(2)}) collective-permute-start(bf16[1,72,128]{2,1,0:T(8,128)(2,1)S(1)} %bitcast.3), channel_id=1, source_target_pairs={{12,1},{13,0},{8,5},{9,4},{0,9},{1,8},{4,13},{5,12},{14,3},{15,2},... | collective-permute-start | bytes 55304 | tf_op jit(solution)/shard_map/ppermute | solution.py:290
  5.8 4.1 %collective-permute-start.1 = (bf16[1,72,128]{2,1,0:T(8,128)(2,1)S(1)}, bf16[1,72,128]{2,1,0:T(8,128)(2,1)S(1)}, u32[]{:S(2)}, u32[]{:S(2)}) collective-permute-start(bf16[1,72,128]{2,1,0:T(8,128)(2,1)S(1)} %bitcast.4), channel_id=1, source_target_pairs={{8,1},{9,0},{12,5},{13,4},{4,9},{5,8},{0,13},{1,12},{10,3},{11,2},... | collective-permute-start | bytes 55304 | tf_op jit(solution)/shard_map/ppermute | solution.py:290
  6.8 3.2 %collective-permute-start = (bf16[1,72,128]{2,1,0:T(8,128)(2,1)S(1)}, bf16[1,72,128]{2,1,0:T(8,128)(2,1)S(1)}, u32[]{:S(2)}, u32[]{:S(2)}) collective-permute-start(bf16[1,72,128]{2,1,0:T(8,128)(2,1)S(1)} %bitcast.5), channel_id=1, source_target_pairs={{4,1},{5,0},{0,5},{1,4},{12,9},{13,8},{8,13},{9,12},{6,3},{7,2},{2... | collective-permute-start | bytes 55304 | tf_op jit(solution)/shard_map/ppermute | solution.py:290
  10.1 1.7 %collective-permute-start.3 = (bf16[4,72,128]{2,1,0:T(8,128)(2,1)S(1)}, bf16[4,72,128]{2,1,0:T(8,128)(2,1)S(1)}, u32[]{:S(2)}, u32[]{:S(2)}) collective-permute-start(bf16[4,72,128]{2,1,0:T(8,128)(2,1)S(1)} %pad_maximum_fusion.near_ref), channel_id=1, source_target_pairs={{0,1},{1,0},{4,5},{5,4},{8,9},{9,8},{12,13},{13,12},{2,3},{3,2},{6... | collective-permute-start | bytes 221192 | tf_op jit(solution)/shard_map/ppermute | solution.py:290

commit v6 on v5

--- a/solution.py
+++ b/solution.py
@@ -194,8 +194,8 @@
         return [lanes(part, 0) for part in both], [lanes(part, 1) for part in both]
 
     seven, fault = spread_of(count, [block[:slots] for block in fresh])
+    factor = [*spread_of(0, pieces)]
     seven = exchange(seven)
-    factor = [*spread_of(0, pieces)]
 
     def seen(drive):
         total = fault[0] * drive[0].astype(jnp.float32)
@@ -219,12 +219,12 @@
     row_b = seen(drive)
     arrived = exchange([rounded(part) for part in result])
     later = [later[o] + factor[1][o] * arrived[o] for o in range(owners)]
-    drive = [part + pltpu.roll(part, 2 * columns, 1) for part in later]
-    own = drive[0].T[columns : 2 * columns].astype(jnp.bfloat16)
+    turned = later[0].T
+    own = (turned[columns : 2 * columns] + turned[3 * columns :]).astype(jnp.bfloat16)
     first_ref[0] = dot(own, rows_ref[...]).astype(jnp.bfloat16)
     save_first = pltpu.make_async_copy(first_ref, first_hbm, semaphores.at[0])
     save_first.start()
-    row_c = seen([part.astype(jnp.bfloat16) for part in drive])
+    row_c = seen([(part + pltpu.roll(part, 2 * columns, 1)).astype(jnp.bfloat16) for part in later])
     row_s = sum(block[slots + 7 : slots + 8].astype(jnp.float32) for block in blocks)
 
     def back(value, quarters):

time: 13.4 us -> 13.4 us (level)
  no operation moved by 1% of the time
where the time goes in v6:
time: 13.4 us; the launch traced here: 13.2 us
  starting transfers between devices  6.11 us (46%)
  waiting for transfers between devices  2.95 us (22%)
  Pallas kernels  2.37 us (18%)
  between operations  1.45 us (11%)
  local copies, waits for them, and re-layouts  0.25 us (2%)
    ppermute x4, starting transfers between devices, send(): return lax.ppermute(held, OWNER_AXES, pairs)  6.11 us
    ppermute x4, waiting for transfers between devices, send(): return lax.ppermute(held, OWNER_AXES, pairs)  2.95 us
    pallas_call x1, Pallas kernels, gathered_plan(): pl.pallas_call(march_kernel, out_shape=outputs, in_specs=[vmem] * 5, out_...  1.51 us
    pallas_call x1, Pallas kernels, gathered_plan(): pl.pallas_call(pick_kernel, out_shape=(jax.ShapeDtypeStruct((height, LANE...  0.49 us
    pallas_call x1, Pallas kernels, gathered_plan(): pl.pallas_call(widen_kernel, out_shape=jax.ShapeDtypeStruct((near.shape[0...  0.36 us
  transfers between devices with their start and end apart: 4, of which 4 were waited for; matrix products, arithmetic and copies ran while one was open for 0% of the time, Pallas kernels for 3%

profile of v6, /device:TPU:0, one launch (start us, length us, event | category | flops | bytes accessed | tf_op | source)
XLA Modules:
  0.0 13.2 jit_solution(1048715727359253512)
XLA Ops:
  0.6 0.0 copy-start.2
  0.6 0.0 copy-start.1
  0.7 0.0 copy-start.3
  0.7 0.0 copy-start.4
  0.7 0.0 copy-start.5
  0.7 0.0 copy-start.6
  0.7 0.0 copy-start.7
  0.7 0.0 copy-start.8
  1.4 0.0 copy-done.8
  1.4 0.1 add_bitcast_fusion.packed_ref
  1.5 0.0 copy-done.2
  1.5 0.2 %copy-done.1 = bf16[1,512,512]{2,1,0:T(8,128)(2,1)S(1)} copy-done((bf16[1,512,512]{2,1,0:T(8,128)(2,1)S(1)}, bf16[1,512,512]{2,1,0:T(8,128)(2,1)}, u32[]{:S(2)}) %copy-start.1) | copy-done | bytes 524312
  1.7 0.0 copy-done.3
  1.7 0.0 copy-done.4
  1.7 0.0 copy-done.5
  1.7 0.0 copy-done.6
  1.7 0.0 copy-done.7
  1.7 0.0 copy-start
  1.8 0.5 %pick.1 = (bf16[72,128]{1,0:T(8,128)(2,1)S(1)}, bf16[64,512]{1,0:T(8,128)(2,1)S(1)}) custom-call(s32[1,33]{1,0:T(1,128)S(1)} %add_bitcast_fusion.packed_ref, f32[8,512]{1,0:T(8,128)S(1)} %lane.1.lane_ref, s32[1,8,8]{2,1,0:T(8,128)S(1)} %copy-done.3, s32[1,8,8]{2,1,0:T(8,128)S(1)} %copy-done.4, s32[1,8,8]{2,1,0:T(8,128)S(1)} %copy-done.5, ...), custom_call_target="tpu_custom_call" | custom-call | tf_op jit(solution)/shard_map/pick/pallas_call | solution.py:273
  2.3 3.5 %collective-permute-start.2 = (bf16[1,72,128]{2,1,0:T(8,128)(2,1)S(1)}, bf16[1,72,128]{2,1,0:T(8,128)(2,1)S(1)}, u32[]{:S(2)}, u32[]{:S(2)}) collective-permute-start(bf16[1,72,128]{2,1,0:T(8,128)(2,1)S(1)} %bitcast.3), channel_id=1, source_target_pairs={{12,1},{13,0},{8,5},{9,4},{0,9},{1,8},{4,13},{5,12},{14,3},{15,2},... | collective-permute-start | bytes 55304 | tf_op jit(solution)/shard_map/ppermute | solution.py:290
  5.8 1.1 %collective-permute-start.1 = (bf16[1,72,128]{2,1,0:T(8,128)(2,1)S(1)}, bf16[1,72,128]{2,1,0:T(8,128)(2,1)S(1)}, u32[]{:S(2)}, u32[]{:S(2)}) collective-permute-start(bf16[1,72,128]{2,1,0:T(8,128)(2,1)S(1)} %bitcast.4), channel_id=1, source_target_pairs={{8,1},{9,0},{12,5},{13,4},{4,9},{5,8},{0,13},{1,12},{10,3},{11,2},... | collective-permute-start | bytes 55304 | tf_op jit(solution)/shard_map/ppermute | solution.py:290
  6.8 0.8 %collective-permute-start = (bf16[1,72,128]{2,1,0:T(8,128)(2,1)S(1)}, bf16[1,72,128]{2,1,0:T(8,128)(2,1)S(1)}, u32[]{:S(2)}, u32[]{:S(2)}) collective-permute-start(bf16[1,72,128]{2,1,0:T(8,128)(2,1)S(1)} %bitcast.5), channel_id=1, source_target_pairs={{4,1},{5,0},{0,5},{1,4},{12,9},{13,8},{8,13},{9,12},{6,3},{7,2},{2... | collective-permute-start | bytes 55304 | tf_op jit(solution)/shard_map/ppermute | solution.py:290
  7.6 0.7 %collective-permute-done.2 = bf16[1,72,128]{2,1,0:T(8,128)(2,1)S(1)} collective-permute-done((bf16[1,72,128]{2,1,0:T(8,128)(2,1)S(1)}, bf16[1,72,128]{2,1,0:T(8,128)(2,1)S(1)}, u32[]{:S(2)}, u32[]{:S(2)}) %collective-permute-start.2) | collective-permute-done | bytes 18464 | tf_op jit(solution)/shard_map/ppermute | solution.py:290
  8.3 1.5 %collective-permute-done.1 = bf16[1,72,128]{2,1,0:T(8,128)(2,1)S(1)} collective-permute-done((bf16[1,72,128]{2,1,0:T(8,128)(2,1)S(1)}, bf16[1,72,128]{2,1,0:T(8,128)(2,1)S(1)}, u32[]{:S(2)}, u32[]{:S(2)}) %collective-permute-start.1) | collective-permute-done | bytes 18464 | tf_op jit(solution)/shard_map/ppermute | solution.py:290
  9.9 0.2 %collective-permute-done = bf16[1,72,128]{2,1,0:T(8,128)(2,1)S(1)} collective-permute-done((bf16[1,72,128]{2,1,0:T(8,128)(2,1)S(1)}, bf16[1,72,128]{2,1,0:T(8,128)(2,1)S(1)}, u32[]{:S(2)}, u32[]{:S(2)}) %collective-permute-start) | collective-permute-done | bytes 18464 | tf_op jit(solution)/shard_map/ppermute | solution.py:290
  10.1 0.7 %collective-permute-start.3 = (bf16[4,72,128]{2,1,0:T(8,128)(2,1)S(1)}, bf16[4,72,128]{2,1,0:T(8,128)(2,1)S(1)}, u32[]{:S(2)}, u32[]{:S(2)}) collective-permute-start(bf16[4,72,128]{2,1,0:T(8,128)(2,1)S(1)} %pad_maximum_fusion.near_ref), channel_id=1, source_target_pairs={{0,1},{1,0},{4,5},{5,4},{8,9},{9,8},{12,13},{13,12},{2,3},{3,2},{6... | collective-permute-start | bytes 221192 | tf_op jit(solution)/shard_map/ppermute | solution.py:290
  10.8 0.0 copy-done
  10.8 0.4 %widen.1.wide_ref = f32[4,64,1024]{2,1,0:T(8,128)S(1)} custom-call(bf16[4,72,128]{2,1,0:T(8,128)(2,1)S(1)} %pad_maximum_fusion.near_ref, bf16[128,1024]{1,0:T(8,128)(2,1)S(1)} %copy-done), custom_call_target="tpu_custom_call" | custom-call | flops 67108864 | bytes 1048576 | tf_op jit(solution)/shard_map/widen/pallas_call | solution.py:297
  11.2 0.5 %collective-permute-done.3.far_ref = bf16[4,72,128]{2,1,0:T(8,128)(2,1)S(1)} collective-permute-done((bf16[4,72,128]{2,1,0:T(8,128)(2,1)S(1)}, bf16[4,72,128]{2,1,0:T(8,128)(2,1)S(1)}, u32[]{:S(2)}, u32[]{:S(2)}) %collective-permute-start.3) | collective-permute-done | bytes 73760 | tf_op jit(solution)/shard_map/ppermute | solution.py:290
  11.7 1.5 %march.1 = (bf16[1,32,512]{2,1,0:T(8,128)(2,1)}, f32[8,32]{1,0:T(8,128)}) custom-call(bf16[4,72,128]{2,1,0:T(8,128)(2,1)S(1)} %pad_maximum_fusion.near_ref, bf16[4,72,128]{2,1,0:T(8,128)(2,1)S(1)} %collective-permute-done.3.far_ref, f32[4,64,1024]{2,1,0:T(8,128)S(1)} %widen.1.wide_ref, bf16[128,1024]{1,0:T(8,128)(2,1)S(1)} %copy-done, ...), custom_call_target="tpu_custom_call" | custom-call | tf_op jit(solution)/shard_map/march/pallas_call | solution.py:312
  (3 shorter events, 0.0 us)
Async XLA Ops:
  0.6 0.9 %copy-start.2 = (bf16[1,32,512]{2,1,0:T(8,128)(2,1)S(1)}, bf16[1,32,512]{2,1,0:T(8,128)(2,1)}, u32[]{:S(2)}) copy-start(bf16[1,32,512]{2,1,0:T(8,128)(2,1)} %cotangent_ref.1) | copy-start | bytes 98308
  0.6 1.1 %copy-start.1 = (bf16[1,512,512]{2,1,0:T(8,128)(2,1)S(1)}, bf16[1,512,512]{2,1,0:T(8,128)(2,1)}, u32[]{:S(2)}) copy-start(bf16[1,512,512]{2,1,0:T(8,128)(2,1)} %inverse_ref.1) | copy-start | bytes 1572868
  0.7 1.1 %copy-start.3 = (s32[1,8,8]{2,1,0:T(8,128)S(1)}, s32[1,8,8]{2,1,0:T(8,128)}, u32[]{:S(2)}) copy-start(s32[1,8,8]{2,1,0:T(8,128)} %into_ref.1) | copy-start | bytes 772
  0.7 1.1 %copy-start.4 = (s32[1,8,8]{2,1,0:T(8,128)S(1)}, s32[1,8,8]{2,1,0:T(8,128)}, u32[]{:S(2)}) copy-start(s32[1,8,8]{2,1,0:T(8,128)} %from_ref.1) | copy-start | bytes 772
  0.7 1.1 %copy-start.5 = (s32[1,8,8]{2,1,0:T(8,128)S(1)}, s32[1,8,8]{2,1,0:T(8,128)}, u32[]{:S(2)}) copy-start(s32[1,8,8]{2,1,0:T(8,128)} %offset_ref.1) | copy-start | bytes 772
  0.7 1.1 %copy-start.6 = (f32[1,8,8]{2,1,0:T(8,128)S(1)}, f32[1,8,8]{2,1,0:T(8,128)}, u32[]{:S(2)}) copy-start(f32[1,8,8]{2,1,0:T(8,128)} %weight_ref.1) | copy-start | bytes 772
  0.7 1.0 %copy-start.7 = (f32[1,8,8]{2,1,0:T(8,128)S(1)}, f32[1,8,8]{2,1,0:T(8,128)}, u32[]{:S(2)}) copy-start(f32[1,8,8]{2,1,0:T(8,128)} %admit_ref.1) | copy-start | bytes 772
  0.7 0.7 %copy-start.8 = (s32[32]{0:T(128)S(1)}, s32[32]{0:T(128)}, u32[]{:S(2)}) copy-start(s32[32]{0:T(128)} %param.18) | copy-start | bytes 388
  1.7 9.1 %copy-start = (bf16[128,1024]{1,0:T(8,128)(2,1)S(1)}, bf16[128,1024]{1,0:T(8,128)(2,1)}, u32[]{:S(2)}) copy-start(bf16[128,1024]{1,0:T(8,128)(2,1)} %constant.9.clone.spread_ref) | copy-start | bytes 786436
  2.3 6.1 %collective-permute-start.2 = (bf16[1,72,128]{2,1,0:T(8,128)(2,1)S(1)}, bf16[1,72,128]{2,1,0:T(8,128)(2,1)S(1)}, u32[]{:S(2)}, u32[]{:S(2)}) collective-permute-start(bf16[1,72,128]{2,1,0:T(8,128)(2,1)S(1)} %bitcast.3), channel_id=1, source_target_pairs={{12,1},{13,0},{8,5},{9,4},{0,9},{1,8},{4,13},{5,12},{14,3},{15,2},... | collective-permute-start | bytes 55304 | tf_op jit(solution)/shard_map/ppermute | solution.py:290
  5.8 4.1 %collective-permute-start.1 = (bf16[1,72,128]{2,1,0:T(8,128)(2,1)S(1)}, bf16[1,72,128]{2,1,0:T(8,128)(2,1)S(1)}, u32[]{:S(2)}, u32[]{:S(2)}) collective-permute-start(bf16[1,72,128]{2,1,0:T(8,128)(2,1)S(1)} %bitcast.4), channel_id=1, source_target_pairs={{8,1},{9,0},{12,5},{13,4},{4,9},{5,8},{0,13},{1,12},{10,3},{11,2},... | collective-permute-start | bytes 55304 | tf_op jit(solution)/shard_map/ppermute | solution.py:290
  6.8 3.2 %collective-permute-start = (bf16[1,72,128]{2,1,0:T(8,128)(2,1)S(1)}, bf16[1,72,128]{2,1,0:T(8,128)(2,1)S(1)}, u32[]{:S(2)}, u32[]{:S(2)}) collective-permute-start(bf16[1,72,128]{2,1,0:T(8,128)(2,1)S(1)} %bitcast.5), channel_id=1, source_target_pairs={{4,1},{5,0},{0,5},{1,4},{12,9},{13,8},{8,13},{9,12},{6,3},{7,2},{2... | collective-permute-start | bytes 55304 | tf_op jit(solution)/shard_map/ppermute | solution.py:290
  10.1 1.7 %collective-permute-start.3 = (bf16[4,72,128]{2,1,0:T(8,128)(2,1)S(1)}, bf16[4,72,128]{2,1,0:T(8,128)(2,1)S(1)}, u32[]{:S(2)}, u32[]{:S(2)}) collective-permute-start(bf16[4,72,128]{2,1,0:T(8,128)(2,1)S(1)} %pad_maximum_fusion.near_ref), channel_id=1, source_target_pairs={{0,1},{1,0},{4,5},{5,4},{8,9},{9,8},{12,13},{13,12},{2,3},{3,2},{6... | collective-permute-start | bytes 221192 | tf_op jit(solution)/shard_map/ppermute | solution.py:290

commit v7 on v6

--- a/solution.py
+++ b/solution.py
@@ -43,8 +43,19 @@
     return spread
 
 
-SOURCES = ((1, 0, 3, 2), (2, 3, 1, 0), (3, 2, 0, 1))
+SOURCES = (
+    ((1, 2, 3, 0), (2, 3, 0, 1), (3, 0, 1, 2)),
+    ((1, 3, 0, 2), (3, 2, 1, 0), (2, 0, 3, 1)),
+)
 HELD = (0, 3, 5, 7, 1, 2, 4, 6)
+
+
+def spot_of(place, apart):
+    if apart == 0:
+        return 0
+    spots = [1 + [p[z] for p in SOURCES[core]].index(z ^ apart) for z in range(4) for core in range(2)]
+    bits = sum(spot << (2 * device) for device, spot in enumerate(spots))
+    return (jnp.int32(bits) >> (2 * place)) & 3
 
 
 def column_of(ref, place):
@@ -152,7 +163,8 @@
 
 
 def widen_kernel(near_ref, spread_ref, wide_ref):
-    messages = [near_ref[p] for p in range(near_ref.shape[0])]
+    place = owner_here()
+    messages = [near_ref[spot_of(place, p)] for p in range(near_ref.shape[0])]
     count = LANES * len(VARIANTS)
     for index, piece in enumerate(turned_pieces(messages)):
         wide_ref[index, :, :count] = dot(piece, spread_ref[:, :count])
@@ -162,8 +174,9 @@
 def march_kernel(
     near_ref, far_ref, wide_ref, spread_ref, rows_ref, first_hbm, fault_hbm, first_ref, fault_ref, semaphores
 ):
-    held = (near_ref, far_ref)
-    owners = sum(ref.shape[0] for ref in held)
+    place = owner_here()
+    held = ((near_ref, place), (far_ref, lax.bitwise_xor(place, jnp.int32(1))))
+    owners = sum(ref.shape[0] for ref, _ in held)
     slots = rows_ref.shape[0]
     columns = first_ref.shape[1]
     depth = slots // owners
@@ -182,7 +195,7 @@
     def rounded(value):
         return value.astype(jnp.bfloat16).astype(jnp.float32)
 
-    blocks = [ref[p] for ref in held for p in range(ref.shape[0])]
+    blocks = [ref[spot_of(holder, p)] for ref, holder in held for p in range(ref.shape[0])]
     system = [block[:slots, :slots] for block in blocks]
     fresh = blocks[-far_ref.shape[0] :]
     pieces = turned_pieces(fresh)
@@ -285,15 +298,13 @@
     width = spread.shape[1]
 
 
-    def send(held, sources):
-        pairs = [(2 * source + core, 2 * z + 1 - core) for z, source in enumerate(sources) for core in range(2)]
+    def send(held, *sources):
+        pairs = [(2 * sources[core][z] + 1 - core, 2 * z + core) for z in range(4) for core in range(2)]
         return lax.ppermute(held, OWNER_AXES, pairs)
 
     own = message[None]
-    beside, second, third = (send(own, sources) for sources in SOURCES)
-    low = lax.axis_index(OWNER_AXES[0]) < 2
-    near = jnp.concatenate([own, beside, jnp.where(low, second, third), jnp.where(low, third, second)], axis=0)
-    far = send(near, range(len(SOURCES) + 1))
+    near = jnp.concatenate([own] + [send(own, *pair) for pair in zip(*SOURCES)], axis=0)
+    far = send(near, range(4), range(4))
     wide = pl.pallas_call(
         widen_kernel,
         out_shape=jax.ShapeDtypeStruct((near.shape[0], slots, width), jnp.float32),

time: 13.4 us -> 13.2 us (0.985)
  starting transfers between devices: 6.11 us -> 5.72 us
  waiting for transfers between devices: 2.95 us -> 3.09 us
    ppermute x4, starting transfers between devices: 6.11 us -> 5.72 us  [send(): return lax.ppermute(held, OWNER_AXES, pairs)]
where the time goes in v7:
time: 13.2 us; the launch traced here: 13 us
  starting transfers between devices  5.72 us (43%)
  waiting for transfers between devices  3.09 us (23%)
  Pallas kernels  2.42 us (18%)
  between operations  1.45 us (11%)
  local copies, waits for them, and re-layouts  0.25 us (2%)
    ppermute x4, starting transfers between devices, send(): return lax.ppermute(held, OWNER_AXES, pairs)  5.72 us
    ppermute x4, waiting for transfers between devices, send(): return lax.ppermute(held, OWNER_AXES, pairs)  3.09 us
    pallas_call x1, Pallas kernels, gathered_plan(): pl.pallas_call(march_kernel, out_shape=outputs, in_specs=[vmem] * 5, out_...  1.54 us
    pallas_call x1, Pallas kernels, gathered_plan(): pl.pallas_call(pick_kernel, out_shape=(jax.ShapeDtypeStruct((height, LANE...  0.49 us
    pallas_call x1, Pallas kernels, gathered_plan(): pl.pallas_call(widen_kernel, out_shape=jax.ShapeDtypeStruct((near.shape[0...  0.37 us
  transfers between devices with their start and end apart: 4, of which 4 were waited for; matrix products, arithmetic and copies ran while one was open for 0% of the time, Pallas kernels for 3%

profile of v7, /device:TPU:0, one launch (start us, length us, event | category | flops | bytes accessed | tf_op | source)
XLA Modules:
  0.0 13.0 jit_solution(6969354703594176519)
XLA Ops:
  0.6 0.0 copy-start.2
  0.6 0.0 copy-start.1
  0.7 0.0 copy-start.3
  0.7 0.0 copy-start.4
  0.7 0.0 copy-start.5
  0.7 0.0 copy-start.6
  0.7 0.0 copy-start.7
  0.7 0.0 copy-start.8
  1.4 0.0 copy-done.8
  1.4 0.1 add_bitcast_fusion.packed_ref
  1.5 0.0 copy-done.2
  1.5 0.2 %copy-done.1 = bf16[1,512,512]{2,1,0:T(8,128)(2,1)S(1)} copy-done((bf16[1,512,512]{2,1,0:T(8,128)(2,1)S(1)}, bf16[1,512,512]{2,1,0:T(8,128)(2,1)}, u32[]{:S(2)}) %copy-start.1) | copy-done | bytes 524312
  1.7 0.0 copy-done.3
  1.7 0.0 copy-done.4
  1.7 0.0 copy-done.5
  1.7 0.0 copy-done.6
  1.7 0.0 copy-done.7
  1.7 0.0 copy-start
  1.8 0.5 %pick.1 = (bf16[72,128]{1,0:T(8,128)(2,1)S(1)}, bf16[64,512]{1,0:T(8,128)(2,1)S(1)}) custom-call(s32[1,33]{1,0:T(1,128)S(1)} %add_bitcast_fusion.packed_ref, f32[8,512]{1,0:T(8,128)S(1)} %lane.1.lane_ref, s32[1,8,8]{2,1,0:T(8,128)S(1)} %copy-done.3, s32[1,8,8]{2,1,0:T(8,128)S(1)} %copy-done.4, s32[1,8,8]{2,1,0:T(8,128)S(1)} %copy-done.5, ...), custom_call_target="tpu_custom_call" | custom-call | tf_op jit(solution)/shard_map/pick/pallas_call | solution.py:286
  2.3 2.5 %collective-permute-start.2 = (bf16[1,72,128]{2,1,0:T(8,128)(2,1)S(1)}, bf16[1,72,128]{2,1,0:T(8,128)(2,1)S(1)}, u32[]{:S(2)}, u32[]{:S(2)}) collective-permute-start(bf16[1,72,128]{2,1,0:T(8,128)(2,1)S(1)} %bitcast.3), channel_id=1, source_target_pairs={{13,0},{8,1},{1,4},{0,5},{5,8},{12,9},{9,12},{4,13},{15,2},{10,3},... | collective-permute-start | bytes 55304 | tf_op jit(solution)/shard_map/ppermute | solution.py:303
  4.7 2.1 %collective-permute-start.1 = (bf16[1,72,128]{2,1,0:T(8,128)(2,1)S(1)}, bf16[1,72,128]{2,1,0:T(8,128)(2,1)S(1)}, u32[]{:S(2)}, u32[]{:S(2)}) collective-permute-start(bf16[1,72,128]{2,1,0:T(8,128)(2,1)S(1)} %bitcast.4), channel_id=1, source_target_pairs={{9,0},{12,1},{13,4},{8,5},{1,8},{4,9},{5,12},{0,13},{11,2},{14,3},... | collective-permute-start | bytes 55304 | tf_op jit(solution)/shard_map/ppermute | solution.py:303
  6.8 0.8 %collective-permute-start = (bf16[1,72,128]{2,1,0:T(8,128)(2,1)S(1)}, bf16[1,72,128]{2,1,0:T(8,128)(2,1)S(1)}, u32[]{:S(2)}, u32[]{:S(2)}) collective-permute-start(bf16[1,72,128]{2,1,0:T(8,128)(2,1)S(1)} %bitcast.5), channel_id=1, source_target_pairs={{5,0},{4,1},{9,4},{12,5},{13,8},{0,9},{1,12},{8,13},{7,2},{6,3},{1... | collective-permute-start | bytes 55304 | tf_op jit(solution)/shard_map/ppermute | solution.py:303
  7.6 0.6 %collective-permute-done.2 = bf16[1,72,128]{2,1,0:T(8,128)(2,1)S(1)} collective-permute-done((bf16[1,72,128]{2,1,0:T(8,128)(2,1)S(1)}, bf16[1,72,128]{2,1,0:T(8,128)(2,1)S(1)}, u32[]{:S(2)}, u32[]{:S(2)}) %collective-permute-start.2) | collective-permute-done | bytes 18464 | tf_op jit(solution)/shard_map/ppermute | solution.py:303
  8.2 0.8 %collective-permute-done.1 = bf16[1,72,128]{2,1,0:T(8,128)(2,1)S(1)} collective-permute-done((bf16[1,72,128]{2,1,0:T(8,128)(2,1)S(1)}, bf16[1,72,128]{2,1,0:T(8,128)(2,1)S(1)}, u32[]{:S(2)}, u32[]{:S(2)}) %collective-permute-start.1) | collective-permute-done | bytes 18464 | tf_op jit(solution)/shard_map/ppermute | solution.py:303
  9.1 1.1 %collective-permute-done = bf16[1,72,128]{2,1,0:T(8,128)(2,1)S(1)} collective-permute-done((bf16[1,72,128]{2,1,0:T(8,128)(2,1)S(1)}, bf16[1,72,128]{2,1,0:T(8,128)(2,1)S(1)}, u32[]{:S(2)}, u32[]{:S(2)}) %collective-permute-start) | collective-permute-done | bytes 18464 | tf_op jit(solution)/shard_map/ppermute | solution.py:303
  10.1 0.4 %collective-permute-start.3 = (bf16[4,72,128]{2,1,0:T(8,128)(2,1)S(1)}, bf16[4,72,128]{2,1,0:T(8,128)(2,1)S(1)}, u32[]{:S(2)}, u32[]{:S(2)}) collective-permute-start(bf16[4,72,128]{2,1,0:T(8,128)(2,1)S(1)} %pad_maximum_fusion.near_ref), channel_id=1, source_target_pairs={{1,0},{0,1},{5,4},{4,5},{9,8},{8,9},{13,12},{12,13},{3,2},{2,3},{7... | collective-permute-start | bytes 221192 | tf_op jit(solution)/shard_map/ppermute | solution.py:303
  10.5 0.0 copy-done
  10.5 0.4 %widen.1.wide_ref = f32[4,64,1024]{2,1,0:T(8,128)S(1)} custom-call(bf16[4,72,128]{2,1,0:T(8,128)(2,1)S(1)} %pad_maximum_fusion.near_ref, bf16[128,1024]{1,0:T(8,128)(2,1)S(1)} %copy-done), custom_call_target="tpu_custom_call" | custom-call | flops 67108864 | bytes 1048576 | tf_op jit(solution)/shard_map/widen/pallas_call | solution.py:308
  10.9 0.6 %collective-permute-done.3.far_ref = bf16[4,72,128]{2,1,0:T(8,128)(2,1)S(1)} collective-permute-done((bf16[4,72,128]{2,1,0:T(8,128)(2,1)S(1)}, bf16[4,72,128]{2,1,0:T(8,128)(2,1)S(1)}, u32[]{:S(2)}, u32[]{:S(2)}) %collective-permute-start.3) | collective-permute-done | bytes 73760 | tf_op jit(solution)/shard_map/ppermute | solution.py:303
  11.5 1.5 %march.1 = (bf16[1,32,512]{2,1,0:T(8,128)(2,1)}, f32[8,32]{1,0:T(8,128)}) custom-call(bf16[4,72,128]{2,1,0:T(8,128)(2,1)S(1)} %pad_maximum_fusion.near_ref, bf16[4,72,128]{2,1,0:T(8,128)(2,1)S(1)} %collective-permute-done.3.far_ref, f32[4,64,1024]{2,1,0:T(8,128)S(1)} %widen.1.wide_ref, bf16[128,1024]{1,0:T(8,128)(2,1)S(1)} %copy-done, ...), custom_call_target="tpu_custom_call" | custom-call | tf_op jit(solution)/shard_map/march/pallas_call | solution.py:323
  (2 shorter events, 0.0 us)
Async XLA Ops:
  0.6 0.9 %copy-start.2 = (bf16[1,32,512]{2,1,0:T(8,128)(2,1)S(1)}, bf16[1,32,512]{2,1,0:T(8,128)(2,1)}, u32[]{:S(2)}) copy-start(bf16[1,32,512]{2,1,0:T(8,128)(2,1)} %cotangent_ref.1) | copy-start | bytes 98308
  0.6 1.1 %copy-start.1 = (bf16[1,512,512]{2,1,0:T(8,128)(2,1)S(1)}, bf16[1,512,512]{2,1,0:T(8,128)(2,1)}, u32[]{:S(2)}) copy-start(bf16[1,512,512]{2,1,0:T(8,128)(2,1)} %inverse_ref.1) | copy-start | bytes 1572868
  0.7 1.1 %copy-start.3 = (s32[1,8,8]{2,1,0:T(8,128)S(1)}, s32[1,8,8]{2,1,0:T(8,128)}, u32[]{:S(2)}) copy-start(s32[1,8,8]{2,1,0:T(8,128)} %into_ref.1) | copy-start | bytes 772
  0.7 1.1 %copy-start.4 = (s32[1,8,8]{2,1,0:T(8,128)S(1)}, s32[1,8,8]{2,1,0:T(8,128)}, u32[]{:S(2)}) copy-start(s32[1,8,8]{2,1,0:T(8,128)} %from_ref.1) | copy-start | bytes 772
  0.7 1.1 %copy-start.5 = (s32[1,8,8]{2,1,0:T(8,128)S(1)}, s32[1,8,8]{2,1,0:T(8,128)}, u32[]{:S(2)}) copy-start(s32[1,8,8]{2,1,0:T(8,128)} %offset_ref.1) | copy-start | bytes 772
  0.7 1.1 %copy-start.6 = (f32[1,8,8]{2,1,0:T(8,128)S(1)}, f32[1,8,8]{2,1,0:T(8,128)}, u32[]{:S(2)}) copy-start(f32[1,8,8]{2,1,0:T(8,128)} %weight_ref.1) | copy-start | bytes 772
  0.7 1.0 %copy-start.7 = (f32[1,8,8]{2,1,0:T(8,128)S(1)}, f32[1,8,8]{2,1,0:T(8,128)}, u32[]{:S(2)}) copy-start(f32[1,8,8]{2,1,0:T(8,128)} %admit_ref.1) | copy-start | bytes 772
  0.7 0.7 %copy-start.8 = (s32[32]{0:T(128)S(1)}, s32[32]{0:T(128)}, u32[]{:S(2)}) copy-start(s32[32]{0:T(128)} %param.18) | copy-start | bytes 388
  1.7 8.7 %copy-start = (bf16[128,1024]{1,0:T(8,128)(2,1)S(1)}, bf16[128,1024]{1,0:T(8,128)(2,1)}, u32[]{:S(2)}) copy-start(bf16[128,1024]{1,0:T(8,128)(2,1)} %constant.2.clone.spread_ref) | copy-start | bytes 786436
  2.3 6.0 %collective-permute-start.2 = (bf16[1,72,128]{2,1,0:T(8,128)(2,1)S(1)}, bf16[1,72,128]{2,1,0:T(8,128)(2,1)S(1)}, u32[]{:S(2)}, u32[]{:S(2)}) collective-permute-start(bf16[1,72,128]{2,1,0:T(8,128)(2,1)S(1)} %bitcast.3), channel_id=1, source_target_pairs={{13,0},{8,1},{1,4},{0,5},{5,8},{12,9},{9,12},{4,13},{15,2},{10,3},... | collective-permute-start | bytes 55304 | tf_op jit(solution)/shard_map/ppermute | solution.py:303
  4.7 4.3 %collective-permute-start.1 = (bf16[1,72,128]{2,1,0:T(8,128)(2,1)S(1)}, bf16[1,72,128]{2,1,0:T(8,128)(2,1)S(1)}, u32[]{:S(2)}, u32[]{:S(2)}) collective-permute-start(bf16[1,72,128]{2,1,0:T(8,128)(2,1)S(1)} %bitcast.4), channel_id=1, source_target_pairs={{9,0},{12,1},{13,4},{8,5},{1,8},{4,9},{5,12},{0,13},{11,2},{14,3},... | collective-permute-start | bytes 55304 | tf_op jit(solution)/shard_map/ppermute | solution.py:303
  6.8 3.3 %collective-permute-start = (bf16[1,72,128]{2,1,0:T(8,128)(2,1)S(1)}, bf16[1,72,128]{2,1,0:T(8,128)(2,1)S(1)}, u32[]{:S(2)}, u32[]{:S(2)}) collective-permute-start(bf16[1,72,128]{2,1,0:T(8,128)(2,1)S(1)} %bitcast.5), channel_id=1, source_target_pairs={{5,0},{4,1},{9,4},{12,5},{13,8},{0,9},{1,12},{8,13},{7,2},{6,3},{1... | collective-permute-start | bytes 55304 | tf_op jit(solution)/shard_map/ppermute | solution.py:303
  10.1 1.3 %collective-permute-start.3 = (bf16[4,72,128]{2,1,0:T(8,128)(2,1)S(1)}, bf16[4,72,128]{2,1,0:T(8,128)(2,1)S(1)}, u32[]{:S(2)}, u32[]{:S(2)}) collective-permute-start(bf16[4,72,128]{2,1,0:T(8,128)(2,1)S(1)} %pad_maximum_fusion.near_ref), channel_id=1, source_target_pairs={{1,0},{0,1},{5,4},{4,5},{9,8},{8,9},{13,12},{12,13},{3,2},{2,3},{7... | collective-permute-start | bytes 221192 | tf_op jit(solution)/shard_map/ppermute | solution.py:303

commit v8 on v7

--- a/solution.py
+++ b/solution.py
@@ -219,9 +219,10 @@
     near = [(factor[0][o] * seven[o]).astype(jnp.bfloat16) for o in range(owners)]
     wide = [(factor[1][o] * seven[o]).astype(jnp.bfloat16) for o in range(owners)]
     result = [dot(system[o], jnp.concatenate([near[o], wide[o]], axis=1)) for o in range(owners)]
-    factor += [*spread_of(2, pieces), *spread_of(4, pieces)]
+    factor += [*spread_of(2, pieces)]
+    arrived = exchange([rounded(part) for part in result])
+    factor += [*spread_of(4, pieces)]
     row_a = seen(near)
-    arrived = exchange([rounded(part) for part in result])
     drive = [
         factor[2][o] * seven[o] + factor[3][o] * lanes(arrived[o], 0) + factor[4][o] * lanes(arrived[o], 1)
         for o in range(owners)

time: 13.2 us -> 13.2 us (level)
  no operation moved by 1% of the time
where the time goes in v8:
time: 13.2 us; the launch traced here: 13 us
  starting transfers between devices  5.72 us (43%)
  waiting for transfers between devices  3.09 us (23%)
  Pallas kernels  2.42 us (18%)
  between operations  1.45 us (11%)
  local copies, waits for them, and re-layouts  0.25 us (2%)
    ppermute x4, starting transfers between devices, send(): return lax.ppermute(held, OWNER_AXES, pairs)  5.72 us
    ppermute x4, waiting for transfers between devices, send(): return lax.ppermute(held, OWNER_AXES, pairs)  3.09 us
    pallas_call x1, Pallas kernels, gathered_plan(): pl.pallas_call(march_kernel, out_shape=outputs, in_specs=[vmem] * 5, out_...  1.54 us
    pallas_call x1, Pallas kernels, gathered_plan(): pl.pallas_call(pick_kernel, out_shape=(jax.ShapeDtypeStruct((height, LANE...  0.49 us
    pallas_call x1, Pallas kernels, gathered_plan(): pl.pallas_call(widen_kernel, out_shape=jax.ShapeDtypeStruct((near.shape[0...  0.37 us
  transfers between devices with their start and end apart: 4, of which 4 were waited for; matrix products, arithmetic and copies ran while one was open for 0% of the time, Pallas kernels for 3%

profile of v8, /device:TPU:0, one launch (start us, length us, event | category | flops | bytes accessed | tf_op | source)
XLA Modules:
  0.0 13.0 jit_solution(4702122101368525950)
XLA Ops:
  0.6 0.0 copy-start.2
  0.6 0.0 copy-start.1
  0.7 0.0 copy-start.3
  0.7 0.0 copy-start.4
  0.7 0.0 copy-start.5
  0.7 0.0 copy-start.6
  0.7 0.0 copy-start.7
  0.7 0.0 copy-start.8
  1.4 0.0 copy-done.8
  1.4 0.1 add_bitcast_fusion.packed_ref
  1.5 0.0 copy-done.2
  1.5 0.2 %copy-done.1 = bf16[1,512,512]{2,1,0:T(8,128)(2,1)S(1)} copy-done((bf16[1,512,512]{2,1,0:T(8,128)(2,1)S(1)}, bf16[1,512,512]{2,1,0:T(8,128)(2,1)}, u32[]{:S(2)}) %copy-start.1) | copy-done | bytes 524312
  1.7 0.0 copy-done.3
  1.7 0.0 copy-done.4
  1.7 0.0 copy-done.5
  1.7 0.0 copy-done.6
  1.7 0.0 copy-done.7
  1.7 0.0 copy-start
  1.8 0.5 %pick.1 = (bf16[72,128]{1,0:T(8,128)(2,1)S(1)}, bf16[64,512]{1,0:T(8,128)(2,1)S(1)}) custom-call(s32[1,33]{1,0:T(1,128)S(1)} %add_bitcast_fusion.packed_ref, f32[8,512]{1,0:T(8,128)S(1)} %lane.1.lane_ref, s32[1,8,8]{2,1,0:T(8,128)S(1)} %copy-done.3, s32[1,8,8]{2,1,0:T(8,128)S(1)} %copy-done.4, s32[1,8,8]{2,1,0:T(8,128)S(1)} %copy-done.5, ...), custom_call_target="tpu_custom_call" | custom-call | tf_op jit(solution)/shard_map/pick/pallas_call | solution.py:287
  2.3 2.5 %collective-permute-start.2 = (bf16[1,72,128]{2,1,0:T(8,128)(2,1)S(1)}, bf16[1,72,128]{2,1,0:T(8,128)(2,1)S(1)}, u32[]{:S(2)}, u32[]{:S(2)}) collective-permute-start(bf16[1,72,128]{2,1,0:T(8,128)(2,1)S(1)} %bitcast.3), channel_id=1, source_target_pairs={{13,0},{8,1},{1,4},{0,5},{5,8},{12,9},{9,12},{4,13},{15,2},{10,3},... | collective-permute-start | bytes 55304 | tf_op jit(solution)/shard_map/ppermute | solution.py:304
  4.7 2.1 %collective-permute-start.1 = (bf16[1,72,128]{2,1,0:T(8,128)(2,1)S(1)}, bf16[1,72,128]{2,1,0:T(8,128)(2,1)S(1)}, u32[]{:S(2)}, u32[]{:S(2)}) collective-permute-start(bf16[1,72,128]{2,1,0:T(8,128)(2,1)S(1)} %bitcast.4), channel_id=1, source_target_pairs={{9,0},{12,1},{13,4},{8,5},{1,8},{4,9},{5,12},{0,13},{11,2},{14,3},... | collective-permute-start | bytes 55304 | tf_op jit(solution)/shard_map/ppermute | solution.py:304
  6.8 0.8 %collective-permute-start = (bf16[1,72,128]{2,1,0:T(8,128)(2,1)S(1)}, bf16[1,72,128]{2,1,0:T(8,128)(2,1)S(1)}, u32[]{:S(2)}, u32[]{:S(2)}) collective-permute-start(bf16[1,72,128]{2,1,0:T(8,128)(2,1)S(1)} %bitcast.5), channel_id=1, source_target_pairs={{5,0},{4,1},{9,4},{12,5},{13,8},{0,9},{1,12},{8,13},{7,2},{6,3},{1... | collective-permute-start | bytes 55304 | tf_op jit(solution)/shard_map/ppermute | solution.py:304
  7.6 0.6 %collective-permute-done.2 = bf16[1,72,128]{2,1,0:T(8,128)(2,1)S(1)} collective-permute-done((bf16[1,72,128]{2,1,0:T(8,128)(2,1)S(1)}, bf16[1,72,128]{2,1,0:T(8,128)(2,1)S(1)}, u32[]{:S(2)}, u32[]{:S(2)}) %collective-permute-start.2) | collective-permute-done | bytes 18464 | tf_op jit(solution)/shard_map/ppermute | solution.py:304
  8.2 0.8 %collective-permute-done.1 = bf16[1,72,128]{2,1,0:T(8,128)(2,1)S(1)} collective-permute-done((bf16[1,72,128]{2,1,0:T(8,128)(2,1)S(1)}, bf16[1,72,128]{2,1,0:T(8,128)(2,1)S(1)}, u32[]{:S(2)}, u32[]{:S(2)}) %collective-permute-start.1) | collective-permute-done | bytes 18464 | tf_op jit(solution)/shard_map/ppermute | solution.py:304
  9.1 1.1 %collective-permute-done = bf16[1,72,128]{2,1,0:T(8,128)(2,1)S(1)} collective-permute-done((bf16[1,72,128]{2,1,0:T(8,128)(2,1)S(1)}, bf16[1,72,128]{2,1,0:T(8,128)(2,1)S(1)}, u32[]{:S(2)}, u32[]{:S(2)}) %collective-permute-start) | collective-permute-done | bytes 18464 | tf_op jit(solution)/shard_map/ppermute | solution.py:304
  10.1 0.4 %collective-permute-start.3 = (bf16[4,72,128]{2,1,0:T(8,128)(2,1)S(1)}, bf16[4,72,128]{2,1,0:T(8,128)(2,1)S(1)}, u32[]{:S(2)}, u32[]{:S(2)}) collective-permute-start(bf16[4,72,128]{2,1,0:T(8,128)(2,1)S(1)} %pad_maximum_fusion.near_ref), channel_id=1, source_target_pairs={{1,0},{0,1},{5,4},{4,5},{9,8},{8,9},{13,12},{12,13},{3,2},{2,3},{7... | collective-permute-start | bytes 221192 | tf_op jit(solution)/shard_map/ppermute | solution.py:304
  10.5 0.0 copy-done
  10.5 0.4 %widen.1.wide_ref = f32[4,64,1024]{2,1,0:T(8,128)S(1)} custom-call(bf16[4,72,128]{2,1,0:T(8,128)(2,1)S(1)} %pad_maximum_fusion.near_ref, bf16[128,1024]{1,0:T(8,128)(2,1)S(1)} %copy-done), custom_call_target="tpu_custom_call" | custom-call | flops 67108864 | bytes 1048576 | tf_op jit(solution)/shard_map/widen/pallas_call | solution.py:309
  10.9 0.6 %collective-permute-done.3.far_ref = bf16[4,72,128]{2,1,0:T(8,128)(2,1)S(1)} collective-permute-done((bf16[4,72,128]{2,1,0:T(8,128)(2,1)S(1)}, bf16[4,72,128]{2,1,0:T(8,128)(2,1)S(1)}, u32[]{:S(2)}, u32[]{:S(2)}) %collective-permute-start.3) | collective-permute-done | bytes 73760 | tf_op jit(solution)/shard_map/ppermute | solution.py:304
  11.5 1.5 %march.1 = (bf16[1,32,512]{2,1,0:T(8,128)(2,1)}, f32[8,32]{1,0:T(8,128)}) custom-call(bf16[4,72,128]{2,1,0:T(8,128)(2,1)S(1)} %pad_maximum_fusion.near_ref, bf16[4,72,128]{2,1,0:T(8,128)(2,1)S(1)} %collective-permute-done.3.far_ref, f32[4,64,1024]{2,1,0:T(8,128)S(1)} %widen.1.wide_ref, bf16[128,1024]{1,0:T(8,128)(2,1)S(1)} %copy-done, ...), custom_call_target="tpu_custom_call" | custom-call | tf_op jit(solution)/shard_map/march/pallas_call | solution.py:324
  (2 shorter events, 0.0 us)
Async XLA Ops:
  0.6 0.9 %copy-start.2 = (bf16[1,32,512]{2,1,0:T(8,128)(2,1)S(1)}, bf16[1,32,512]{2,1,0:T(8,128)(2,1)}, u32[]{:S(2)}) copy-start(bf16[1,32,512]{2,1,0:T(8,128)(2,1)} %cotangent_ref.1) | copy-start | bytes 98308
  0.6 1.1 %copy-start.1 = (bf16[1,512,512]{2,1,0:T(8,128)(2,1)S(1)}, bf16[1,512,512]{2,1,0:T(8,128)(2,1)}, u32[]{:S(2)}) copy-start(bf16[1,512,512]{2,1,0:T(8,128)(2,1)} %inverse_ref.1) | copy-start | bytes 1572868
  0.7 1.1 %copy-start.3 = (s32[1,8,8]{2,1,0:T(8,128)S(1)}, s32[1,8,8]{2,1,0:T(8,128)}, u32[]{:S(2)}) copy-start(s32[1,8,8]{2,1,0:T(8,128)} %into_ref.1) | copy-start | bytes 772
  0.7 1.1 %copy-start.4 = (s32[1,8,8]{2,1,0:T(8,128)S(1)}, s32[1,8,8]{2,1,0:T(8,128)}, u32[]{:S(2)}) copy-start(s32[1,8,8]{2,1,0:T(8,128)} %from_ref.1) | copy-start | bytes 772
  0.7 1.1 %copy-start.5 = (s32[1,8,8]{2,1,0:T(8,128)S(1)}, s32[1,8,8]{2,1,0:T(8,128)}, u32[]{:S(2)}) copy-start(s32[1,8,8]{2,1,0:T(8,128)} %offset_ref.1) | copy-start | bytes 772
  0.7 1.1 %copy-start.6 = (f32[1,8,8]{2,1,0:T(8,128)S(1)}, f32[1,8,8]{2,1,0:T(8,128)}, u32[]{:S(2)}) copy-start(f32[1,8,8]{2,1,0:T(8,128)} %weight_ref.1) | copy-start | bytes 772
  0.7 1.0 %copy-start.7 = (f32[1,8,8]{2,1,0:T(8,128)S(1)}, f32[1,8,8]{2,1,0:T(8,128)}, u32[]{:S(2)}) copy-start(f32[1,8,8]{2,1,0:T(8,128)} %admit_ref.1) | copy-start | bytes 772
  0.7 0.7 %copy-start.8 = (s32[32]{0:T(128)S(1)}, s32[32]{0:T(128)}, u32[]{:S(2)}) copy-start(s32[32]{0:T(128)} %param.18) | copy-start | bytes 388
  1.7 8.7 %copy-start = (bf16[128,1024]{1,0:T(8,128)(2,1)S(1)}, bf16[128,1024]{1,0:T(8,128)(2,1)}, u32[]{:S(2)}) copy-start(bf16[128,1024]{1,0:T(8,128)(2,1)} %constant.2.clone.spread_ref) | copy-start | bytes 786436
  2.3 6.0 %collective-permute-start.2 = (bf16[1,72,128]{2,1,0:T(8,128)(2,1)S(1)}, bf16[1,72,128]{2,1,0:T(8,128)(2,1)S(1)}, u32[]{:S(2)}, u32[]{:S(2)}) collective-permute-start(bf16[1,72,128]{2,1,0:T(8,128)(2,1)S(1)} %bitcast.3), channel_id=1, source_target_pairs={{13,0},{8,1},{1,4},{0,5},{5,8},{12,9},{9,12},{4,13},{15,2},{10,3},... | collective-permute-start | bytes 55304 | tf_op jit(solution)/shard_map/ppermute | solution.py:304
  4.7 4.3 %collective-permute-start.1 = (bf16[1,72,128]{2,1,0:T(8,128)(2,1)S(1)}, bf16[1,72,128]{2,1,0:T(8,128)(2,1)S(1)}, u32[]{:S(2)}, u32[]{:S(2)}) collective-permute-start(bf16[1,72,128]{2,1,0:T(8,128)(2,1)S(1)} %bitcast.4), channel_id=1, source_target_pairs={{9,0},{12,1},{13,4},{8,5},{1,8},{4,9},{5,12},{0,13},{11,2},{14,3},... | collective-permute-start | bytes 55304 | tf_op jit(solution)/shard_map/ppermute | solution.py:304
  6.8 3.3 %collective-permute-start = (bf16[1,72,128]{2,1,0:T(8,128)(2,1)S(1)}, bf16[1,72,128]{2,1,0:T(8,128)(2,1)S(1)}, u32[]{:S(2)}, u32[]{:S(2)}) collective-permute-start(bf16[1,72,128]{2,1,0:T(8,128)(2,1)S(1)} %bitcast.5), channel_id=1, source_target_pairs={{5,0},{4,1},{9,4},{12,5},{13,8},{0,9},{1,12},{8,13},{7,2},{6,3},{1... | collective-permute-start | bytes 55304 | tf_op jit(solution)/shard_map/ppermute | solution.py:304
  10.1 1.3 %collective-permute-start.3 = (bf16[4,72,128]{2,1,0:T(8,128)(2,1)S(1)}, bf16[4,72,128]{2,1,0:T(8,128)(2,1)S(1)}, u32[]{:S(2)}, u32[]{:S(2)}) collective-permute-start(bf16[4,72,128]{2,1,0:T(8,128)(2,1)S(1)} %pad_maximum_fusion.near_ref), channel_id=1, source_target_pairs={{1,0},{0,1},{5,4},{4,5},{9,8},{8,9},{13,12},{12,13},{3,2},{2,3},{7... | collective-permute-start | bytes 221192 | tf_op jit(solution)/shard_map/ppermute | solution.py:304
